TPU v7x, 256 devices: a whole 4x4x8 slice. The times are simulated.
256 devices in a mesh: grp: 4 (over x), blk: 64 (over z, y, core).
Axes of the slice: x: 4, y: 4, z: 8, core: 2. Of those that a mesh axis runs over, the one named last changes fastest.
Arguments:
- amplitudes: float32 [1600, 500, 256], P('blk', 'grp'), may hold values from -16 to 16
- cycle_weight: float32 [500, 20000], P(None, 'grp'), may hold values from -0.375 to 0.375
- occ_irrep: int32 [40], replicated, may hold values from 0 to 7
- vir_irrep: int32 [500], replicated, may hold values from 0 to 7
- occ_energy: float32 [40], replicated, may hold values from -1.5 to -0.4
- vir_energy: float32 [500], replicated, may hold values from 0.1 to 2.5
Outputs:
- increment: float32 [500, 10240], P('grp', 'blk')
Inputs may be any that keep to these rules, and one draw needn't show every extreme that they name: `occ_irrep`: D2h irrep labels. `vir_irrep`: D2h irrep labels.
All inputs are finite; a program needn't handle non-finite values.
Results may differ from a plain program's by a relative error of at most 0.0001.
Values sent between devices are 32-bit elements; how exact they have to be, the bound alone decides.
No kernel may reach another device: no remote copies, remote signals or barrier semaphores. Data moves between devices by JAX's collectives and lax.ppermute only.
A program may use at most 128 MiB of HBM per device.

v0:
```python
import jax
import jax.numpy as jnp
from jax import lax
from jax.sharding import PartitionSpec as P

O = 40
V = 500
IW = 1


HIGHEST = lax.Precision.HIGHEST


def shards(amplitudes, cycle_weight, occ_irrep, vir_irrep, occ_energy, vir_energy):
    n_blk = lax.axis_size("blk")
    n_grp = lax.axis_size("grp")
    grp_index = lax.axis_index("grp")
    blk_index = lax.axis_index("blk")
    pair_loc, c_loc, slab = amplitudes.shape
    b_loc = slab // n_blk
    rows = IW * V
    out_rows = rows // n_grp
    vir_local = lax.dynamic_slice_in_dim(vir_irrep, grp_index * c_loc, c_loc)
    row_irrep = jnp.bitwise_xor(occ_irrep[:IW][:, None], vir_irrep[None, :]).reshape(rows)
    col_irrep = jnp.bitwise_xor(vir_local[:, None], occ_irrep[None, :])
    weight_all = cycle_weight.reshape(rows, c_loc, O)
    weight = jnp.where(
        row_irrep[:, None, None] == col_irrep[None, :, :], weight_all, jnp.zeros_like(weight_all)
    )
    row_energy = (occ_energy[:IW][:, None] - vir_energy[None, :]).reshape(rows)
    row_share = lax.dynamic_slice_in_dim(row_energy, grp_index * out_rows, out_rows)
    slab_energy = lax.dynamic_slice_in_dim(vir_energy, blk_index * b_loc, b_loc)
    col_energy = (occ_energy[None, :] - slab_energy[:, None]).reshape(b_loc * O)
    pair_index = blk_index * pair_loc + jnp.arange(pair_loc, dtype=jnp.int32)
    k_index = pair_index // O
    j_index = pair_index % O
    occ_ids = jnp.arange(O, dtype=jnp.int32)
    match_k = k_index[:, None] == occ_ids[None, :]
    match_j = j_index[:, None] == occ_ids[None, :]
    irrep_k = jnp.sum(jnp.where(match_k, occ_irrep[None, :], 0), axis=1)
    irrep_j = jnp.sum(jnp.where(match_j, occ_irrep[None, :], 0), axis=1)
    pair_irrep = jnp.bitwise_xor(irrep_k, irrep_j)
    parity = jnp.bitwise_xor(
        jnp.bitwise_xor(pair_irrep[:, None, None], vir_local[None, :, None]),
        vir_irrep[:slab][None, None, :],
    )
    masked = jnp.where(parity == 0, amplitudes, jnp.zeros_like(amplitudes))
    pick_k = match_k.astype(jnp.float32)
    pick_j = match_j.astype(jnp.float32)
    selected = jnp.einsum("xck,tk->xct", weight, pick_k, precision=HIGHEST)
    per_pair = jnp.einsum("xct,tcb->tbx", selected, masked, precision=HIGHEST)
    placed = jnp.einsum("tbx,tj->bjx", per_pair, pick_j, precision=HIGHEST)
    reduced = lax.psum_scatter(
        placed.reshape(b_loc * O * lax.axis_size("blk"), rows),
        "blk",
        scatter_dimension=0,
        tiled=True,
    )
    summed = jnp.transpose(lax.psum_scatter(reduced, "grp", scatter_dimension=1, tiled=True))
    denominator = row_share[:, None] + col_energy[None, :]
    return summed / denominator


def solution(mesh):
    in_specs = (P("blk", "grp", None), P(None, "grp"), P(), P(), P(), P())
    out_specs = P("grp", "blk")
    return jax.shard_map(shards, mesh=mesh, in_specs=in_specs, out_specs=out_specs, check_vma=False)
```

profile of v0, /device:TPU:8, one launch (start us, length us, event | category | flops | bytes accessed | tf_op | source)
XLA Modules:
  0.0 349.3 jit_solution(9360654212679594122)
XLA Ops:
  6.5 0.0 reduce-scatter.3.cloned.1.call-start
  6.6 0.8 dynamic_slice.7
  7.3 0.7 broadcast_xor_fusion
  8.0 0.8 select_reduce_fusion
  8.9 0.1 broadcast_xor_fusion.1
  9.0 12.2 %copy.8 = f32[500,125,40]{1,2,0:T(8,128)} copy(f32[500,125,40]{0,2,1:T(8,128)} %bitcast.22) | data formatting | bytes 20000000 | tf_op jit(solution)/shard_map/reshape | solution.py:26
  21.2 0.0 copy-done.1
  21.2 9.8 %fusion.2 = f32[500,125,25]{1,2,0:T(8,128)} fusion(f32[500,125,40]{1,2,0:T(8,128)} %copy.8, s32[125,40]{0,1:T(8,128)S(1)} %broadcast_xor_fusion, s32[500]{0:T(512)S(1)} %broadcast_xor_fusion.2, s32[25]{0:T(128)S(1)} %get-tuple-element.7), kind=kOutput, calls=%fused_computation.2 | convolution fusion | flops 755001024 | bytes 16272100 | tf_op jit(solution)/shard_map/xck,tk->xct/dot_general | solution.py:50
  31.0 0.0 slice-done
  31.0 17.5 %fusion.8 = f32[25,256,500]{1,2,0:T(8,128)S(1)} fusion(f32[500,125,25]{1,2,0:T(8,128)} %fusion.2, f32[25,125,256]{2,1,0:T(8,128)S(1)} %copy-done, s32[256]{0:T(256)S(1)} %slice-done, s32[25,125]{1,0:T(8,128)S(1)} %broadcast_xor_fusion.1), kind=kOutput, calls=%fused_computation.6 | convolution fusion | flops 4802400256 | bytes 22263524 | tf_op jit(solution)/shard_map/xct,tcb->tbx/dot_general | solution.py:51
  48.5 15.2 %fusion.5 = f32[256,40,500]{0,1,2:T(8,128)} fusion(f32[25,256,500]{1,2,0:T(8,128)S(1)} %fusion.8, s32[25]{0:T(128)S(1)} %get-tuple-element.8), kind=kOutput, calls=%fused_computation.5 | convolution fusion | flops 1536001024 | bytes 33280100 | tf_op jit(solution)/shard_map/tbx,tj->bjx/dot_general | solution.py:52
  63.7 22.2 %copy.11 = f32[256,40,500]{2,1,0:T(8,128)} copy(f32[256,40,500]{0,1,2:T(8,128)} %fusion.5) | data formatting | bytes 40960000 | tf_op jit(solution)/shard_map/tbx,tj->bjx/transpose | solution.py:52
  85.9 0.0 reduce-scatter.3.cloned.1.call-update
  85.9 0.0 all-reduce.3.cloned.1.call-start
  86.0 0.6 copy-done.3
  86.6 0.1 dynamic_slice.8
  86.7 205.6 %reduce-scatter.3.cloned.1.call-done = f32[160,500]{1,0:T(8,128)} async-done(((f32[10240,500]{1,0:T(8,128)}), f32[160,500]{1,0:T(8,128)}) %reduce-scatter.3.cloned.1.call-update) | async-done | bytes 320016 | tf_op jit(solution)/shard_map/reduce_scatter | solution.py:53
  292.2 0.0 all-reduce.3.cloned.1.call-update
  292.3 0.1 broadcast_subtract_fusion
  292.3 0.1 sub.42
  292.5 0.1 dynamic-slice.4
  292.6 0.6 dynamic-slice.5
  293.8 47.0 %all-reduce.3.cloned.1.call-done = f32[160,500]{1,0:T(8,128)} async-done(((f32[160,500]{1,0:T(8,128)}), f32[160,500]{1,0:T(8,128)}) %all-reduce.3.cloned.1.call-update) | async-done | bytes 320016
  340.8 1.7 fusion.18
  (15 shorter events, 0.1 us)
Async XLA Ops:
  6.5 285.7 %reduce-scatter.3.cloned.1.call-start = ((), (), s32[]{:S(2)}) async-start(), calls=%async_computation.1 | async-start | bytes 21299200 | tf_op jit(solution)/shard_map/reduce_scatter | solution.py:53
  9.0 12.2 %copy-start.1 = (s32[40]{0:T(128)S(1)}, s32[40]{0:T(128)}, u32[]{:S(2)}) copy-start(s32[40]{0:T(128)} %param.8) | copy-start | bytes 484
  9.0 12.2 %copy-start.2 = (s32[500]{0:T(512)S(1)}, s32[500]{0:T(512)}, u32[]{:S(2)}) copy-start(s32[500]{0:T(512)} %param.9) | copy-start | bytes 6004
  21.2 9.9 %copy-start = (f32[25,125,256]{2,1,0:T(8,128)S(1)}, f32[25,125,256]{2,1,0:T(8,128)}, u32[]{:S(2)}) copy-start(f32[25,125,256]{2,1,0:T(8,128)} %param.6) | copy-start | bytes 9600004
  21.2 9.9 %slice-start = ((s32[500]{0:T(512)}), s32[256]{0:T(256)S(1)}, s32[]{:S(2)}) async-start(s32[500]{0:T(512)} %param.9), calls=%async_computation.3 | async-start | bytes 2048 | tf_op jit(solution)/shard_map/slice | solution.py:45
  85.9 0.7 copy-start.3
  85.9 206.3 %copy-start.4 = (f32[40]{0:T(128)S(1)}, f32[40]{0:T(128)}, u32[]{:S(2)}) copy-start(f32[40]{0:T(128)} %param.10) | copy-start | bytes 484
  85.9 206.6 %copy-start.5 = (u32[256]{0:T(256)S(1)}, u32[256]{0:T(256)}, u32[]{:S(2)}) copy-start(u32[256]{0:T(256)} %constant.46) | copy-start | bytes 3076
  85.9 254.9 %all-reduce.3.cloned.1.call-start = ((), (), s32[]{:S(2)}) async-start(), calls=%async_computation.2 | async-start | bytes 655360
Sparse Core Ops, SparseCore 0:
  86.1 206.1 reduce-scatter.2
  294.6 46.2 all-reduce.2
where the time goes:
time: 350 us; the launch traced here: 349 us
  waiting for transfers between devices  253 us (72%)
  matrix products  42.5 us (12%)
  local copies, waits for them, and re-layouts  36.6 us (10%)
  between operations  14.1 us (4%)
    reduce_scatter x1, waiting for transfers between devices, shards(): lax.psum_scatter(placed.reshape(b_loc * O * lax.axis_size('blk'), rows),...  206 us
    unnamed x3, waiting for transfers between devices  47.1 us
    transpose x1, local copies, waits for them, and re-layouts, shards(): placed = jnp.einsum('tbx,tj->bjx', per_pair, pick_j, precision=HIGHEST)  22.2 us
    dot_general x1, matrix products, shards(): per_pair = jnp.einsum('xct,tcb->tbx', selected, masked, precision=HIGHEST)  17.5 us
    dot_general x1, matrix products, shards(): placed = jnp.einsum('tbx,tj->bjx', per_pair, pick_j, precision=HIGHEST)  15.2 us
    reshape x1, local copies, waits for them, and re-layouts, shards(): weight_all = cycle_weight.reshape(rows, c_loc, O)  12.2 us
    dot_general x1, matrix products, shards(): selected = jnp.einsum('xck,tk->xct', weight, pick_k, precision=HIGHEST)  9.82 us
  transfers between devices with their start and end apart: 2, of which 2 were waited for; matrix products, arithmetic and copies ran while one was open for 0% of the time, Pallas kernels for 0%

commit v1 on v0

--- a/solution.py
+++ b/solution.py
@@ -1,17 +1,280 @@
 import jax
 import jax.numpy as jnp
 from jax import lax
+from jax.experimental import pallas as pl
+from jax.experimental.pallas import tpu as pltpu
 from jax.sharding import PartitionSpec as P
 
 O = 40
 V = 500
 IW = 1
-
+BW = 256
+G = 4
+M = 64
+CL = V // G
+CP = 128
+T = O * O // M
+TS = 5
+BL = BW // M
+J4 = O * BL
+SLOTS = 640
+FOLD = 40
+NF = G * FOLD
+NONE = 16
 
 HIGHEST = lax.Precision.HIGHEST
-
-
-def shards(amplitudes, cycle_weight, occ_irrep, vir_irrep, occ_energy, vir_energy):
+F32 = jnp.float32
+BF16 = jnp.bfloat16
+I32 = jnp.int32
+
+
+def dot(a, b):
+    return jnp.dot(a, b, preferred_element_type=F32)
+
+
+def halves(x):
+    high = x.astype(BF16)
+    return high, (x - high.astype(F32)).astype(BF16)
+
+
+def iota(shape, dim):
+    return lax.broadcasted_iota(I32, shape, dim)
+
+
+def pack_kernel(occ_ref, vir_ref, amp_ref, out_ref, rank_ref, column_ref, count_ref, base_ref, total_ref, pick_ref, high_ref, low_ref):
+    step = pl.program_id(0)
+    g = lax.axis_index("grp")
+    m = lax.axis_index("blk")
+    row = vir_ref[:, 0:CP]
+    for other in range(1, G):
+        row = jnp.where(g == other, vir_ref[:, other * CL : other * CL + CP], row)
+    row = jnp.where(iota((1, CP), 1) < CL, row, NONE)
+
+    @pl.when(step == 0)
+    def _():
+        wide = jnp.broadcast_to(row, (CP, CP))
+        column = jnp.transpose(wide)
+        column_ref[...] = column
+        before = (wide == column) & (iota((CP, CP), 0) < iota((CP, CP), 1))
+        rank_ref[...] = jnp.sum(before.astype(F32), axis=0, keepdims=True).astype(I32)
+        for q in range(8):
+            same = (iota((8, CP), 0) == jnp.bitwise_xor(row, q)).astype(F32)
+            count_ref[q] = jnp.broadcast_to(jnp.sum(same, axis=1, keepdims=True), (8, CP)).astype(I32)
+        base_ref[...] = jnp.zeros_like(base_ref)
+        total_ref[...] = jnp.zeros_like(total_ref)
+
+    for t in range(TS):
+        pair = m * T + step * TS + t
+        q = jnp.bitwise_xor(occ_ref[pair // O], occ_ref[pair % O])
+        same = iota((8, CP), 0) == jnp.bitwise_xor(row, q)
+        base = jnp.sum(jnp.where(same, base_ref[...], 0).astype(F32), axis=0, keepdims=True).astype(I32)
+        slot = base + rank_ref[...]
+        base_ref[...] += count_ref[q]
+        pick_ref[:, t * CP : (t + 1) * CP] = (iota((SLOTS, CP), 0) == slot).astype(F32).astype(BF16)
+        need = jnp.bitwise_xor(column_ref[...], q)
+        for half in range(BW // CP):
+            lanes = slice(half * CP, (half + 1) * CP)
+            block = jnp.where(need == vir_ref[:, lanes], amp_ref[t, :, lanes], 0.0)
+            high, low = halves(block)
+            high_ref[t * CP : (t + 1) * CP, lanes] = high
+            low_ref[t * CP : (t + 1) * CP, lanes] = low
+    total_ref[...] += dot(pick_ref[...], high_ref[...]) + dot(pick_ref[...], low_ref[...])
+
+    @pl.when(step == pl.num_programs(0) - 1)
+    def _():
+        out_ref[...] = jnp.transpose(total_ref[...]).reshape(M, BL, SLOTS)
+
+
+def pack(occ_irrep, vir_row, amplitudes):
+    return pl.pallas_call(
+        pack_kernel,
+        name="pack_amplitudes",
+        grid=(T // TS,),
+        out_shape=jax.ShapeDtypeStruct((M, BL, SLOTS), F32),
+        in_specs=[
+            pl.BlockSpec(memory_space=pltpu.SMEM),
+            pl.BlockSpec((1, G * CP), lambda s: (0, 0)),
+            pl.BlockSpec((TS, CP, BW), lambda s: (s, 0, 0)),
+        ],
+        out_specs=pl.BlockSpec((M, BL, SLOTS), lambda s: (0, 0, 0)),
+        scratch_shapes=[
+            pltpu.VMEM((1, CP), I32),
+            pltpu.VMEM((CP, CP), I32),
+            pltpu.VMEM((8, 8, CP), I32),
+            pltpu.VMEM((8, CP), I32),
+            pltpu.VMEM((SLOTS, BW), F32),
+            pltpu.VMEM((SLOTS, TS * CP), BF16),
+            pltpu.VMEM((TS * CP, BW), BF16),
+            pltpu.VMEM((TS * CP, BW), BF16),
+        ],
+        compiler_params=pltpu.CompilerParams(vmem_limit_bytes=32 << 20),
+    )(occ_irrep, vir_row, amplitudes)
+
+
+CS = 16
+
+
+def fold_kernel(place_ref, need_ref, have_ref, w_ref, high_ref, low_ref, pick_ref, turn_ref, rest_ref):
+    step = pl.program_id(0)
+
+    @pl.when(step == 0)
+    def _():
+        pick_ref[...] = (iota((NF, V), 0) == place_ref[...]).astype(F32).astype(BF16)
+
+    block = jnp.where(need_ref[...] == have_ref[...], w_ref[...], 0.0)
+    high, low = halves(block)
+    folded = dot(pick_ref[...], high) + dot(pick_ref[...], low)
+    turned = jnp.transpose(folded)
+    turn_ref[...] = turned[:, 0:CP]
+    rest_ref[:, 0 : NF - CP] = turned[:, CP:NF]
+    for k in range(O):
+        rows = pl.ds(k, CS, stride=O)
+        part = jnp.concatenate([turn_ref[rows, :], rest_ref[rows, :]], axis=1)
+        high, low = halves(part[:, 0:NF])
+        high_ref[k] = high
+        low_ref[k] = low
+
+
+def fold(place, need, have, weight):
+    lanes = CS * O
+    out = jax.ShapeDtypeStruct((O, CP, NF), BF16)
+    spec = pl.BlockSpec((O, CS, NF), lambda s: (0, s, 0))
+    return pl.pallas_call(
+        fold_kernel,
+        name="fold_weights",
+        grid=(CP // CS,),
+        out_shape=(out, out),
+        in_specs=[
+            pl.BlockSpec((1, V), lambda s: (0, 0)),
+            pl.BlockSpec((V, 1), lambda s: (0, 0)),
+            pl.BlockSpec((1, lanes), lambda s: (0, s)),
+            pl.BlockSpec((V, lanes), lambda s: (0, s)),
+        ],
+        out_specs=(spec, spec),
+        scratch_shapes=[pltpu.VMEM((NF, V), BF16), pltpu.VMEM((lanes, CP), F32), pltpu.VMEM((lanes, CP), F32)],
+        compiler_params=pltpu.CompilerParams(vmem_limit_bytes=32 << 20),
+    )(place, need, have, weight)
+
+
+def contract_kernel(x_ref, slot_ref, high_ref, low_ref, out_ref, wide_ref, total_ref):
+    g = lax.axis_index("grp")
+
+    @pl.loop(0, M // 2)
+    def _(i):
+        packed = x_ref[pl.ds(2 * i, 2)].reshape(2 * BL, SLOTS)
+        for t in range(T):
+            slot = slot_ref[t, pl.ds(pl.multiple_of(8 * i, 8), 8), :]
+            lane = jnp.bitwise_and(slot, CP - 1)
+            where = jnp.right_shift(slot, 7)
+            found = jnp.zeros((8, CP), F32)
+            for part in range(SLOTS // CP):
+                taken = jnp.take_along_axis(
+                    packed[:, part * CP : (part + 1) * CP], lane, axis=1, mode="promise_in_bounds"
+                )
+                found = jnp.where(where == part, taken, found)
+            first = pl.multiple_of(2 * T * BL * i, 8)
+            wide_ref[pl.ds(first + BL * t, BL), :] = found[0:BL]
+            wide_ref[pl.ds(first + T * BL + BL * t, BL), :] = found[BL : 2 * BL]
+
+    total_ref[...] = jnp.zeros_like(total_ref)
+
+    @pl.loop(0, O // 2)
+    def _(i):
+        first = pl.multiple_of(2 * J4 * i, 8)
+        amp = jnp.concatenate([wide_ref[pl.ds(first, J4), :], wide_ref[pl.ds(first + J4, J4), :]], axis=1)
+        a_high, a_low = halves(amp)
+        w_high = high_ref[pl.ds(2 * i, 2)].reshape(2 * CP, NF)
+        w_low = low_ref[pl.ds(2 * i, 2)].reshape(2 * CP, NF)
+        total_ref[...] += dot(a_high, w_high) + dot(a_high, w_low) + dot(a_low, w_high)
+
+    turned = jnp.transpose(total_ref[...])
+    for block in range(G):
+        out_ref[jnp.bitwise_xor(g, block)] = turned[block * FOLD : (block + 1) * FOLD]
+
+
+def contract(received, slots, high, low):
+    return pl.pallas_call(
+        contract_kernel,
+        name="contract",
+        out_shape=jax.ShapeDtypeStruct((G, FOLD, J4), F32),
+        scratch_shapes=[pltpu.VMEM((O * O * BL, CP), F32), pltpu.VMEM((J4, NF), F32)],
+        compiler_params=pltpu.CompilerParams(vmem_limit_bytes=40 << 20),
+    )(received, slots, high, low)
+
+
+def finish_kernel(a_ref, b_ref, rank_ref, need_ref, have_ref, row_ref, column_ref, out_ref):
+    folded = a_ref[...] + b_ref[...]
+    source = iota((J4, J4), 0)
+    target = iota((J4, J4), 1)
+    move = (source % BL) * O + source // BL == target
+    folded = jnp.dot(folded, move.astype(F32), precision=HIGHEST, preferred_element_type=F32)
+    pick = (iota((CL, FOLD), 1) == rank_ref[...]).astype(F32)
+    wide = jnp.dot(pick, folded, precision=HIGHEST, preferred_element_type=F32)
+    wide = jnp.where(need_ref[...] == have_ref[...], wide, 0.0)
+    out_ref[...] = wide / (row_ref[...] + column_ref[...])
+
+
+def finish(a, b, rank, need, have, row, column):
+    return pl.pallas_call(
+        finish_kernel, name="finish", out_shape=jax.ShapeDtypeStruct((CL, J4), F32)
+    )(a, b, rank, need, have, row, column)
+
+
+def packed_form(amplitudes, cycle_weight, occ_irrep, vir_irrep, occ_energy, vir_energy):
+    g = lax.axis_index("grp")
+    m = lax.axis_index("blk")
+    labels = jnp.arange(8, dtype=I32)
+    sent = pack(occ_irrep, vir_irrep.reshape(1, V), amplitudes)
+    received = lax.all_to_all(sent, "blk", 0, 0, tiled=True)
+
+    shares = vir_irrep.reshape(G, CL)
+    orbital = jnp.arange(CL)
+    earlier = orbital[:, None] < orbital[None, :]
+    ranks = jnp.sum((shares[:, :, None] == shares[:, None, :]) & earlier[None], axis=1).astype(I32)
+    counts = jnp.sum(shares[:, :, None] == labels, axis=1).astype(I32)
+    own = lax.dynamic_index_in_dim(shares, g, 0, keepdims=False)
+    own_rank = lax.dynamic_index_in_dim(ranks, g, 0, keepdims=False)
+    own_count = lax.dynamic_index_in_dim(counts, g, 0, keepdims=False)
+    own_c = jnp.concatenate([own, jnp.full((CP - CL,), NONE, I32)])
+    rank_c = jnp.concatenate([own_rank, jnp.zeros((CP - CL,), I32)])
+
+    pairs = jnp.bitwise_xor(occ_irrep[:, None], occ_irrep[None, :]).reshape(M, T)
+    kinds = (pairs[:, :, None] == labels).astype(I32)
+    passed = jnp.cumsum(kinds, axis=1) - kinds
+    crossed = jnp.bitwise_xor(labels[:, None], labels[None, :])
+    per_kind = jnp.sum(jnp.where(crossed[:, :, None] == labels, own_count, 0), axis=2)
+    base = jnp.sum(passed[:, :, :, None] * per_kind, axis=2)
+    reach = jnp.bitwise_xor(pairs[:, :, None], own_c)
+    slot = rank_c + sum(jnp.where(reach == u, base[:, :, u : u + 1], 0) for u in range(8))
+    own_b = lax.dynamic_slice_in_dim(vir_irrep, m * BL, BL)
+    slots = jnp.where(reach[:, :, None, :] == own_b[:, None], slot[:, :, None, :], -1)
+    slots = jnp.transpose(slots, (1, 0, 2, 3)).reshape(T, M * BL, CP)
+
+    totals = jnp.sum(kinds, axis=1)
+    all_kinds = jnp.sum(jnp.where(crossed[:, :, None] == labels, counts[:, None, None, :], 0), axis=3)
+    filled = jnp.sum(totals[None, :, :, None] * all_kinds[:, None], axis=2)
+    fits = (jnp.max(filled) <= SLOTS) & (jnp.max(counts) <= FOLD)
+
+    place = (jnp.minimum(ranks, FOLD) + jnp.where(ranks < FOLD, jnp.arange(G, dtype=I32)[:, None] * FOLD, V)).reshape(1, V)
+    need = jnp.bitwise_xor(vir_irrep, occ_irrep[0]).reshape(V, 1)
+    have = jnp.bitwise_xor(own_c[:, None], occ_irrep[None, :]).reshape(1, CP * O)
+    high, low = fold(place, need, have, cycle_weight)
+
+    partial = contract(received, slots, high, low)
+    near = lax.ppermute(partial[1:3], "grp", [(d, d ^ 1) for d in range(G)])
+    mine = partial[0] + near[0]
+    last = lax.ppermute(partial[3] + near[1], "grp", [(d, d ^ 3) for d in range(G)])
+
+    row_energy = occ_energy[0] - lax.dynamic_slice_in_dim(vir_energy, g * CL, CL)
+    slab_energy = lax.dynamic_slice_in_dim(vir_energy, m * BL, BL)
+    col_energy = (occ_energy[None, :] - slab_energy[:, None]).reshape(1, J4)
+    row_need = jnp.bitwise_xor(own, occ_irrep[0]).reshape(CL, 1)
+    col_have = jnp.bitwise_xor(occ_irrep[None, :], own_b[:, None]).reshape(1, J4)
+    out = finish(mine, last, own_rank.reshape(CL, 1), row_need, col_have, row_energy.reshape(CL, 1), col_energy)
+    return out, fits
+
+
+def plain_form(amplitudes, cycle_weight, occ_irrep, vir_irrep, occ_energy, vir_energy):
     n_blk = lax.axis_size("blk")
     n_grp = lax.axis_size("grp")
     grp_index = lax.axis_index("grp")
@@ -61,6 +324,11 @@
     return summed / denominator
 
 
+def shards(*arrays):
+    out, fits = packed_form(*arrays)
+    return lax.cond(fits, lambda: out, lambda: plain_form(*arrays))
+
+
 def solution(mesh):
     in_specs = (P("blk", "grp", None), P(None, "grp"), P(), P(), P(), P())
     out_specs = P("grp", "blk")

time: 350 us -> 105 us (0.30)
  waiting for transfers between devices: 253 us -> 2.91 us
  matrix products: 42.5 us -> 0 us
  Pallas kernels: 0 us -> 33.4 us
  starting transfers between devices: 0.04 us -> 16.6 us
  local copies, waits for them, and re-layouts: 36.6 us -> 26.7 us
  other arithmetic: 3.46 us -> 9.97 us
    reduce_scatter x1 -> x0, waiting for transfers between devices: 206 us -> none  [shards(): lax.psum_scatter(placed.reshape(b_loc * O * lax.axis_size('blk'), rows),...]
    unnamed x3 -> x0, waiting for transfers between devices: 47.1 us -> none
    dot_general x3 -> x0, matrix products: 42.5 us -> none  [the longest x1 17.5 us: shards(): per_pair = jnp.einsum('xct,tcb->tbx', selected, masked, precision=HIGHEST)]
    pallas_call x0 -> x4, Pallas kernels: none -> 33.4 us  [the longest x1 15.4 us: contract(): pl.pallas_call(contract_kernel, name='contract', out_shape=jax.ShapeDtype...]
    transpose x1 -> x0, local copies, waits for them, and re-layouts: 22.2 us -> none  [shards(): placed = jnp.einsum('tbx,tj->bjx', per_pair, pick_j, precision=HIGHEST)]
    unnamed x13 -> x23, local copies, waits for them, and re-layouts: 1.2 us -> 19.8 us
    all_to_all x0 -> x1, starting transfers between devices: none -> 12.3 us  [packed_form(): received = lax.all_to_all(sent, 'blk', 0, 0, tiled=True)]
    reshape x1 -> x4, local copies, waits for them, and re-layouts: 12.2 us -> 1.63 us  [the longest x2 0.76 us: packed_form(): own_rank.reshape(CL, 1)]
  transfers between devices with their start and end apart: 2 -> 3, of which waited for: 2 -> 1; matrix products, arithmetic and copies ran while one was open for 0% -> 26% of each run, Pallas kernels for 0% -> 8%
where the time goes in v1:
time: 105 us
  Pallas kernels  33.4 us (32%)
  local copies, waits for them, and re-layouts  26.7 us (25%)
  starting transfers between devices  16.6 us (16%)
  between operations  15 us (14%)
  other arithmetic  9.97 us (9%)
  waiting for transfers between devices  2.91 us (3%)
    unnamed x23, local copies, waits for them, and re-layouts  19.8 us
    pallas_call x1, Pallas kernels, contract(): pl.pallas_call(contract_kernel, name='contract', out_shape=jax.ShapeDtype...  15.4 us
    all_to_all x1, starting transfers between devices, packed_form(): received = lax.all_to_all(sent, 'blk', 0, 0, tiled=True)  12.3 us
    pallas_call x1, Pallas kernels, fold(): pl.pallas_call(fold_kernel, name='fold_weights', grid=(CP // CS,), out_sh...  8.36 us
    pallas_call x1, Pallas kernels, pack(): pl.pallas_call(pack_kernel, name='pack_amplitudes', grid=(T // TS,), out_...  8.13 us
    ppermute x1, waiting for transfers between devices, packed_form(): near = lax.ppermute(partial[1:3], 'grp', [(d, d ^ 1) for d in range(G)])  2.9 us
    ppermute x1, starting transfers between devices, packed_form(): lax.ppermute(partial[3] + near[1], 'grp', [(d, d ^ 3) for d in range(G)])  2.76 us
  transfers between devices with their start and end apart: 3, of which 1 were waited for; matrix products, arithmetic and copies ran while one was open for 26% of the time, Pallas kernels for 8%

profile of v1, /device:TPU:8, one launch (start us, length us, event | category | flops | bytes accessed | tf_op | source)
XLA Modules:
  0.0 104.9 jit_solution(246502014380972709)
XLA Ops:
  6.5 8.1 %pack_amplitudes.1 = f32[64,4,640]{2,1,0:T(4,128)} custom-call(s32[40]{0:T(128)} %occ_ref.1, s32[1,500]{1,0:T(1,128)} %bitcast.86, f32[25,125,256]{2,1,0:T(8,128)} %amp_ref.1), custom_call_target="tpu_custom_call" | custom-call | tf_op jit(solution)/shard_map/pack_amplitudes/pallas_call | solution.py:89
  14.7 12.3 %all-to-all-start = ((f32[64,4,640]{2,1,0:T(4,128)}), f32[64,4,640]{2,1,0:T(4,128)}, u32[]{:S(2)}, u32[]{:S(2)}) async-start(f32[64,4,640]{2,1,0:T(4,128)} %pack_amplitudes.1), calls=%async_computation.1 | async-start | bytes 1310720 | tf_op jit(solution)/shard_map/all_to_all | solution.py:228
  27.0 0.8 eq.234
  27.7 0.8 broadcast_xor_fusion.5
  29.8 1.3 %broadcast_xor_fusion.7 = s32[500]{0:T(512)S(1)} fusion(s32[500]{0:T(512)} %param.11, s32[]{:T(128)} %bitcast.83), kind=kLoop, calls=%fused_computation.83 | loop fusion | flops 500 | bytes 4004 | tf_op jit(solution)/shard_map/xor | solution.py:259
  31.1 0.7 xor_bitcast_fusion
  33.8 11.2 %copy.63.w_ref = f32[500,5000]{1,0:T(8,128)} copy(f32[500,5000]{0,1:T(8,128)} %param.9) | data formatting | bytes 20000000 | tf_op args[1]
  45.2 3.9 %copy-done = f32[500,5000]{1,0:T(8,128)S(1)} copy-done((f32[500,5000]{1,0:T(8,128)S(1)}, f32[500,5000]{1,0:T(8,128)}, u32[]{:S(2)}) %copy-start) | copy-done | bytes 10000024
  49.1 8.4 %fold_weights.1 = (bf16[40,128,160]{2,1,0:T(8,128)(2,1)S(1)}, bf16[40,128,160]{2,1,0:T(8,128)(2,1)S(1)}) custom-call(s32[1,500]{1,0:T(1,128)S(1)} %add.175.place_ref, s32[500,1]{1,0:T(8,128)S(1)} %copy.62.need_ref, s32[1,5120]{1,0:T(1,128)S(1)} %xor.217.have_ref, f32[500,5000]{1,0:T(8,128)S(1)} %copy-done), custom_call_target="tpu_custom_call" | custom-call | tf_op jit(solution)/shard_map/fold_weights/pallas_call | solution.py:142
  58.2 2.0 %broadcast_xor_fusion.3 = (s32[25,64,128]{2,1,0:T(8,128)S(1)}, s32[25,64,128]{2,1,0:T(8,128)S(1)}) fusion(s32[128]{0:T(128)S(1)} %concatenate.6, s32[25,64]{1,0:T(8,128)S(1)} %copy.59, s32[25,64]{1,0:T(8,128)S(1)} %get-tuple-element.58, s32[25,64]{1,0:T(8,128)S(1)} %get-tuple-element.59, s32[25,64]{1,0:T(8,128)S(1)} %get-tuple-element.60, ...), kind=kLoop, calls=%fused_computation.55 | loop fusion | flops 5120000 | bytes 1697024 | tf_op jit(solution)/shard_map/xor | solution.py:247
  61.8 1.7 %copy-done.2 = bf16[40,128,160]{2,1,0:T(8,128)(2,1)S(1)} copy-done((bf16[40,128,160]{2,1,0:T(8,128)(2,1)S(1)}, bf16[40,128,160]{2,1,0:T(8,128)(2,1)}, u32[]{:S(2)}) %copy-start.2) | copy-done | bytes 1638424
  63.6 1.7 %copy-done.4 = bf16[40,128,160]{2,1,0:T(8,128)(2,1)S(1)} copy-done((bf16[40,128,160]{2,1,0:T(8,128)(2,1)S(1)}, bf16[40,128,160]{2,1,0:T(8,128)(2,1)}, u32[]{:S(2)}) %copy-start.4) | copy-done | bytes 1638424
  65.3 15.4 %contract.1 = f32[4,40,160]{2,1,0:T(8,128)S(1)} custom-call(f32[64,4,640]{2,1,0:T(4,128)} %all-to-all-done.x_ref, s32[25,256,128]{2,1,0:T(8,128)S(1)} %compare_select_fusion.slot_ref, bf16[40,128,160]{2,1,0:T(8,128)(2,1)S(1)} %copy-done.2, bf16[40,128,160]{2,1,0:T(8,128)(2,1)S(1)} %copy-done.4), custom_call_target="tpu_custom_call" | custom-call | tf_op jit(solution)/shard_map/contract/pallas_call | solution.py:196
  80.7 1.6 %collective-permute-start = (f32[2,40,160]{2,1,0:T(8,128)S(1)}, f32[2,40,160]{2,1,0:T(8,128)S(1)}, u32[]{:S(2)}, u32[]{:S(2)}) collective-permute-start(f32[2,40,160]{2,1,0:T(8,128)S(1)} %slice.79), channel_id=1, source_target_pairs={{0,64},{64,0},{128,192},{192,128},{1,65},{65,1},{129,193},{193,129... | collective-permute-start | bytes 153608 | tf_op jit(solution)/shard_map/ppermute | solution.py:264
  82.4 2.9 %collective-permute-done = f32[2,40,160]{2,1,0:T(8,128)S(1)} collective-permute-done((f32[2,40,160]{2,1,0:T(8,128)S(1)}, f32[2,40,160]{2,1,0:T(8,128)S(1)}, u32[]{:S(2)}, u32[]{:S(2)}) %collective-permute-start) | collective-permute-done | bytes 51232 | tf_op jit(solution)/shard_map/ppermute | solution.py:264
  85.9 2.8 %collective-permute-start.1 = (f32[40,160]{1,0:T(8,128)S(1)}, f32[40,160]{1,0:T(8,128)S(1)}, u32[]{:S(2)}, u32[]{:S(2)}) collective-permute-start(f32[40,160]{1,0:T(8,128)S(1)} %get-tuple-element.42), channel_id=1, source_target_pairs={{0,192},{64,128},{128,64},{192,0},{1,193},{65,129},{129,65},{193,1... | collective-permute-start | bytes 76808 | tf_op jit(solution)/shard_map/ppermute | solution.py:266
  88.8 0.7 copy.64.rank_ref
  89.5 0.7 copy.65.need_ref
  90.3 0.7 copy.66.row_ref
  91.6 0.6 sub.77.column_ref
  92.2 0.7 reduce_max.19
  92.9 0.7 reduce_max.18
  95.5 1.5 %finish.1 = f32[125,160]{1,0:T(8,128)S(1)} custom-call(f32[40,160]{1,0:T(8,128)} %get-tuple-element.43.a_ref, f32[40,160]{1,0:T(8,128)} %copy-done.9, s32[125,1]{1,0:T(8,128)} %copy.64.rank_ref, s32[125,1]{1,0:T(8,128)} %copy.65.need_ref, s32[1,160]{1,0:T(1,128)} %xor.224.have_ref, f32[125,1]{1,0:T(8,128)} %copy.66.row_ref, f32[1,160]{1,0:T(1,128)} %sub.77.column_ref), custom_call_target="tpu_custom_call" | custom-call | tf_op jit(solution)/shard_map/finish/pallas_call | solution.py:218
  97.4 0.6 copy-done.6
  (67 shorter events, 8.2 us)
Async XLA Ops:
  6.5 26.5 %copy-start.7 = (s32[40]{0:T(128)S(1)}, s32[40]{0:T(128)}, u32[]{:S(2)}) copy-start(s32[40]{0:T(128)} %occ_ref.1) | copy-start | bytes 484
  6.5 26.5 %copy-start.8 = (s32[500]{0:T(512)S(1)}, s32[500]{0:T(512)}, u32[]{:S(2)}) copy-start(s32[500]{0:T(512)} %param.11) | copy-start | bytes 6004
  14.7 47.1 %all-to-all-start = ((f32[64,4,640]{2,1,0:T(4,128)}), f32[64,4,640]{2,1,0:T(4,128)}, u32[]{:S(2)}, u32[]{:S(2)}) async-start(f32[64,4,640]{2,1,0:T(4,128)} %pack_amplitudes.1), calls=%async_computation.1 | async-start | bytes 1310720 | tf_op jit(solution)/shard_map/all_to_all | solution.py:228
  33.8 11.2 %copy-start.11 = (f32[500]{0:T(512)S(1)}, f32[500]{0:T(512)}, u32[]{:S(2)}) copy-start(f32[500]{0:T(512)} %param.13) | copy-start | bytes 6004
  33.8 11.3 %copy-start.10 = (f32[40]{0:T(128)S(1)}, f32[40]{0:T(128)}, u32[]{:S(2)}) copy-start(f32[40]{0:T(128)} %param.12) | copy-start | bytes 484
  45.2 3.9 %copy-start = (f32[500,5000]{1,0:T(8,128)S(1)}, f32[500,5000]{1,0:T(8,128)}, u32[]{:S(2)}) copy-start(f32[500,5000]{1,0:T(8,128)} %copy.63.w_ref) | copy-start | bytes 30000004
  57.5 3.8 %copy-start.1 = (bf16[40,128,160]{2,1,0:T(8,128)(2,1)}, bf16[40,128,160]{2,1,0:T(8,128)(2,1)S(1)}, u32[]{:S(2)}) copy-start(bf16[40,128,160]{2,1,0:T(8,128)(2,1)S(1)} %get-tuple-element.29.high_ref) | copy-start | bytes 4915204
  57.5 3.8 %copy-start.3 = (bf16[40,128,160]{2,1,0:T(8,128)(2,1)}, bf16[40,128,160]{2,1,0:T(8,128)(2,1)S(1)}, u32[]{:S(2)}) copy-start(bf16[40,128,160]{2,1,0:T(8,128)(2,1)S(1)} %get-tuple-element.30.low_ref) | copy-start | bytes 4915204
  61.8 1.7 %copy-start.2 = (bf16[40,128,160]{2,1,0:T(8,128)(2,1)S(1)}, bf16[40,128,160]{2,1,0:T(8,128)(2,1)}, u32[]{:S(2)}) copy-start(bf16[40,128,160]{2,1,0:T(8,128)(2,1)} %copy-done.1) | copy-start | bytes 4915204
  63.6 1.7 %copy-start.4 = (bf16[40,128,160]{2,1,0:T(8,128)(2,1)S(1)}, bf16[40,128,160]{2,1,0:T(8,128)(2,1)}, u32[]{:S(2)}) copy-start(bf16[40,128,160]{2,1,0:T(8,128)(2,1)} %copy-done.3) | copy-start | bytes 4915204
  80.7 4.6 %collective-permute-start = (f32[2,40,160]{2,1,0:T(8,128)S(1)}, f32[2,40,160]{2,1,0:T(8,128)S(1)}, u32[]{:S(2)}, u32[]{:S(2)}) collective-permute-start(f32[2,40,160]{2,1,0:T(8,128)S(1)} %slice.79), channel_id=1, source_target_pairs={{0,64},{64,0},{128,192},{192,128},{1,65},{65,1},{129,193},{193,129... | collective-permute-start | bytes 153608 | tf_op jit(solution)/shard_map/ppermute | solution.py:264
  85.9 9.0 %collective-permute-start.1 = (f32[40,160]{1,0:T(8,128)S(1)}, f32[40,160]{1,0:T(8,128)S(1)}, u32[]{:S(2)}, u32[]{:S(2)}) collective-permute-start(f32[40,160]{1,0:T(8,128)S(1)} %get-tuple-element.42), channel_id=1, source_target_pairs={{0,192},{64,128},{128,64},{192,0},{1,193},{65,129},{129,65},{193,1... | collective-permute-start | bytes 76808 | tf_op jit(solution)/shard_map/ppermute | solution.py:266
  94.9 0.6 copy-start.9
  97.4 0.6 copy-start.6

commit v2 on v1

v2 whole, which is shorter than its diff:
```python
import jax
import jax.numpy as jnp
from jax import lax
from jax.experimental import pallas as pl
from jax.experimental.pallas import tpu as pltpu
from jax.sharding import PartitionSpec as P

O = 40
V = 500
IW = 1
BW = 256
G = 4
M = 64
CL = V // G
CP = 128
T = O * O // M
TS = 5
BL = BW // M
J4 = O * BL
SLOTS = 640
FOLD = 40
NF = G * FOLD
STEP_SLOTS = ((0, 176), (16, 304), (48, 416), (112, 528), (160, SLOTS))
PAIR_BLOCKS = ((0, 1),) * 3 + ((0, 2),) * 5 + ((0, 3),) * 5 + ((0, 4),) * 4 + ((1, 4),) * 2 + ((1, 5),) * 6
SLOT_FROM = tuple(max(CP * PAIR_BLOCKS[t][0], STEP_SLOTS[t // TS][0]) for t in range(T))
SLOT_TO = tuple(min(CP * PAIR_BLOCKS[t][1], STEP_SLOTS[t // TS][1]) for t in range(T))
NONE = 16

HIGHEST = lax.Precision.HIGHEST
F32 = jnp.float32
BF16 = jnp.bfloat16
I32 = jnp.int32


def dot(a, b):
    return jnp.dot(a, b, preferred_element_type=F32)


def halves(x):
    high = x.astype(BF16)
    return high, (x - high.astype(F32)).astype(BF16)


def iota(shape, dim):
    return lax.broadcasted_iota(I32, shape, dim)


def pack_kernel(occ_ref, vir_ref, amp_ref, out_ref, rank_ref, column_ref, count_ref, base_ref, total_ref, pick_ref, high_ref, low_ref):
    step = pl.program_id(0)
    g = lax.axis_index("grp")
    m = lax.axis_index("blk")
    row = vir_ref[:, 0:CP]
    for other in range(1, G):
        row = jnp.where(g == other, vir_ref[:, other * CL : other * CL + CP], row)
    row = jnp.where(iota((1, CP), 1) < CL, row, NONE)

    @pl.when(step == 0)
    def _():
        wide = jnp.broadcast_to(row, (CP, CP))
        column = jnp.transpose(wide)
        column_ref[...] = column
        before = (wide == column) & (iota((CP, CP), 0) < iota((CP, CP), 1))
        rank_ref[...] = jnp.sum(before.astype(F32), axis=0, keepdims=True).astype(I32)
        for q in range(8):
            same = (iota((8, CP), 0) == jnp.bitwise_xor(row, q)).astype(F32)
            count_ref[q] = jnp.broadcast_to(jnp.sum(same, axis=1, keepdims=True), (8, CP)).astype(I32)
        base_ref[...] = jnp.zeros_like(base_ref)
        total_ref[...] = jnp.zeros_like(total_ref)

    for phase, (first, last) in enumerate(STEP_SLOTS):

        @pl.when(step == phase)
        def _():
            for t in range(TS):
                pair = m * T + phase * TS + t
                q = jnp.bitwise_xor(occ_ref[pair // O], occ_ref[pair % O])
                same = iota((8, CP), 0) == jnp.bitwise_xor(row, q)
                base = jnp.sum(jnp.where(same, base_ref[...], 0).astype(F32), axis=0, keepdims=True).astype(I32)
                slot = base + rank_ref[...] - first
                base_ref[...] += count_ref[q]
                columns = slice(t * CP, (t + 1) * CP)
                pick_ref[0 : last - first, columns] = (iota((last - first, CP), 0) == slot).astype(F32).astype(BF16)
                need = jnp.bitwise_xor(column_ref[...], q)
                for half in range(BW // CP):
                    lanes = slice(half * CP, (half + 1) * CP)
                    block = jnp.where(need == vir_ref[:, lanes], amp_ref[t, :, lanes], 0.0)
                    high, low = halves(block)
                    high_ref[columns, lanes] = high
                    low_ref[columns, lanes] = low
            pick = pick_ref[0 : last - first]
            total_ref[first:last] += dot(pick, high_ref[...]) + dot(pick, low_ref[...])

    @pl.when(step == pl.num_programs(0) - 1)
    def _():
        out_ref[...] = jnp.transpose(total_ref[...]).reshape(M, BL, SLOTS)


def pack(occ_irrep, vir_row, amplitudes):
    return pl.pallas_call(
        pack_kernel,
        name="pack_amplitudes",
        grid=(T // TS,),
        out_shape=jax.ShapeDtypeStruct((M, BL, SLOTS), F32),
        in_specs=[
            pl.BlockSpec(memory_space=pltpu.SMEM),
            pl.BlockSpec((1, G * CP), lambda s: (0, 0)),
            pl.BlockSpec((TS, CP, BW), lambda s: (s, 0, 0)),
        ],
        out_specs=pl.BlockSpec((M, BL, SLOTS), lambda s: (0, 0, 0)),
        scratch_shapes=[
            pltpu.VMEM((1, CP), I32),
            pltpu.VMEM((CP, CP), I32),
            pltpu.VMEM((8, 8, CP), I32),
            pltpu.VMEM((8, CP), I32),
            pltpu.VMEM((SLOTS, BW), F32),
            pltpu.VMEM((SLOTS, TS * CP), BF16),
            pltpu.VMEM((TS * CP, BW), BF16),
            pltpu.VMEM((TS * CP, BW), BF16),
        ],
        compiler_params=pltpu.CompilerParams(vmem_limit_bytes=16 << 20),
    )(occ_irrep, vir_row, amplitudes)


CS = 16


def fold_kernel(place_ref, need_ref, have_ref, w_ref, high_ref, low_ref, pick_ref, turn_ref, rest_ref, first_ref, second_ref):
    step = pl.program_id(0)

    @pl.when(step == 0)
    def _():
        for first in range(0, V, CP):
            lanes = slice(first, min(first + CP, V))
            place = jnp.transpose(jnp.broadcast_to(place_ref[:, lanes], (CP, min(CP, V - first))))
            for at in range(0, NF, CP):
                wide = min(CP, NF - at)
                hit = iota((min(CP, V - first), wide), 1) + at == place[:, 0:wide]
                pick_ref[lanes, at : at + wide] = hit.astype(F32).astype(BF16)

    for part in range(CS * O // CP):
        rows = slice(part * CP, (part + 1) * CP)
        have = jnp.transpose(jnp.broadcast_to(have_ref[:, rows], (CP, CP)))
        for first in range(0, V, CP):
            lanes = slice(first, min(first + CP, V))
            kept = jnp.where(need_ref[:, lanes] == have[:, : min(CP, V - first)], w_ref[rows, lanes], 0.0)
            high, low = halves(kept)
            first_ref[rows, lanes] = high
            second_ref[rows, lanes] = low
    folded = dot(first_ref[...], pick_ref[...]) + dot(second_ref[...], pick_ref[...])
    turn_ref[...] = folded[:, 0:CP]
    rest_ref[:, 0 : NF - CP] = folded[:, CP:NF]
    for k in range(O):
        rows = pl.ds(k, CS, stride=O)
        part = jnp.concatenate([turn_ref[rows, :], rest_ref[rows, :]], axis=1)
        high, low = halves(part[:, 0:NF])
        high_ref[k] = high
        low_ref[k] = low


def fold(place, need, have, turned_weight):
    rows = CS * O
    out = jax.ShapeDtypeStruct((O, CP, NF), BF16)
    spec = pl.BlockSpec((O, CS, NF), lambda s: (0, s, 0))
    return pl.pallas_call(
        fold_kernel,
        name="fold_weights",
        grid=(CP // CS,),
        out_shape=(out, out),
        in_specs=[
            pl.BlockSpec((1, V), lambda s: (0, 0)),
            pl.BlockSpec((1, V), lambda s: (0, 0)),
            pl.BlockSpec((1, rows), lambda s: (0, s)),
            pl.BlockSpec((rows, V), lambda s: (s, 0)),
        ],
        out_specs=(spec, spec),
        scratch_shapes=[pltpu.VMEM((V, NF), BF16), pltpu.VMEM((rows, CP), F32), pltpu.VMEM((rows, CP), F32)]
        + [pltpu.VMEM((rows, V), BF16)] * 2,
        compiler_params=pltpu.CompilerParams(vmem_limit_bytes=16 << 20),
    )(place, need, have, turned_weight)


def contract_kernel(x_ref, slot_ref, far_high_ref, far_low_ref, out_ref, wide_ref, high_ref, low_ref, sem):
    g = lax.axis_index("grp")
    copies = [
        pltpu.make_async_copy(far_high_ref, high_ref, sem.at[0]),
        pltpu.make_async_copy(far_low_ref, low_ref, sem.at[1]),
    ]
    for copy in copies:
        copy.start()

    @pl.loop(0, M // 2)
    def _(i):
        packed = x_ref[pl.ds(2 * i, 2)].reshape(2 * BL, SLOTS)
        for t in range(T):
            slot = slot_ref[t, pl.ds(pl.multiple_of(8 * i, 8), 8), :]
            lane = jnp.bitwise_and(slot, CP - 1)
            where = jnp.right_shift(slot, 7)
            found = jnp.zeros((8, CP), F32)
            for part in range(*PAIR_BLOCKS[t]):
                taken = jnp.take_along_axis(
                    packed[:, part * CP : (part + 1) * CP], lane, axis=1, mode="promise_in_bounds"
                )
                found = jnp.where(where == part, taken, found)
            first = pl.multiple_of(2 * T * BL * i, 8)
            wide_ref[pl.ds(first + BL * t, BL), :] = found[0:BL]
            wide_ref[pl.ds(first + T * BL + BL * t, BL), :] = found[BL : 2 * BL]

    for copy in copies:
        copy.wait()
    total = jnp.zeros((J4, NF), F32)
    for i in range(O // 2):
        first = 2 * J4 * i
        amp = jnp.concatenate([wide_ref[first : first + J4], wide_ref[first + J4 : first + 2 * J4]], axis=1)
        a_high, a_low = halves(amp)
        w_high = high_ref[2 * i : 2 * i + 2].reshape(2 * CP, NF)
        w_low = low_ref[2 * i : 2 * i + 2].reshape(2 * CP, NF)
        total = total + (dot(a_high, w_high) + dot(a_high, w_low) + dot(a_low, w_high))

    turned = jnp.transpose(total)
    for block in range(G):
        out_ref[jnp.bitwise_xor(g, block)] = turned[block * FOLD : (block + 1) * FOLD]


def contract(received, slots, high, low):
    return pl.pallas_call(
        contract_kernel,
        name="contract",
        out_shape=jax.ShapeDtypeStruct((G, FOLD, J4), F32),
        in_specs=[
            pl.BlockSpec(memory_space=pltpu.VMEM),
            pl.BlockSpec(memory_space=pltpu.VMEM),
            pl.BlockSpec(memory_space=pl.ANY),
            pl.BlockSpec(memory_space=pl.ANY),
        ],
        scratch_shapes=[
            pltpu.VMEM((O * O * BL, CP), F32),
            pltpu.VMEM((O, CP, NF), BF16),
            pltpu.VMEM((O, CP, NF), BF16),
            pltpu.SemaphoreType.DMA((2,)),
        ],
        compiler_params=pltpu.CompilerParams(vmem_limit_bytes=24 << 20),
    )(received, slots, high, low)


def finish_kernel(a_ref, b_ref, rank_ref, need_ref, have_ref, row_ref, column_ref, out_ref):
    folded = a_ref[...] + b_ref[...]
    source = iota((J4, J4), 0)
    target = iota((J4, J4), 1)
    move = (source % BL) * O + source // BL == target
    folded = jnp.dot(folded, move.astype(F32), precision=HIGHEST, preferred_element_type=F32)
    pick = (iota((FOLD, CL), 0) == rank_ref[...]).astype(F32)
    wide = jnp.dot(jnp.transpose(folded), pick, precision=HIGHEST, preferred_element_type=F32)
    wide = jnp.where(need_ref[...] == have_ref[...], wide, 0.0)
    out_ref[...] = wide / (row_ref[...] + column_ref[...])


def finish(a, b, rank, need, have, row, column):
    return pl.pallas_call(
        finish_kernel,
        name="finish",
        out_shape=jax.ShapeDtypeStruct((J4, CL), F32),
        compiler_params=pltpu.CompilerParams(vmem_limit_bytes=4 << 20),
    )(a, b, rank, need, have, row, column)


def packed_form(amplitudes, cycle_weight, occ_irrep, vir_irrep, occ_energy, vir_energy):
    g = lax.axis_index("grp")
    m = lax.axis_index("blk")
    labels = jnp.arange(8, dtype=I32)
    sent = pack(occ_irrep, vir_irrep.reshape(1, V), amplitudes)
    received = lax.all_to_all(sent, "blk", 0, 0, tiled=True)

    shares = vir_irrep.reshape(G, CL)
    orbital = jnp.arange(CL)
    earlier = orbital[:, None] < orbital[None, :]
    ranks = jnp.sum((shares[:, :, None] == shares[:, None, :]) & earlier[None], axis=1).astype(I32)
    counts = jnp.sum(shares[:, :, None] == labels, axis=1).astype(I32)
    own = lax.dynamic_index_in_dim(shares, g, 0, keepdims=False)
    own_rank = lax.dynamic_index_in_dim(ranks, g, 0, keepdims=False)
    own_count = lax.dynamic_index_in_dim(counts, g, 0, keepdims=False)
    own_c = jnp.concatenate([own, jnp.full((CP - CL,), NONE, I32)])
    rank_c = jnp.concatenate([own_rank, jnp.zeros((CP - CL,), I32)])

    pairs = jnp.bitwise_xor(occ_irrep[:, None], occ_irrep[None, :]).reshape(M, T)
    kinds = (pairs[:, :, None] == labels).astype(I32)
    passed = jnp.cumsum(kinds, axis=1) - kinds
    crossed = jnp.bitwise_xor(labels[:, None], labels[None, :])
    per_kind = jnp.sum(jnp.where(crossed[:, :, None] == labels, own_count, 0), axis=2)
    base = jnp.sum(passed[:, :, :, None] * per_kind, axis=2)
    reach = jnp.bitwise_xor(pairs[:, :, None], own_c)
    slot = rank_c + sum(jnp.where(reach == u, base[:, :, u : u + 1], 0) for u in range(8))
    own_b = lax.dynamic_slice_in_dim(vir_irrep, m * BL, BL)
    slots = jnp.where(reach[:, :, None, :] == own_b[:, None], slot[:, :, None, :], -1)
    slots = jnp.transpose(slots, (1, 0, 2, 3)).reshape(T, M * BL, CP)

    all_kinds = jnp.sum(jnp.where(crossed[:, :, None] == labels, counts[:, None, None, :], 0), axis=3)
    before = jnp.sum(passed[None, :, :, :, None] * all_kinds[:, None, None], axis=3)
    least = jnp.min(before, axis=(0, 1, 3))
    most = jnp.max(before, axis=(0, 1, 3)) + jnp.max(counts)
    inside = (least >= jnp.array(SLOT_FROM)) & (most <= jnp.array(SLOT_TO))
    fits = jnp.all(inside) & (jnp.max(counts) <= FOLD)

    place = (jnp.minimum(ranks, FOLD) + jnp.where(ranks < FOLD, jnp.arange(G, dtype=I32)[:, None] * FOLD, V)).reshape(1, V)
    need = jnp.bitwise_xor(vir_irrep, occ_irrep[0]).reshape(1, V)
    have = jnp.bitwise_xor(own_c[:, None], occ_irrep[None, :]).reshape(1, CP * O)
    high, low = fold(place, need, have, cycle_weight.T)

    row_energy = (occ_energy[0] - lax.dynamic_slice_in_dim(vir_energy, g * CL, CL)).reshape(1, CL)
    slab_energy = lax.dynamic_slice_in_dim(vir_energy, m * BL, BL)
    col_energy = (occ_energy[None, :] - slab_energy[:, None]).reshape(J4, 1)
    row_need = jnp.bitwise_xor(own, occ_irrep[0]).reshape(1, CL)
    col_have = jnp.bitwise_xor(occ_irrep[None, :], own_b[:, None]).reshape(J4, 1)
    row_rank = own_rank.reshape(1, CL)
    slots, fits, row_rank, row_need, col_have, row_energy, col_energy = lax.optimization_barrier(
        (slots, fits, row_rank, row_need, col_have, row_energy, col_energy)
    )

    partial = contract(received, slots, high, low)
    near = lax.ppermute(partial[1:3], "grp", [(d, d ^ 1) for d in range(G)])
    mine = partial[0] + near[0]
    last = lax.ppermute(partial[3] + near[1], "grp", [(d, d ^ 3) for d in range(G)])
    out = finish(mine, last, row_rank, row_need, col_have, row_energy, col_energy)
    return out.T, fits


def plain_form(amplitudes, cycle_weight, occ_irrep, vir_irrep, occ_energy, vir_energy):
    g = lax.axis_index("grp")
    m = lax.axis_index("blk")
    own = lax.dynamic_slice_in_dim(vir_irrep, g * CL, CL)
    own_b = lax.dynamic_slice_in_dim(vir_irrep, m * BL, BL)
    sent = jnp.transpose(amplitudes.reshape(T * CL, BW)).reshape(M, BL, T * CL)
    received = lax.all_to_all(sent, "blk", 0, 0, tiled=True)
    amp = jnp.transpose(received.reshape(M, BL, T, CL), (0, 2, 1, 3)).reshape(O, O, BL, CL)
    pairs = jnp.bitwise_xor(occ_irrep[:, None], occ_irrep[None, :])
    allowed = jnp.bitwise_xor(pairs[:, :, None], own_b)[..., None] == own
    amp = jnp.where(allowed, amp, jnp.zeros_like(amp))
    weight = cycle_weight.reshape(V, CL, O)
    need = jnp.bitwise_xor(vir_irrep, occ_irrep[0])
    have = jnp.bitwise_xor(own[:, None], occ_irrep[None, :])
    weight = jnp.where(need[:, None, None] == have, weight, jnp.zeros_like(weight))
    partial = jnp.einsum("kjbc,xck->xbj", amp, weight, precision=HIGHEST).reshape(G, CL, J4)
    cycle = jnp.sum(lax.all_to_all(partial, "grp", 0, 0, tiled=True).reshape(G, CL, J4), axis=0)
    row_energy = occ_energy[0] - lax.dynamic_slice_in_dim(vir_energy, g * CL, CL)
    slab_energy = lax.dynamic_slice_in_dim(vir_energy, m * BL, BL)
    col_energy = (occ_energy[None, :] - slab_energy[:, None]).reshape(J4)
    return cycle / (row_energy[:, None] + col_energy[None, :])


def shards(*arrays):
    out, fits = packed_form(*arrays)
    return lax.cond(fits, lambda: out, lambda: plain_form(*arrays))


def solution(mesh):
    in_specs = (P("blk", "grp", None), P(None, "grp"), P(), P(), P(), P())
    out_specs = P("grp", "blk")
    return jax.shard_map(shards, mesh=mesh, in_specs=in_specs, out_specs=out_specs, check_vma=False)
```

time: 105 us -> 71.1 us (0.68)
  local copies, waits for them, and re-layouts: 26.7 us -> 9.99 us
  between operations: 15 us -> 1.68 us
  Pallas kernels: 33.4 us -> 28 us
  waiting for transfers between devices: 2.91 us -> 5.23 us
  other arithmetic: 9.97 us -> 8.63 us
    unnamed x23 -> x22, local copies, waits for them, and re-layouts: 19.8 us -> 7.16 us
    pallas_call x1, Pallas kernels: 15.4 us -> 10.5 us  [contract(): pl.pallas_call(contract_kernel, name='contract', out_shape=jax.ShapeDtype...]
    ppermute x1, waiting for transfers between devices: 0.01 us -> 2.22 us  [packed_form(): lax.ppermute(partial[3] + near[1], 'grp', [(d, d ^ 3) for d in range(G)])]
    xor x3, other arithmetic: 2.05 us -> 0.15 us  [the longest x1 0.07 us: packed_form(): jnp.bitwise_xor(occ_irrep[None, :], own_b[:, None]).reshape(J4, 1)]
    reshape x4 -> x2, local copies, waits for them, and re-layouts: 1.63 us -> 0.21 us  [packed_form(): shares = vir_irrep.reshape(G, CL)]
    pallas_call x1, Pallas kernels: 8.36 us -> 9.77 us  [fold(): pl.pallas_call(fold_kernel, name='fold_weights', grid=(CP // CS,), out_sh...]
    reduce_and x0 -> x1, other arithmetic: none -> 1.36 us  [packed_form(): fits = jnp.all(inside) & (jnp.max(counts) <= FOLD)]
    xor x2 -> x1, local copies, waits for them, and re-layouts: 1.36 us -> 0.08 us  [packed_form(): jnp.bitwise_xor(occ_irrep[None, :], own_b[:, None]).reshape(J4, 1)]
  transfers between devices with their start and end apart: 3 -> 3, of which waited for: 1 -> 2; matrix products, arithmetic and copies ran while one was open for 26% -> 16% of each run, Pallas kernels for 8% -> 14%
where the time goes in v2:
time: 71.1 us; the launch traced here: 70.3 us
  Pallas kernels  28 us (39%)
  starting transfers between devices  16.8 us (24%)
  local copies, waits for them, and re-layouts  9.99 us (14%)
  other arithmetic  8.63 us (12%)
  waiting for transfers between devices  5.23 us (7%)
  between operations  1.68 us (2%)
    all_to_all x1, starting transfers between devices, packed_form(): received = lax.all_to_all(sent, 'blk', 0, 0, tiled=True)  12.4 us
    pallas_call x1, Pallas kernels, contract(): pl.pallas_call(contract_kernel, name='contract', out_shape=jax.ShapeDtype...  10.5 us
    pallas_call x1, Pallas kernels, fold(): pl.pallas_call(fold_kernel, name='fold_weights', grid=(CP // CS,), out_sh...  9.77 us
    unnamed x22, local copies, waits for them, and re-layouts  7.16 us
    pallas_call x1, Pallas kernels, pack(): pl.pallas_call(pack_kernel, name='pack_amplitudes', grid=(T // TS,), out_...  7.12 us
    ppermute x1, waiting for transfers between devices, packed_form(): near = lax.ppermute(partial[1:3], 'grp', [(d, d ^ 1) for d in range(G)])  3.01 us
    ppermute x1, starting transfers between devices, packed_form(): lax.ppermute(partial[3] + near[1], 'grp', [(d, d ^ 3) for d in range(G)])  2.84 us
    ppermute x1, waiting for transfers between devices, packed_form(): lax.ppermute(partial[3] + near[1], 'grp', [(d, d ^ 3) for d in range(G)])  2.22 us
  transfers between devices with their start and end apart: 3, of which 2 were waited for; matrix products, arithmetic and copies ran while one was open for 16% of the time, Pallas kernels for 14%

profile of v2, /device:TPU:8, one launch (start us, length us, event | category | flops | bytes accessed | tf_op | source)
XLA Modules:
  0.0 70.3 jit_solution(18044381340825605091)
XLA Ops:
  0.0 7.1 %pack_amplitudes.1 = f32[64,4,640]{2,1,0:T(4,128)} custom-call(s32[40]{0:T(128)} %occ_ref.1, s32[1,500]{1,0:T(1,128)} %bitcast.90, f32[25,125,256]{2,1,0:T(8,128)} %amp_ref.1), custom_call_target="tpu_custom_call" | custom-call | tf_op jit(solution)/shard_map/pack_amplitudes/pallas_call | solution.py:99
  7.1 12.4 %all-to-all-start.2 = ((f32[64,4,640]{2,1,0:T(4,128)}), f32[64,4,640]{2,1,0:T(4,128)}, u32[]{:S(2)}, u32[]{:S(2)}) async-start(f32[64,4,640]{2,1,0:T(4,128)} %pack_amplitudes.1), calls=%async_computation.2 | async-start | bytes 1310720 | tf_op jit(solution)/shard_map/all_to_all | solution.py:271
  20.8 0.5 convert_subtract_fusion
  22.1 0.6 select_reduce_fusion
  22.7 0.5 multiply_reduce_fusion
  23.2 1.0 %fusion.17 = (s32[25]{0:T(128)S(1)}, s32[25]{0:T(128)S(1)}) fusion(s32[4,64,25,8]{1,3,2,0:T(8,128)S(1)} %multiply_reduce_fusion), kind=kLoop, calls=%fused_computation.66 | loop fusion | flops 102350 | bytes 205000 | tf_op jit(solution)/shard_map/reduce_max | solution.py:299
  24.2 0.6 reduce_max.20
  25.1 1.4 %and_reduce_fusion = pred[]{:T(512)} fusion(s32[25]{0:T(128)S(1)} %copy-done.11, s32[25]{0:T(128)S(1)} %get-tuple-element.59, s32[25]{0:T(128)S(1)} %copy-done.10, s32[25]{0:T(128)S(1)} %get-tuple-element.58, s32[]{:T(128)} %reduce_max.20), kind=kLoop, calls=%fused_computation.54 | loop fusion | flops 124 | bytes 405 | tf_op jit(solution)/shard_map/reduce_and | solution.py:301
  26.5 2.0 %broadcast_xor_fusion.4 = (s32[25,64,128]{2,1,0:T(8,128)S(1)}, s32[25,64,128]{2,1,0:T(8,128)S(1)}) fusion(s32[128]{0:T(128)S(1)} %concatenate.6, s32[25,64]{1,0:T(8,128)S(1)} %copy.64, s32[25,64]{1,0:T(8,128)S(1)} %get-tuple-element.74, s32[25,64]{1,0:T(8,128)S(1)} %get-tuple-element.75, s32[25,64]{1,0:T(8,128)S(1)} %get-tuple-element.76, ...), kind=kLoop, calls=%fused_computation.30 | loop fusion | flops 5120000 | bytes 1697024 | tf_op jit(solution)/shard_map/xor | solution.py:290
  30.2 0.6 eq.208
  30.8 0.6 broadcast_in_dim.202
  31.4 0.6 compare_select_fusion.2.slot_ref
  32.4 9.8 %fold_weights.1 = (bf16[40,128,160]{2,1,0:T(8,128)(2,1)S(1)}, bf16[40,128,160]{2,1,0:T(8,128)(2,1)S(1)}) custom-call(s32[1,500]{1,0:T(1,128)S(1)} %add.153.place_ref, s32[1,500]{1,0:T(1,128)S(1)} %bitcast.77, s32[1,5120]{1,0:T(1,128)S(1)} %xor.205.have_ref, f32[5000,500]{1,0:T(8,128)} %bitcast.78), custom_call_target="tpu_custom_call" | custom-call | tf_op jit(solution)/shard_map/fold_weights/pallas_call | solution.py:164
  42.2 1.5 %copy-done = bf16[40,128,160]{2,1,0:T(8,128)(2,1)} copy-done((bf16[40,128,160]{2,1,0:T(8,128)(2,1)}, bf16[40,128,160]{2,1,0:T(8,128)(2,1)S(1)}, u32[]{:S(2)}) %copy-start) | copy-done | bytes 1638424
  43.7 1.5 %copy-done.2 = bf16[40,128,160]{2,1,0:T(8,128)(2,1)} copy-done((bf16[40,128,160]{2,1,0:T(8,128)(2,1)}, bf16[40,128,160]{2,1,0:T(8,128)(2,1)S(1)}, u32[]{:S(2)}) %copy-start.2) | copy-done | bytes 1638424
  45.2 1.7 %copy-done.1 = bf16[40,128,160]{2,1,0:T(8,128)(2,1)S(1)} copy-done((bf16[40,128,160]{2,1,0:T(8,128)(2,1)S(1)}, bf16[40,128,160]{2,1,0:T(8,128)(2,1)}, u32[]{:S(2)}) %copy-start.1) | copy-done | bytes 1638424
  46.9 1.7 %copy-done.3 = bf16[40,128,160]{2,1,0:T(8,128)(2,1)S(1)} copy-done((bf16[40,128,160]{2,1,0:T(8,128)(2,1)S(1)}, bf16[40,128,160]{2,1,0:T(8,128)(2,1)}, u32[]{:S(2)}) %copy-start.3) | copy-done | bytes 1638424
  48.7 10.5 %contract.1 = f32[4,40,160]{2,1,0:T(8,128)S(1)} custom-call(f32[64,4,640]{2,1,0:T(4,128)} %all-to-all-done.2.x_ref, s32[25,256,128]{2,1,0:T(8,128)S(1)} %compare_select_fusion.2.slot_ref, bf16[40,128,160]{2,1,0:T(8,128)(2,1)S(1)} %copy-done.1, bf16[40,128,160]{2,1,0:T(8,128)(2,1)S(1)} %copy-done.3), custom_call_target="tpu_custom_call" | custom-call | tf_op jit(solution)/shard_map/contract/pallas_call | solution.py:225
  59.2 1.6 %collective-permute-start = (f32[2,40,160]{2,1,0:T(8,128)S(1)}, f32[2,40,160]{2,1,0:T(8,128)S(1)}, u32[]{:S(2)}, u32[]{:S(2)}) collective-permute-start(f32[2,40,160]{2,1,0:T(8,128)S(1)} %slice.76), channel_id=1, source_target_pairs={{0,64},{64,0},{128,192},{192,128},{1,65},{65,1},{129,193},{193,129... | collective-permute-start | bytes 153608 | tf_op jit(solution)/shard_map/ppermute | solution.py:319
  60.8 3.0 %collective-permute-done = f32[2,40,160]{2,1,0:T(8,128)S(1)} collective-permute-done((f32[2,40,160]{2,1,0:T(8,128)S(1)}, f32[2,40,160]{2,1,0:T(8,128)S(1)}, u32[]{:S(2)}, u32[]{:S(2)}) %collective-permute-start) | collective-permute-done | bytes 51232 | tf_op jit(solution)/shard_map/ppermute | solution.py:319
  63.8 2.8 %collective-permute-start.1 = (f32[40,160]{1,0:T(8,128)S(1)}, f32[40,160]{1,0:T(8,128)S(1)}, u32[]{:S(2)}, u32[]{:S(2)}) collective-permute-start(f32[40,160]{1,0:T(8,128)S(1)} %get-tuple-element.60), channel_id=1, source_target_pairs={{0,192},{64,128},{128,64},{192,0},{1,193},{65,129},{129,65},{193,1... | collective-permute-start | bytes 76808 | tf_op jit(solution)/shard_map/ppermute | solution.py:321
  66.9 2.2 %collective-permute-done.1.b_ref = f32[40,160]{1,0:T(8,128)S(1)} collective-permute-done((f32[40,160]{1,0:T(8,128)S(1)}, f32[40,160]{1,0:T(8,128)S(1)}, u32[]{:S(2)}, u32[]{:S(2)}) %collective-permute-start.1) | collective-permute-done | bytes 25632 | tf_op jit(solution)/shard_map/ppermute | solution.py:321
  69.1 0.6 finish.1
  69.7 0.6 copy-done.5
  (63 shorter events, 3.2 us)
Async XLA Ops:
  0.0 19.7 %copy-start.6 = (s32[40]{0:T(128)S(1)}, s32[40]{0:T(128)}, u32[]{:S(2)}) copy-start(s32[40]{0:T(128)} %occ_ref.1) | copy-start | bytes 484
  0.0 19.6 %copy-start.7 = (s32[500]{0:T(512)S(1)}, s32[500]{0:T(512)}, u32[]{:S(2)}) copy-start(s32[500]{0:T(512)} %param.13) | copy-start | bytes 6004
  7.1 17.8 %copy-start.9 = (f32[500]{0:T(512)S(1)}, f32[500]{0:T(512)}, u32[]{:S(2)}) copy-start(f32[500]{0:T(512)} %param.15) | copy-start | bytes 6004
  7.1 17.9 %copy-start.8 = (f32[40]{0:T(128)S(1)}, f32[40]{0:T(128)}, u32[]{:S(2)}) copy-start(f32[40]{0:T(128)} %param.14) | copy-start | bytes 484
  7.1 18.0 %copy-start.10 = (s32[25]{0:T(128)S(1)}, s32[25]{0:T(128)}, u32[]{:S(2)}) copy-start(s32[25]{0:T(128)} %constant.84.clone) | copy-start | bytes 304
  7.1 18.0 %copy-start.11 = (s32[25]{0:T(128)S(1)}, s32[25]{0:T(128)}, u32[]{:S(2)}) copy-start(s32[25]{0:T(128)} %constant.85.clone) | copy-start | bytes 304
  7.1 38.0 %all-to-all-start.2 = ((f32[64,4,640]{2,1,0:T(4,128)}), f32[64,4,640]{2,1,0:T(4,128)}, u32[]{:S(2)}, u32[]{:S(2)}) async-start(f32[64,4,640]{2,1,0:T(4,128)} %pack_amplitudes.1), calls=%async_computation.2 | async-start | bytes 1310720 | tf_op jit(solution)/shard_map/all_to_all | solution.py:271
  42.2 1.5 %copy-start = (bf16[40,128,160]{2,1,0:T(8,128)(2,1)}, bf16[40,128,160]{2,1,0:T(8,128)(2,1)S(1)}, u32[]{:S(2)}) copy-start(bf16[40,128,160]{2,1,0:T(8,128)(2,1)S(1)} %get-tuple-element.38.far_high_ref) | copy-start | bytes 4915204
  43.7 1.5 %copy-start.2 = (bf16[40,128,160]{2,1,0:T(8,128)(2,1)}, bf16[40,128,160]{2,1,0:T(8,128)(2,1)S(1)}, u32[]{:S(2)}) copy-start(bf16[40,128,160]{2,1,0:T(8,128)(2,1)S(1)} %get-tuple-element.39.far_low_ref) | copy-start | bytes 4915204
  45.2 1.7 %copy-start.1 = (bf16[40,128,160]{2,1,0:T(8,128)(2,1)S(1)}, bf16[40,128,160]{2,1,0:T(8,128)(2,1)}, u32[]{:S(2)}) copy-start(bf16[40,128,160]{2,1,0:T(8,128)(2,1)} %copy-done) | copy-start | bytes 4915204
  46.9 1.7 %copy-start.3 = (bf16[40,128,160]{2,1,0:T(8,128)(2,1)S(1)}, bf16[40,128,160]{2,1,0:T(8,128)(2,1)}, u32[]{:S(2)}) copy-start(bf16[40,128,160]{2,1,0:T(8,128)(2,1)} %copy-done.2) | copy-start | bytes 4915204
  59.2 4.6 %collective-permute-start = (f32[2,40,160]{2,1,0:T(8,128)S(1)}, f32[2,40,160]{2,1,0:T(8,128)S(1)}, u32[]{:S(2)}, u32[]{:S(2)}) collective-permute-start(f32[2,40,160]{2,1,0:T(8,128)S(1)} %slice.76), channel_id=1, source_target_pairs={{0,64},{64,0},{128,192},{192,128},{1,65},{65,1},{129,193},{193,129... | collective-permute-start | bytes 153608 | tf_op jit(solution)/shard_map/ppermute | solution.py:319
  63.8 5.3 %collective-permute-start.1 = (f32[40,160]{1,0:T(8,128)S(1)}, f32[40,160]{1,0:T(8,128)S(1)}, u32[]{:S(2)}, u32[]{:S(2)}) collective-permute-start(f32[40,160]{1,0:T(8,128)S(1)} %get-tuple-element.60), channel_id=1, source_target_pairs={{0,192},{64,128},{128,64},{192,0},{1,193},{65,129},{129,65},{193,1... | collective-permute-start | bytes 76808 | tf_op jit(solution)/shard_map/ppermute | solution.py:321
  69.7 0.6 copy-start.5

commit v3 on v2

--- a/solution.py
+++ b/solution.py
@@ -41,6 +41,10 @@
     return high, (x - high.astype(F32)).astype(BF16)
 
 
+def in_hbm(x):
+    return pltpu.with_memory_space_constraint(x, pltpu.HBM)
+
+
 def iota(shape, dim):
     return lax.broadcasted_iota(I32, shape, dim)
 
@@ -117,7 +121,7 @@
             pltpu.VMEM((TS * CP, BW), BF16),
             pltpu.VMEM((TS * CP, BW), BF16),
         ],
-        compiler_params=pltpu.CompilerParams(vmem_limit_bytes=16 << 20),
+        compiler_params=pltpu.CompilerParams(vmem_limit_bytes=10 << 20),
     )(occ_irrep, vir_row, amplitudes)
 
 
@@ -159,7 +163,7 @@
 
 def fold(place, need, have, turned_weight):
     rows = CS * O
-    out = jax.ShapeDtypeStruct((O, CP, NF), BF16)
+    out = pltpu.HBM((O, CP, NF), BF16)
     spec = pl.BlockSpec((O, CS, NF), lambda s: (0, s, 0))
     return pl.pallas_call(
         fold_kernel,
@@ -175,7 +179,7 @@
         out_specs=(spec, spec),
         scratch_shapes=[pltpu.VMEM((V, NF), BF16), pltpu.VMEM((rows, CP), F32), pltpu.VMEM((rows, CP), F32)]
         + [pltpu.VMEM((rows, V), BF16)] * 2,
-        compiler_params=pltpu.CompilerParams(vmem_limit_bytes=16 << 20),
+        compiler_params=pltpu.CompilerParams(vmem_limit_bytes=10 << 20),
     )(place, need, have, turned_weight)
 
 
@@ -229,8 +233,8 @@
         in_specs=[
             pl.BlockSpec(memory_space=pltpu.VMEM),
             pl.BlockSpec(memory_space=pltpu.VMEM),
-            pl.BlockSpec(memory_space=pl.ANY),
-            pl.BlockSpec(memory_space=pl.ANY),
+            pl.BlockSpec(memory_space=pltpu.HBM),
+            pl.BlockSpec(memory_space=pltpu.HBM),
         ],
         scratch_shapes=[
             pltpu.VMEM((O * O * BL, CP), F32),
@@ -238,8 +242,8 @@
             pltpu.VMEM((O, CP, NF), BF16),
             pltpu.SemaphoreType.DMA((2,)),
         ],
-        compiler_params=pltpu.CompilerParams(vmem_limit_bytes=24 << 20),
-    )(received, slots, high, low)
+        compiler_params=pltpu.CompilerParams(vmem_limit_bytes=14 << 20),
+    )(received, slots, in_hbm(high), in_hbm(low))
 
 
 def finish_kernel(a_ref, b_ref, rank_ref, need_ref, have_ref, row_ref, column_ref, out_ref):
@@ -258,7 +262,7 @@
     return pl.pallas_call(
         finish_kernel,
         name="finish",
-        out_shape=jax.ShapeDtypeStruct((J4, CL), F32),
+        out_shape=pltpu.HBM((J4, CL), F32),
         compiler_params=pltpu.CompilerParams(vmem_limit_bytes=4 << 20),
     )(a, b, rank, need, have, row, column)
 

time: 71.1 us -> 65.6 us (0.923)
  local copies, waits for them, and re-layouts: 9.99 us -> 2.85 us
  Pallas kernels: 28 us -> 29.7 us
    unnamed x22 -> x12, local copies, waits for them, and re-layouts: 7.16 us -> 0.03 us
    pallas_call x1, Pallas kernels: 9.77 us -> 11.2 us  [fold(): pl.pallas_call(fold_kernel, name='fold_weights', grid=(CP // CS,), out_sh...]
  transfers between devices with their start and end apart: 3 -> 3, of which waited for: 2 -> 2; matrix products, arithmetic and copies ran while one was open for 16% -> 18% of each run, Pallas kernels for 14% -> 17%
where the time goes in v3:
time: 65.6 us; the launch traced here: 64.9 us
  Pallas kernels  29.7 us (45%)
  starting transfers between devices  16.8 us (26%)
  other arithmetic  8.63 us (13%)
  waiting for transfers between devices  5.22 us (8%)
  local copies, waits for them, and re-layouts  2.85 us (4%)
  between operations  1.64 us (2%)
    all_to_all x1, starting transfers between devices, packed_form(): received = lax.all_to_all(sent, 'blk', 0, 0, tiled=True)  12.4 us
    pallas_call x1, Pallas kernels, fold(): pl.pallas_call(fold_kernel, name='fold_weights', grid=(CP // CS,), out_sh...  11.2 us
    pallas_call x1, Pallas kernels, contract(): pl.pallas_call(contract_kernel, name='contract', out_shape=jax.ShapeDtype...  10.1 us
    pallas_call x1, Pallas kernels, pack(): pl.pallas_call(pack_kernel, name='pack_amplitudes', grid=(T // TS,), out_...  7.12 us
    ppermute x1, waiting for transfers between devices, packed_form(): near = lax.ppermute(partial[1:3], 'grp', [(d, d ^ 1) for d in range(G)])  3.01 us
    ppermute x1, starting transfers between devices, packed_form(): lax.ppermute(partial[3] + near[1], 'grp', [(d, d ^ 3) for d in range(G)])  2.85 us
    ppermute x1, waiting for transfers between devices, packed_form(): lax.ppermute(partial[3] + near[1], 'grp', [(d, d ^ 3) for d in range(G)])  2.21 us
    xor x1, other arithmetic, packed_form(): reach = jnp.bitwise_xor(pairs[:, :, None], own_c)  1.96 us
  transfers between devices with their start and end apart: 3, of which 2 were waited for; matrix products, arithmetic and copies ran while one was open for 18% of the time, Pallas kernels for 17%

profile of v3, /device:TPU:8, one launch (start us, length us, event | category | flops | bytes accessed | tf_op | source)
XLA Modules:
  0.0 64.9 jit_solution(1332622723215298635)
XLA Ops:
  0.0 7.1 %pack_amplitudes.1 = f32[64,4,640]{2,1,0:T(4,128)} custom-call(s32[40]{0:T(128)} %occ_ref.1, s32[1,500]{1,0:T(1,128)} %bitcast.90, f32[25,125,256]{2,1,0:T(8,128)} %amp_ref.1), custom_call_target="tpu_custom_call" | custom-call | tf_op jit(solution)/shard_map/pack_amplitudes/pallas_call | solution.py:103
  7.1 12.4 %all-to-all-start.2 = ((f32[64,4,640]{2,1,0:T(4,128)}), f32[64,4,640]{2,1,0:T(4,128)}, u32[]{:S(2)}, u32[]{:S(2)}) async-start(f32[64,4,640]{2,1,0:T(4,128)} %pack_amplitudes.1), calls=%async_computation.2 | async-start | bytes 1310720 | tf_op jit(solution)/shard_map/all_to_all | solution.py:275
  19.8 0.1 convert_reduce_fusion.1
  20.1 0.2 convert_reduce_fusion
  20.4 0.3 select_reduce_fusion.1
  20.8 0.5 convert_subtract_fusion
  21.4 0.3 copy.67
  21.6 0.2 multiply_reduce_fusion.1
  22.1 0.6 select_reduce_fusion
  22.7 0.5 multiply_reduce_fusion
  23.2 1.0 %fusion.17 = (s32[25]{0:T(128)S(1)}, s32[25]{0:T(128)S(1)}) fusion(s32[4,64,25,8]{1,3,2,0:T(8,128)S(1)} %multiply_reduce_fusion), kind=kLoop, calls=%fused_computation.66 | loop fusion | flops 102350 | bytes 205000 | tf_op jit(solution)/shard_map/reduce_max | solution.py:303
  24.2 0.6 reduce_max.20
  25.1 1.4 %and_reduce_fusion = pred[]{:T(512)} fusion(s32[25]{0:T(128)S(1)} %copy-done.6, s32[25]{0:T(128)S(1)} %get-tuple-element.59, s32[25]{0:T(128)S(1)} %copy-done.5, s32[25]{0:T(128)S(1)} %get-tuple-element.58, s32[]{:T(128)} %reduce_max.20), kind=kLoop, calls=%fused_computation.54 | loop fusion | flops 124 | bytes 405 | tf_op jit(solution)/shard_map/reduce_and | solution.py:305
  26.5 2.0 %broadcast_xor_fusion.4 = (s32[25,64,128]{2,1,0:T(8,128)S(1)}, s32[25,64,128]{2,1,0:T(8,128)S(1)}) fusion(s32[128]{0:T(128)S(1)} %concatenate.6, s32[25,64]{1,0:T(8,128)S(1)} %copy.64, s32[25,64]{1,0:T(8,128)S(1)} %get-tuple-element.74, s32[25,64]{1,0:T(8,128)S(1)} %get-tuple-element.75, s32[25,64]{1,0:T(8,128)S(1)} %get-tuple-element.76, ...), kind=kLoop, calls=%fused_computation.30 | loop fusion | flops 5120000 | bytes 1697024 | tf_op jit(solution)/shard_map/xor | solution.py:294
  30.2 0.6 eq.208
  30.8 0.6 broadcast_in_dim.202
  31.4 0.6 compare_select_fusion.2.slot_ref
  32.4 11.2 %fold_weights.1 = (bf16[40,128,160]{2,1,0:T(8,128)(2,1)}, bf16[40,128,160]{2,1,0:T(8,128)(2,1)}) custom-call(s32[1,500]{1,0:T(1,128)S(1)} %add.153.place_ref, s32[1,500]{1,0:T(1,128)S(1)} %bitcast.77, s32[1,5120]{1,0:T(1,128)S(1)} %xor.205.have_ref, f32[5000,500]{1,0:T(8,128)} %bitcast.78), custom_call_target="tpu_custom_call" | custom-call | tf_op jit(solution)/shard_map/fold_weights/pallas_call | solution.py:168
  43.6 10.1 %contract.1 = f32[4,40,160]{2,1,0:T(8,128)S(1)} custom-call(f32[64,4,640]{2,1,0:T(4,128)} %all-to-all-done.2.x_ref, s32[25,256,128]{2,1,0:T(8,128)S(1)} %compare_select_fusion.2.slot_ref, bf16[40,128,160]{2,1,0:T(8,128)(2,1)} %get-tuple-element.38.far_high_ref, bf16[40,128,160]{2,1,0:T(8,128)(2,1)} %get-tuple-element.39.far_low_ref), custom_call_target="tpu_custom_call" | custom-call | tf_op jit(solution)/shard_map/contract/pallas_call | solution.py:229
  53.7 1.6 %collective-permute-start = (f32[2,40,160]{2,1,0:T(8,128)S(1)}, f32[2,40,160]{2,1,0:T(8,128)S(1)}, u32[]{:S(2)}, u32[]{:S(2)}) collective-permute-start(f32[2,40,160]{2,1,0:T(8,128)S(1)} %slice.76), channel_id=1, source_target_pairs={{0,64},{64,0},{128,192},{192,128},{1,65},{65,1},{129,193},{193,129... | collective-permute-start | bytes 153608 | tf_op jit(solution)/shard_map/ppermute | solution.py:323
  55.3 3.0 %collective-permute-done = f32[2,40,160]{2,1,0:T(8,128)S(1)} collective-permute-done((f32[2,40,160]{2,1,0:T(8,128)S(1)}, f32[2,40,160]{2,1,0:T(8,128)S(1)}, u32[]{:S(2)}, u32[]{:S(2)}) %collective-permute-start) | collective-permute-done | bytes 51232 | tf_op jit(solution)/shard_map/ppermute | solution.py:323
  58.3 2.8 %collective-permute-start.1 = (f32[40,160]{1,0:T(8,128)S(1)}, f32[40,160]{1,0:T(8,128)S(1)}, u32[]{:S(2)}, u32[]{:S(2)}) collective-permute-start(f32[40,160]{1,0:T(8,128)S(1)} %get-tuple-element.60), channel_id=1, source_target_pairs={{0,192},{64,128},{128,64},{192,0},{1,193},{65,129},{129,65},{193,1... | collective-permute-start | bytes 76808 | tf_op jit(solution)/shard_map/ppermute | solution.py:325
  61.4 2.2 %collective-permute-done.1.b_ref = f32[40,160]{1,0:T(8,128)S(1)} collective-permute-done((f32[40,160]{1,0:T(8,128)S(1)}, f32[40,160]{1,0:T(8,128)S(1)}, u32[]{:S(2)}, u32[]{:S(2)}) %collective-permute-start.1) | collective-permute-done | bytes 25632 | tf_op jit(solution)/shard_map/ppermute | solution.py:325
  63.6 1.2 %finish.1 = f32[160,125]{1,0:T(8,128)} custom-call(f32[40,160]{1,0:T(8,128)S(1)} %get-tuple-element.61.a_ref, f32[40,160]{1,0:T(8,128)S(1)} %collective-permute-done.1.b_ref, s32[1,125]{1,0:T(1,128)S(1)} %constant_dynamic-slice_fusion.1.rank_ref, s32[1,125]{1,0:T(1,128)S(1)} %get-tuple-element.41.need_ref, s32[160,1]{1,0:T(8,128)S(1)} %copy.69.have_ref, ...), custom_call_target="tpu_custom_call" | custom-call | tf_op jit(solution)/shard_map/finish/pallas_call | solution.py:262
  (53 shorter events, 2.1 us)
Async XLA Ops:
  0.0 19.7 %copy-start.1 = (s32[40]{0:T(128)S(1)}, s32[40]{0:T(128)}, u32[]{:S(2)}) copy-start(s32[40]{0:T(128)} %occ_ref.1) | copy-start | bytes 484
  0.0 19.6 %copy-start.2 = (s32[500]{0:T(512)S(1)}, s32[500]{0:T(512)}, u32[]{:S(2)}) copy-start(s32[500]{0:T(512)} %param.13) | copy-start | bytes 6004
  7.1 17.8 %copy-start.4 = (f32[500]{0:T(512)S(1)}, f32[500]{0:T(512)}, u32[]{:S(2)}) copy-start(f32[500]{0:T(512)} %param.15) | copy-start | bytes 6004
  7.1 17.9 %copy-start.3 = (f32[40]{0:T(128)S(1)}, f32[40]{0:T(128)}, u32[]{:S(2)}) copy-start(f32[40]{0:T(128)} %param.14) | copy-start | bytes 484
  7.1 18.0 %copy-start.5 = (s32[25]{0:T(128)S(1)}, s32[25]{0:T(128)}, u32[]{:S(2)}) copy-start(s32[25]{0:T(128)} %constant.84.clone) | copy-start | bytes 304
  7.1 18.0 %copy-start.6 = (s32[25]{0:T(128)S(1)}, s32[25]{0:T(128)}, u32[]{:S(2)}) copy-start(s32[25]{0:T(128)} %constant.85.clone) | copy-start | bytes 304
  7.1 36.4 %all-to-all-start.2 = ((f32[64,4,640]{2,1,0:T(4,128)}), f32[64,4,640]{2,1,0:T(4,128)}, u32[]{:S(2)}, u32[]{:S(2)}) async-start(f32[64,4,640]{2,1,0:T(4,128)} %pack_amplitudes.1), calls=%async_computation.2 | async-start | bytes 1310720 | tf_op jit(solution)/shard_map/all_to_all | solution.py:275
  53.7 4.6 %collective-permute-start = (f32[2,40,160]{2,1,0:T(8,128)S(1)}, f32[2,40,160]{2,1,0:T(8,128)S(1)}, u32[]{:S(2)}, u32[]{:S(2)}) collective-permute-start(f32[2,40,160]{2,1,0:T(8,128)S(1)} %slice.76), channel_id=1, source_target_pairs={{0,64},{64,0},{128,192},{192,128},{1,65},{65,1},{129,193},{193,129... | collective-permute-start | bytes 153608 | tf_op jit(solution)/shard_map/ppermute | solution.py:323
  58.3 5.3 %collective-permute-start.1 = (f32[40,160]{1,0:T(8,128)S(1)}, f32[40,160]{1,0:T(8,128)S(1)}, u32[]{:S(2)}, u32[]{:S(2)}) collective-permute-start(f32[40,160]{1,0:T(8,128)S(1)} %get-tuple-element.60), channel_id=1, source_target_pairs={{0,192},{64,128},{128,64},{192,0},{1,193},{65,129},{129,65},{193,1... | collective-permute-start | bytes 76808 | tf_op jit(solution)/shard_map/ppermute | solution.py:325

commit v4 on v3

--- a/solution.py
+++ b/solution.py
@@ -20,10 +20,12 @@
 SLOTS = 640
 FOLD = 40
 NF = G * FOLD
+GT = 3
+NG = -(-T // GT)
 STEP_SLOTS = ((0, 176), (16, 304), (48, 416), (112, 528), (160, SLOTS))
-PAIR_BLOCKS = ((0, 1),) * 3 + ((0, 2),) * 5 + ((0, 3),) * 5 + ((0, 4),) * 4 + ((1, 4),) * 2 + ((1, 5),) * 6
-SLOT_FROM = tuple(max(CP * PAIR_BLOCKS[t][0], STEP_SLOTS[t // TS][0]) for t in range(T))
-SLOT_TO = tuple(min(CP * PAIR_BLOCKS[t][1], STEP_SLOTS[t // TS][1]) for t in range(T))
+GROUP_BLOCKS = ((0, 1), (0, 2), (0, 3), (0, 3), (0, 4), (0, 4), (1, 5), (1, 5), (1, 5))
+SLOT_FROM = tuple(max(CP * GROUP_BLOCKS[t // GT][0], STEP_SLOTS[t // TS][0]) for t in range(T))
+SLOT_TO = tuple(min(CP * GROUP_BLOCKS[t // GT][1], STEP_SLOTS[t // TS][1]) for t in range(T))
 NONE = 16
 
 HIGHEST = lax.Precision.HIGHEST
@@ -121,7 +123,7 @@
             pltpu.VMEM((TS * CP, BW), BF16),
             pltpu.VMEM((TS * CP, BW), BF16),
         ],
-        compiler_params=pltpu.CompilerParams(vmem_limit_bytes=10 << 20),
+        compiler_params=pltpu.CompilerParams(vmem_limit_bytes=8 << 20),
     )(occ_irrep, vir_row, amplitudes)
 
 
@@ -179,11 +181,13 @@
         out_specs=(spec, spec),
         scratch_shapes=[pltpu.VMEM((V, NF), BF16), pltpu.VMEM((rows, CP), F32), pltpu.VMEM((rows, CP), F32)]
         + [pltpu.VMEM((rows, V), BF16)] * 2,
-        compiler_params=pltpu.CompilerParams(vmem_limit_bytes=10 << 20),
+        compiler_params=pltpu.CompilerParams(vmem_limit_bytes=8 << 20),
     )(place, need, have, turned_weight)
 
 
-def contract_kernel(x_ref, slot_ref, far_high_ref, far_low_ref, out_ref, wide_ref, high_ref, low_ref, sem):
+def contract_kernel(
+    x_ref, slot_ref, valid_ref, rank_ref, far_high_ref, far_low_ref, out_ref, seen_ref, spread_ref, wide_ref, high_ref, low_ref, sem
+):
     g = lax.axis_index("grp")
     copies = [
         pltpu.make_async_copy(far_high_ref, high_ref, sem.at[0]),
@@ -195,19 +199,39 @@
     @pl.loop(0, M // 2)
     def _(i):
         packed = x_ref[pl.ds(2 * i, 2)].reshape(2 * BL, SLOTS)
-        for t in range(T):
-            slot = slot_ref[t, pl.ds(pl.multiple_of(8 * i, 8), 8), :]
+        rows = pl.ds(pl.multiple_of(8 * i, 8), 8)
+        for group, (first, last) in enumerate(GROUP_BLOCKS):
+            slot = slot_ref[group, rows, :]
             lane = jnp.bitwise_and(slot, CP - 1)
             where = jnp.right_shift(slot, 7)
             found = jnp.zeros((8, CP), F32)
-            for part in range(*PAIR_BLOCKS[t]):
+            for part in range(first, last):
                 taken = jnp.take_along_axis(
                     packed[:, part * CP : (part + 1) * CP], lane, axis=1, mode="promise_in_bounds"
                 )
                 found = jnp.where(where == part, taken, found)
-            first = pl.multiple_of(2 * T * BL * i, 8)
-            wide_ref[pl.ds(first + BL * t, BL), :] = found[0:BL]
-            wide_ref[pl.ds(first + T * BL + BL * t, BL), :] = found[BL : 2 * BL]
+            seen_ref[group, rows, :] = found
+
+    place = [(iota((CP, CP), 0) - at * FOLD == rank_ref[...]).astype(F32).astype(BF16) for at in range(GT)]
+    place = jnp.concatenate(place, axis=1)
+    place = jnp.concatenate([place, place], axis=0)
+    for group in range(NG):
+        spread_ref[group] = dot(jnp.concatenate(halves(seen_ref[group]), axis=1), place)
+
+    @pl.loop(0, M // 2)
+    def _(i):
+        rows = pl.ds(pl.multiple_of(8 * i, 8), 8)
+        first = pl.multiple_of(2 * T * BL * i, 8)
+        for t in range(T):
+            at = (t % GT) * CP
+            row = spread_ref[t // GT, rows, at : at + CP] * valid_ref[t, rows, :]
+            if t % 2 == 0:
+                one, two = row[0:BL], row[BL : 2 * BL]
+            else:
+                row = pltpu.roll(row, BL, 0)
+                one, two = row[BL : 2 * BL], row[0:BL]
+            wide_ref[pl.ds(first + BL * t, BL), :] = one
+            wide_ref[pl.ds(first + T * BL + BL * t, BL), :] = two
 
     for copy in copies:
         copy.wait()
@@ -225,25 +249,23 @@
         out_ref[jnp.bitwise_xor(g, block)] = turned[block * FOLD : (block + 1) * FOLD]
 
 
-def contract(received, slots, high, low):
+def contract(received, slots, valid, rank, high, low):
+    vmem = pl.BlockSpec(memory_space=pltpu.VMEM)
     return pl.pallas_call(
         contract_kernel,
         name="contract",
         out_shape=jax.ShapeDtypeStruct((G, FOLD, J4), F32),
-        in_specs=[
-            pl.BlockSpec(memory_space=pltpu.VMEM),
-            pl.BlockSpec(memory_space=pltpu.VMEM),
-            pl.BlockSpec(memory_space=pltpu.HBM),
-            pl.BlockSpec(memory_space=pltpu.HBM),
-        ],
+        in_specs=[vmem] * 4 + [pl.BlockSpec(memory_space=pltpu.HBM)] * 2,
         scratch_shapes=[
+            pltpu.VMEM((NG, M * BL, CP), F32),
+            pltpu.VMEM((NG, M * BL, GT * CP), F32),
             pltpu.VMEM((O * O * BL, CP), F32),
             pltpu.VMEM((O, CP, NF), BF16),
             pltpu.VMEM((O, CP, NF), BF16),
             pltpu.SemaphoreType.DMA((2,)),
         ],
-        compiler_params=pltpu.CompilerParams(vmem_limit_bytes=14 << 20),
-    )(received, slots, in_hbm(high), in_hbm(low))
+        compiler_params=pltpu.CompilerParams(vmem_limit_bytes=16 << 20),
+    )(received, slots, valid, rank, in_hbm(high), in_hbm(low))
 
 
 def finish_kernel(a_ref, b_ref, rank_ref, need_ref, have_ref, row_ref, column_ref, out_ref):
@@ -289,13 +311,23 @@
     kinds = (pairs[:, :, None] == labels).astype(I32)
     passed = jnp.cumsum(kinds, axis=1) - kinds
     crossed = jnp.bitwise_xor(labels[:, None], labels[None, :])
-    per_kind = jnp.sum(jnp.where(crossed[:, :, None] == labels, own_count, 0), axis=2)
-    base = jnp.sum(passed[:, :, :, None] * per_kind, axis=2)
-    reach = jnp.bitwise_xor(pairs[:, :, None], own_c)
-    slot = rank_c + sum(jnp.where(reach == u, base[:, :, u : u + 1], 0) for u in range(8))
     own_b = lax.dynamic_slice_in_dim(vir_irrep, m * BL, BL)
-    slots = jnp.where(reach[:, :, None, :] == own_b[:, None], slot[:, :, None, :], -1)
-    slots = jnp.transpose(slots, (1, 0, 2, 3)).reshape(T, M * BL, CP)
+    per_b = jnp.sum(jnp.where(jnp.bitwise_xor(labels[:, None], own_b)[:, :, None] == labels, own_count, 0), axis=2)
+    start = jnp.sum(passed[:, :, None, :] * per_b.T, axis=3)
+    amount = jnp.sum(kinds[:, :, None, :] * per_b.T, axis=3)
+
+    def by_group(x):
+        x = jnp.pad(jnp.transpose(x, (1, 0, 2)), ((0, NG * GT - T), (0, 0), (0, 0)))
+        return x.reshape(NG, GT, M * BL, 1)
+
+    start, amount = by_group(start), by_group(amount)
+    lanes = jnp.arange(CP, dtype=I32)
+    slots = jnp.full((NG, M * BL, CP), -1, I32)
+    for at in range(GT):
+        rank = lanes - at * FOLD
+        slots = jnp.where((rank >= 0) & (rank < jnp.minimum(amount[:, at], FOLD)), start[:, at] + rank, slots)
+    reach = jnp.bitwise_xor(pairs.T[:, :, None], own_c)
+    valid = (reach[:, :, None, :] == own_b[:, None]).astype(F32).reshape(T, M * BL, CP)
 
     all_kinds = jnp.sum(jnp.where(crossed[:, :, None] == labels, counts[:, None, None, :], 0), axis=3)
     before = jnp.sum(passed[None, :, :, :, None] * all_kinds[:, None, None], axis=3)
@@ -315,11 +347,11 @@
     row_need = jnp.bitwise_xor(own, occ_irrep[0]).reshape(1, CL)
     col_have = jnp.bitwise_xor(occ_irrep[None, :], own_b[:, None]).reshape(J4, 1)
     row_rank = own_rank.reshape(1, CL)
-    slots, fits, row_rank, row_need, col_have, row_energy, col_energy = lax.optimization_barrier(
-        (slots, fits, row_rank, row_need, col_have, row_energy, col_energy)
+    slots, valid, fits, row_rank, row_need, col_have, row_energy, col_energy = lax.optimization_barrier(
+        (slots, valid, fits, row_rank, row_need, col_have, row_energy, col_energy)
     )
 
-    partial = contract(received, slots, high, low)
+    partial = contract(received, slots, valid, rank_c.reshape(1, CP), high, low)
     near = lax.ppermute(partial[1:3], "grp", [(d, d ^ 1) for d in range(G)])
     mine = partial[0] + near[0]
     last = lax.ppermute(partial[3] + near[1], "grp", [(d, d ^ 3) for d in range(G)])

time: 65.6 us -> 70.8 us (1.079)
  local copies, waits for them, and re-layouts: 2.85 us -> 5.92 us
  other arithmetic: 8.63 us -> 10.9 us
    select_n x1, other arithmetic: 0.58 us -> 3.6 us  [packed_form(): jnp.where((rank >= 0) & (rank < jnp.minimum(amount[:, at], FOLD)), start[...]
    unnamed x12 -> x19, local copies, waits for them, and re-layouts: 0.03 us -> 2.16 us
    xor x1 -> x2, other arithmetic: 1.96 us -> 0.35 us  [the longest x1 0.27 us: packed_form(): reach = jnp.bitwise_xor(pairs.T[:, :, None], own_c)]
    reshape x2 -> x3, local copies, waits for them, and re-layouts: 0.21 us -> 1.1 us  [the longest x2 1.09 us: by_group(): return x.reshape(NG, GT, M * BL, 1)]
  transfers between devices with their start and end apart: 3 -> 3, of which waited for: 2 -> 2; matrix products, arithmetic and copies ran while one was open for 18% -> 22% of each run, Pallas kernels for 17% -> 16%
where the time goes in v4:
time: 70.8 us; the launch traced here: 70 us
  Pallas kernels  29.4 us (42%)
  starting transfers between devices  16.9 us (24%)
  other arithmetic  10.9 us (15%)
  local copies, waits for them, and re-layouts  5.92 us (8%)
  waiting for transfers between devices  5.22 us (7%)
  between operations  1.69 us (2%)
    all_to_all x1, starting transfers between devices, packed_form(): received = lax.all_to_all(sent, 'blk', 0, 0, tiled=True)  12.3 us
    pallas_call x1, Pallas kernels, fold(): pl.pallas_call(fold_kernel, name='fold_weights', grid=(CP // CS,), out_sh...  11.2 us
    pallas_call x1, Pallas kernels, contract(): pl.pallas_call(contract_kernel, name='contract', out_shape=jax.ShapeDtype...  9.85 us
    pallas_call x1, Pallas kernels, pack(): pl.pallas_call(pack_kernel, name='pack_amplitudes', grid=(T // TS,), out_...  7.1 us
    select_n x1, other arithmetic, packed_form(): jnp.where((rank >= 0) & (rank < jnp.minimum(amount[:, at], FOLD)), start[...  3.6 us
    ppermute x1, starting transfers between devices, packed_form(): lax.ppermute(partial[3] + near[1], 'grp', [(d, d ^ 3) for d in range(G)])  3.07 us
    ppermute x1, waiting for transfers between devices, packed_form(): near = lax.ppermute(partial[1:3], 'grp', [(d, d ^ 1) for d in range(G)])  3.01 us
    ppermute x1, waiting for transfers between devices, packed_form(): lax.ppermute(partial[3] + near[1], 'grp', [(d, d ^ 3) for d in range(G)])  2.21 us
  transfers between devices with their start and end apart: 3, of which 2 were waited for; matrix products, arithmetic and copies ran while one was open for 22% of the time, Pallas kernels for 16%

profile of v4, /device:TPU:8, one launch (start us, length us, event | category | flops | bytes accessed | tf_op | source)
XLA Modules:
  0.0 70.0 jit_solution(11908908341016071815)
XLA Ops:
  0.0 7.1 %pack_amplitudes.1 = f32[64,4,640]{2,1,0:T(4,128)} custom-call(s32[40]{0:T(128)} %occ_ref.1, s32[1,500]{1,0:T(1,128)} %bitcast.75, f32[25,125,256]{2,1,0:T(8,128)} %amp_ref.1), custom_call_target="tpu_custom_call" | custom-call | tf_op jit(solution)/shard_map/pack_amplitudes/pallas_call | solution.py:105
  7.1 12.3 %all-to-all-start.2 = ((f32[64,4,640]{2,1,0:T(4,128)}), f32[64,4,640]{2,1,0:T(4,128)}, u32[]{:S(2)}, u32[]{:S(2)}) async-start(f32[64,4,640]{2,1,0:T(4,128)} %pack_amplitudes.1), calls=%async_computation.2 | async-start | bytes 1310720 | tf_op jit(solution)/shard_map/all_to_all | solution.py:297
  19.7 0.5 reduce-window_subtract_fusion
  21.8 0.3 multiply_reduce_fusion.2
  22.2 0.3 copy.86
  22.7 0.5 reshape.368
  23.2 0.3 copy.87
  23.7 0.5 reshape.369
  24.6 0.6 select_reduce_fusion
  25.2 0.5 multiply_reduce_fusion
  25.7 1.0 %fusion.14 = (s32[25]{0:T(128)S(1)}, s32[25]{0:T(128)S(1)}) fusion(s32[4,64,25,8]{1,3,2,0:T(8,128)S(1)} %multiply_reduce_fusion), kind=kLoop, calls=%fused_computation.66 | loop fusion | flops 102350 | bytes 205000 | tf_op jit(solution)/shard_map/reduce_max | solution.py:335
  26.7 0.6 reduce_max.20
  27.9 0.6 eq.134
  28.6 0.4 compare_convert_fusion.valid_ref
  29.3 1.4 %and_reduce_fusion = pred[]{:T(512)} fusion(s32[25]{0:T(128)S(1)} %copy-done.7, s32[25]{0:T(128)S(1)} %get-tuple-element.61, s32[25]{0:T(128)S(1)} %copy-done.6, s32[25]{0:T(128)S(1)} %get-tuple-element.60, s32[]{:T(128)} %reduce_max.20), kind=kLoop, calls=%fused_computation.49 | loop fusion | flops 124 | bytes 405 | tf_op jit(solution)/shard_map/reduce_and | solution.py:337
  32.3 3.6 %select_select_fusion.slot_ref = s32[9,256,128]{2,1,0:T(8,128)} fusion(s32[9,256]{1,0:T(8,128)S(1)} %get-tuple-element.76, s32[9,256]{1,0:T(8,128)S(1)} %get-tuple-element.78, s32[9,256]{1,0:T(8,128)S(1)} %get-tuple-element.77, s32[9,256]{1,0:T(8,128)S(1)} %get-tuple-element.79, s32[128]{0:T(128)S(1)} %get-tuple-element.82, ...), kind=kLoop, calls=%fused_computation.15 | loop fusion | flops 3244032 | bytes 1236224 | tf_op jit(solution)/shard_map/jit(_where)/select_n | solution.py:328
  36.3 11.2 %fold_weights.1 = (bf16[40,128,160]{2,1,0:T(8,128)(2,1)}, bf16[40,128,160]{2,1,0:T(8,128)(2,1)}) custom-call(s32[1,500]{1,0:T(1,128)S(1)} %add.143.place_ref, s32[1,500]{1,0:T(1,128)S(1)} %bitcast.61, s32[1,5120]{1,0:T(1,128)S(1)} %xor.212.have_ref, f32[5000,500]{1,0:T(8,128)} %bitcast.62), custom_call_target="tpu_custom_call" | custom-call | tf_op jit(solution)/shard_map/fold_weights/pallas_call | solution.py:170
  47.5 1.3 %copy-done = s32[9,256,128]{2,1,0:T(8,128)S(1)} copy-done((s32[9,256,128]{2,1,0:T(8,128)S(1)}, s32[9,256,128]{2,1,0:T(8,128)}, u32[]{:S(2)}) %copy-start) | copy-done | bytes 1179672
  48.8 9.8 %contract.1 = f32[4,40,160]{2,1,0:T(8,128)S(1)} custom-call(f32[64,4,640]{2,1,0:T(4,128)} %all-to-all-done.2.x_ref, s32[9,256,128]{2,1,0:T(8,128)S(1)} %copy-done, f32[25,256,128]{2,1,0:T(8,128)S(1)} %compare_convert_fusion.valid_ref, s32[1,128]{1,0:T(1,128)S(1)} %pad_bitcast_fusion.rank_ref, bf16[40,128,160]{2,1,0:T(8,128)(2,1)} %get-tuple-element.40.far_high_ref, ...), custom_call_target="tpu_custom_call" | custom-call | tf_op jit(solution)/shard_map/contract/pallas_call | solution.py:254
  58.6 1.6 %collective-permute-start = (f32[2,40,160]{2,1,0:T(8,128)S(1)}, f32[2,40,160]{2,1,0:T(8,128)S(1)}, u32[]{:S(2)}, u32[]{:S(2)}) collective-permute-start(f32[2,40,160]{2,1,0:T(8,128)S(1)} %slice.66), channel_id=1, source_target_pairs={{0,64},{64,0},{128,192},{192,128},{1,65},{65,1},{129,193},{193,129... | collective-permute-start | bytes 153608 | tf_op jit(solution)/shard_map/ppermute | solution.py:355
  60.2 3.0 %collective-permute-done = f32[2,40,160]{2,1,0:T(8,128)S(1)} collective-permute-done((f32[2,40,160]{2,1,0:T(8,128)S(1)}, f32[2,40,160]{2,1,0:T(8,128)S(1)}, u32[]{:S(2)}, u32[]{:S(2)}) %collective-permute-start) | collective-permute-done | bytes 51232 | tf_op jit(solution)/shard_map/ppermute | solution.py:355
  63.2 3.1 %collective-permute-start.1 = (f32[40,160]{1,0:T(8,128)S(1)}, f32[40,160]{1,0:T(8,128)S(1)}, u32[]{:S(2)}, u32[]{:S(2)}) collective-permute-start(f32[40,160]{1,0:T(8,128)S(1)} %get-tuple-element.64), channel_id=1, source_target_pairs={{0,192},{64,128},{128,64},{192,0},{1,193},{65,129},{129,65},{193,1... | collective-permute-start | bytes 76808 | tf_op jit(solution)/shard_map/ppermute | solution.py:357
  66.5 2.2 %collective-permute-done.1.b_ref = f32[40,160]{1,0:T(8,128)S(1)} collective-permute-done((f32[40,160]{1,0:T(8,128)S(1)}, f32[40,160]{1,0:T(8,128)S(1)}, u32[]{:S(2)}, u32[]{:S(2)}) %collective-permute-start.1) | collective-permute-done | bytes 25632 | tf_op jit(solution)/shard_map/ppermute | solution.py:357
  68.8 1.2 %finish.1 = f32[160,125]{1,0:T(8,128)} custom-call(f32[40,160]{1,0:T(8,128)S(1)} %get-tuple-element.65.a_ref, f32[40,160]{1,0:T(8,128)S(1)} %collective-permute-done.1.b_ref, s32[1,125]{1,0:T(1,128)S(1)} %constant_dynamic-slice_fusion.rank_ref, s32[1,125]{1,0:T(1,128)S(1)} %get-tuple-element.43.need_ref, s32[160,1]{1,0:T(8,128)S(1)} %copy.76.have_ref, ...), custom_call_target="tpu_custom_call" | custom-call | tf_op jit(solution)/shard_map/finish/pallas_call | solution.py:284
  (66 shorter events, 4.2 us)
Async XLA Ops:
  0.0 19.5 %copy-start.2 = (s32[40]{0:T(128)S(1)}, s32[40]{0:T(128)}, u32[]{:S(2)}) copy-start(s32[40]{0:T(128)} %occ_ref.1) | copy-start | bytes 484
  0.0 19.4 %copy-start.3 = (s32[500]{0:T(512)S(1)}, s32[500]{0:T(512)}, u32[]{:S(2)}) copy-start(s32[500]{0:T(512)} %param.13) | copy-start | bytes 6004
  7.1 40.4 %all-to-all-start.2 = ((f32[64,4,640]{2,1,0:T(4,128)}), f32[64,4,640]{2,1,0:T(4,128)}, u32[]{:S(2)}, u32[]{:S(2)}) async-start(f32[64,4,640]{2,1,0:T(4,128)} %pack_amplitudes.1), calls=%async_computation.2 | async-start | bytes 1310720 | tf_op jit(solution)/shard_map/all_to_all | solution.py:297
  22.6 4.9 %copy-start.5 = (f32[500]{0:T(512)S(1)}, f32[500]{0:T(512)}, u32[]{:S(2)}) copy-start(f32[500]{0:T(512)} %param.15) | copy-start | bytes 6004
  28.5 0.7 copy-start.4
  28.5 0.7 %copy-start.6 = (s32[25]{0:T(128)S(1)}, s32[25]{0:T(128)}, u32[]{:S(2)}) copy-start(s32[25]{0:T(128)} %constant.79.clone) | copy-start | bytes 304
  28.6 0.7 %copy-start.7 = (s32[25]{0:T(128)S(1)}, s32[25]{0:T(128)}, u32[]{:S(2)}) copy-start(s32[25]{0:T(128)} %constant.80.clone) | copy-start | bytes 304
  47.5 1.3 %copy-start = (s32[9,256,128]{2,1,0:T(8,128)S(1)}, s32[9,256,128]{2,1,0:T(8,128)}, u32[]{:S(2)}) copy-start(s32[9,256,128]{2,1,0:T(8,128)} %select_select_fusion.slot_ref) | copy-start | bytes 3538948
  58.6 4.6 %collective-permute-start = (f32[2,40,160]{2,1,0:T(8,128)S(1)}, f32[2,40,160]{2,1,0:T(8,128)S(1)}, u32[]{:S(2)}, u32[]{:S(2)}) collective-permute-start(f32[2,40,160]{2,1,0:T(8,128)S(1)} %slice.66), channel_id=1, source_target_pairs={{0,64},{64,0},{128,192},{192,128},{1,65},{65,1},{129,193},{193,129... | collective-permute-start | bytes 153608 | tf_op jit(solution)/shard_map/ppermute | solution.py:355
  63.2 5.5 %collective-permute-start.1 = (f32[40,160]{1,0:T(8,128)S(1)}, f32[40,160]{1,0:T(8,128)S(1)}, u32[]{:S(2)}, u32[]{:S(2)}) collective-permute-start(f32[40,160]{1,0:T(8,128)S(1)} %get-tuple-element.64), channel_id=1, source_target_pairs={{0,192},{64,128},{128,64},{192,0},{1,193},{65,129},{129,65},{193,1... | collective-permute-start | bytes 76808 | tf_op jit(solution)/shard_map/ppermute | solution.py:357

commit v5 on v4

--- a/solution.py
+++ b/solution.py
@@ -185,32 +185,92 @@
     )(place, need, have, turned_weight)
 
 
+def amounts(kinds, counts_ref, g):
+    found = jnp.zeros(kinds.shape, I32)
+    for label in range(8):
+        found = jnp.where(kinds == label, counts_ref[g, label], found)
+    return found.astype(F32).astype(BF16)
+
+
+def table_kernel(counts_ref, mine_ref, all_ref, c_ref, from_ref, to_ref, slot_ref, valid_ref, fits_ref):
+    g = lax.axis_index("grp")
+    mine = mine_ref[...]
+    held = amounts(mine, counts_ref, g)
+    pair = iota((T, CP), 0)
+    at = iota((T, CP), 1) // FOLD
+    rank = iota((M * BL, CP), 1) % FOLD
+    real = iota((M * BL, CP), 1) < GT * FOLD
+    for group in range(NG):
+        start = dot(held, (pair < GT * group + at).astype(F32).astype(BF16)).astype(I32)
+        amount = dot(held, (pair == GT * group + at).astype(F32).astype(BF16)).astype(I32)
+        slot_ref[group] = jnp.where(real & (rank < amount), start + rank, -1)
+    label = mine.astype(F32).astype(BF16)
+    for t in range(T):
+        wide = dot(label, (pair == t).astype(F32).astype(BF16)).astype(I32)
+        valid_ref[t] = (wide == c_ref[...]).astype(F32)
+    good = jnp.ones((8 * M, T), F32)
+    earlier = (iota((T, T), 0) < iota((T, T), 1)).astype(F32).astype(BF16)
+    most = counts_ref[0, 0]
+    for other in range(G):
+        for label in range(8):
+            most = jnp.maximum(most, counts_ref[other, label])
+    for other in range(G):
+        start = dot(amounts(all_ref[...], counts_ref, other), earlier).astype(I32)
+        good = jnp.where((start >= from_ref[...]) & (start + most <= to_ref[...]), good, 0.0)
+    fits = jnp.min(good, axis=(0, 1), keepdims=True)
+    fits = jnp.where(most <= FOLD, fits, 0.0)
+    fits_ref[...] = jnp.broadcast_to(fits, (8, CP))
+
+
+def tables(counts, mine, every, own_c, low, high):
+    vmem = pl.BlockSpec(memory_space=pltpu.VMEM)
+    return pl.pallas_call(
+        table_kernel,
+        name="tables",
+        out_shape=(
+            pltpu.HBM((NG, M * BL, CP), I32),
+            jax.ShapeDtypeStruct((T, M * BL, CP), F32),
+            jax.ShapeDtypeStruct((8, CP), F32),
+        ),
+        in_specs=[pl.BlockSpec(memory_space=pltpu.SMEM)] + [vmem] * 5,
+        compiler_params=pltpu.CompilerParams(vmem_limit_bytes=8 << 20),
+    )(counts, mine, every, own_c, low, high)
+
+
 def contract_kernel(
-    x_ref, slot_ref, valid_ref, rank_ref, far_high_ref, far_low_ref, out_ref, seen_ref, spread_ref, wide_ref, high_ref, low_ref, sem
+    far_x_ref, far_slot_ref, valid_ref, rank_ref, far_high_ref, far_low_ref, out_ref,
+    x_ref, slot_ref, seen_ref, spread_ref, wide_ref, high_ref, low_ref, sem,
 ):
     g = lax.axis_index("grp")
+    first_copies = [
+        pltpu.make_async_copy(far_x_ref, x_ref, sem.at[2]),
+        pltpu.make_async_copy(far_slot_ref, slot_ref, sem.at[3]),
+    ]
     copies = [
         pltpu.make_async_copy(far_high_ref, high_ref, sem.at[0]),
         pltpu.make_async_copy(far_low_ref, low_ref, sem.at[1]),
     ]
-    for copy in copies:
+    for copy in first_copies + copies:
         copy.start()
-
-    @pl.loop(0, M // 2)
+    for copy in first_copies:
+        copy.wait()
+
+    @pl.loop(0, M // 8)
     def _(i):
-        packed = x_ref[pl.ds(2 * i, 2)].reshape(2 * BL, SLOTS)
-        rows = pl.ds(pl.multiple_of(8 * i, 8), 8)
-        for group, (first, last) in enumerate(GROUP_BLOCKS):
-            slot = slot_ref[group, rows, :]
-            lane = jnp.bitwise_and(slot, CP - 1)
-            where = jnp.right_shift(slot, 7)
-            found = jnp.zeros((8, CP), F32)
-            for part in range(first, last):
-                taken = jnp.take_along_axis(
-                    packed[:, part * CP : (part + 1) * CP], lane, axis=1, mode="promise_in_bounds"
-                )
-                found = jnp.where(where == part, taken, found)
-            seen_ref[group, rows, :] = found
+        for near in range(4):
+            packed = x_ref[pl.ds(8 * i + 2 * near, 2)].reshape(2 * BL, SLOTS)
+            rows = pl.ds(pl.multiple_of(32 * i, 8) + 8 * near, 8)
+            for group, (first, last) in enumerate(GROUP_BLOCKS):
+                slot = slot_ref[group, rows, :]
+                lane = jnp.bitwise_and(slot, CP - 1)
+                where = jnp.right_shift(slot, 7)
+                found = jnp.zeros((8, CP), F32)
+                for part in range(first, last):
+                    taken = jnp.take_along_axis(
+                        packed[:, part * CP : (part + 1) * CP], lane, axis=1, mode="promise_in_bounds"
+                    )
+                    found = jnp.where(where == part, taken, found)
+                seen_ref[group, rows, :] = found
 
     place = [(iota((CP, CP), 0) - at * FOLD == rank_ref[...]).astype(F32).astype(BF16) for at in range(GT)]
     place = jnp.concatenate(place, axis=1)
@@ -242,7 +302,8 @@
         a_high, a_low = halves(amp)
         w_high = high_ref[2 * i : 2 * i + 2].reshape(2 * CP, NF)
         w_low = low_ref[2 * i : 2 * i + 2].reshape(2 * CP, NF)
-        total = total + (dot(a_high, w_high) + dot(a_high, w_low) + dot(a_low, w_high))
+        both = dot(jnp.concatenate([a_high, a_low], axis=0), w_high)
+        total = total + (both[0:J4] + both[J4 : 2 * J4] + dot(a_high, w_low))
 
     turned = jnp.transpose(total)
     for block in range(G):
@@ -251,21 +312,24 @@
 
 def contract(received, slots, valid, rank, high, low):
     vmem = pl.BlockSpec(memory_space=pltpu.VMEM)
+    hbm = pl.BlockSpec(memory_space=pltpu.HBM)
     return pl.pallas_call(
         contract_kernel,
         name="contract",
         out_shape=jax.ShapeDtypeStruct((G, FOLD, J4), F32),
-        in_specs=[vmem] * 4 + [pl.BlockSpec(memory_space=pltpu.HBM)] * 2,
+        in_specs=[hbm, hbm, vmem, vmem, hbm, hbm],
         scratch_shapes=[
+            pltpu.VMEM((M, BL, SLOTS), F32),
+            pltpu.VMEM((NG, M * BL, CP), I32),
             pltpu.VMEM((NG, M * BL, CP), F32),
             pltpu.VMEM((NG, M * BL, GT * CP), F32),
             pltpu.VMEM((O * O * BL, CP), F32),
             pltpu.VMEM((O, CP, NF), BF16),
             pltpu.VMEM((O, CP, NF), BF16),
-            pltpu.SemaphoreType.DMA((2,)),
+            pltpu.SemaphoreType.DMA((4,)),
         ],
-        compiler_params=pltpu.CompilerParams(vmem_limit_bytes=16 << 20),
-    )(received, slots, valid, rank, in_hbm(high), in_hbm(low))
+        compiler_params=pltpu.CompilerParams(vmem_limit_bytes=20 << 20),
+    )(in_hbm(received), in_hbm(slots), valid, rank, in_hbm(high), in_hbm(low))
 
 
 def finish_kernel(a_ref, b_ref, rank_ref, need_ref, have_ref, row_ref, column_ref, out_ref):
@@ -303,38 +367,16 @@
     counts = jnp.sum(shares[:, :, None] == labels, axis=1).astype(I32)
     own = lax.dynamic_index_in_dim(shares, g, 0, keepdims=False)
     own_rank = lax.dynamic_index_in_dim(ranks, g, 0, keepdims=False)
-    own_count = lax.dynamic_index_in_dim(counts, g, 0, keepdims=False)
     own_c = jnp.concatenate([own, jnp.full((CP - CL,), NONE, I32)])
     rank_c = jnp.concatenate([own_rank, jnp.zeros((CP - CL,), I32)])
 
-    pairs = jnp.bitwise_xor(occ_irrep[:, None], occ_irrep[None, :]).reshape(M, T)
-    kinds = (pairs[:, :, None] == labels).astype(I32)
-    passed = jnp.cumsum(kinds, axis=1) - kinds
-    crossed = jnp.bitwise_xor(labels[:, None], labels[None, :])
+    pairs = jnp.bitwise_xor(occ_irrep[:, None], occ_irrep[None, :]).reshape(M, 1, T)
     own_b = lax.dynamic_slice_in_dim(vir_irrep, m * BL, BL)
-    per_b = jnp.sum(jnp.where(jnp.bitwise_xor(labels[:, None], own_b)[:, :, None] == labels, own_count, 0), axis=2)
-    start = jnp.sum(passed[:, :, None, :] * per_b.T, axis=3)
-    amount = jnp.sum(kinds[:, :, None, :] * per_b.T, axis=3)
-
-    def by_group(x):
-        x = jnp.pad(jnp.transpose(x, (1, 0, 2)), ((0, NG * GT - T), (0, 0), (0, 0)))
-        return x.reshape(NG, GT, M * BL, 1)
-
-    start, amount = by_group(start), by_group(amount)
-    lanes = jnp.arange(CP, dtype=I32)
-    slots = jnp.full((NG, M * BL, CP), -1, I32)
-    for at in range(GT):
-        rank = lanes - at * FOLD
-        slots = jnp.where((rank >= 0) & (rank < jnp.minimum(amount[:, at], FOLD)), start[:, at] + rank, slots)
-    reach = jnp.bitwise_xor(pairs.T[:, :, None], own_c)
-    valid = (reach[:, :, None, :] == own_b[:, None]).astype(F32).reshape(T, M * BL, CP)
-
-    all_kinds = jnp.sum(jnp.where(crossed[:, :, None] == labels, counts[:, None, None, :], 0), axis=3)
-    before = jnp.sum(passed[None, :, :, :, None] * all_kinds[:, None, None], axis=3)
-    least = jnp.min(before, axis=(0, 1, 3))
-    most = jnp.max(before, axis=(0, 1, 3)) + jnp.max(counts)
-    inside = (least >= jnp.array(SLOT_FROM)) & (most <= jnp.array(SLOT_TO))
-    fits = jnp.all(inside) & (jnp.max(counts) <= FOLD)
+    mine = jnp.bitwise_xor(pairs, own_b[:, None]).reshape(M * BL, T)
+    every = jnp.bitwise_xor(pairs, labels[:, None]).reshape(M * 8, T)
+    low, high = (jnp.array(x, I32).reshape(1, T) for x in (SLOT_FROM, SLOT_TO))
+    slots, valid, fits = tables(counts, mine, every, own_c.reshape(1, CP), low, high)
+    fits = fits[0, 0] > 0.5
 
     place = (jnp.minimum(ranks, FOLD) + jnp.where(ranks < FOLD, jnp.arange(G, dtype=I32)[:, None] * FOLD, V)).reshape(1, V)
     need = jnp.bitwise_xor(vir_irrep, occ_irrep[0]).reshape(1, V)

time: 70.8 us -> 68.9 us (0.973)
  other arithmetic: 10.9 us -> 7.55 us
  local copies, waits for them, and re-layouts: 5.92 us -> 7.41 us
    select_n x1 -> x0, other arithmetic: 3.6 us -> none  [packed_form(): jnp.where((rank >= 0) & (rank < jnp.minimum(amount[:, at], FOLD)), start[...]
    pallas_call x0 -> x1, Pallas kernels: none -> 3.3 us  [tables(): pl.pallas_call(table_kernel, name='tables', out_shape=(pltpu.HBM((NG, M *...]
    pallas_call x1, Pallas kernels: 9.85 us -> 7.14 us  [contract(): pl.pallas_call(contract_kernel, name='contract', out_shape=jax.ShapeDtype...]
    reduce_sum x4 -> x0, other arithmetic: 1.68 us -> none  [the longest x1 0.62 us: packed_form(): jnp.sum(jnp.where(crossed[:, :, None] == labels, counts[:, None, None, :]...]
    reduce_max x2 -> x0, other arithmetic: 1.62 us -> none  [packed_form(): most = jnp.max(before, axis=(0, 1, 3)) + jnp.max(counts)]
    reduce_and x1 -> x0, other arithmetic: 1.36 us -> none  [packed_form(): fits = jnp.all(inside) & (jnp.max(counts) <= FOLD)]
    reshape x1, other arithmetic: 0.11 us -> 1.4 us  [packed_form(): (occ_energy[0] - lax.dynamic_slice_in_dim(vir_energy, g * CL, CL)).reshap...]
    xor x1, other arithmetic: 0.04 us -> 1.33 us  [packed_form(): need = jnp.bitwise_xor(vir_irrep, occ_irrep[0]).reshape(1, V)]
  transfers between devices with their start and end apart: 3 -> 3, of which waited for: 2 -> 2; matrix products, arithmetic and copies ran while one was open for 22% -> 20% of each run, Pallas kernels for 16% -> 21%
where the time goes in v5:
time: 68.9 us; the launch traced here: 68.1 us
  Pallas kernels  29.9 us (43%)
  starting transfers between devices  16.7 us (24%)
  other arithmetic  7.55 us (11%)
  local copies, waits for them, and re-layouts  7.41 us (11%)
  waiting for transfers between devices  5.22 us (8%)
  between operations  1.08 us (2%)
    all_to_all x1, starting transfers between devices, packed_form(): received = lax.all_to_all(sent, 'blk', 0, 0, tiled=True)  12.3 us
    pallas_call x1, Pallas kernels, fold(): pl.pallas_call(fold_kernel, name='fold_weights', grid=(CP // CS,), out_sh...  11.2 us
    pallas_call x1, Pallas kernels, contract(): pl.pallas_call(contract_kernel, name='contract', out_shape=jax.ShapeDtype...  7.14 us
    pallas_call x1, Pallas kernels, pack(): pl.pallas_call(pack_kernel, name='pack_amplitudes', grid=(T // TS,), out_...  7.12 us
    pallas_call x1, Pallas kernels, tables(): pl.pallas_call(table_kernel, name='tables', out_shape=(pltpu.HBM((NG, M *...  3.3 us
    ppermute x1, waiting for transfers between devices, packed_form(): near = lax.ppermute(partial[1:3], 'grp', [(d, d ^ 1) for d in range(G)])  3 us
    ppermute x1, starting transfers between devices, packed_form(): lax.ppermute(partial[3] + near[1], 'grp', [(d, d ^ 3) for d in range(G)])  2.85 us
    ppermute x1, waiting for transfers between devices, packed_form(): lax.ppermute(partial[3] + near[1], 'grp', [(d, d ^ 3) for d in range(G)])  2.22 us
  transfers between devices with their start and end apart: 3, of which 2 were waited for; matrix products, arithmetic and copies ran while one was open for 20% of the time, Pallas kernels for 21%

profile of v5, /device:TPU:8, one launch (start us, length us, event | category | flops | bytes accessed | tf_op | source)
XLA Modules:
  0.0 68.1 jit_solution(10947580469755381379)
XLA Ops:
  0.0 7.1 %pack_amplitudes.1 = f32[64,4,640]{2,1,0:T(4,128)} custom-call(s32[40]{0:T(128)} %occ_ref.1, s32[1,500]{1,0:T(1,128)} %bitcast.59, f32[25,125,256]{2,1,0:T(8,128)} %amp_ref.1), custom_call_target="tpu_custom_call" | custom-call | tf_op jit(solution)/shard_map/pack_amplitudes/pallas_call | solution.py:105
  7.2 12.3 %all-to-all-start.2 = ((f32[64,4,640]{2,1,0:T(4,128)}), f32[64,4,640]{2,1,0:T(4,128)}, u32[]{:S(2)}, u32[]{:S(2)}) async-start(f32[64,4,640]{2,1,0:T(4,128)} %pack_amplitudes.1), calls=%async_computation.2 | async-start | bytes 1310720 | tf_op jit(solution)/shard_map/all_to_all | solution.py:361
  20.0 0.7 broadcast_xor_fusion.8
  20.9 0.8 %dynamic_slice.32 = f32[4]{0:T(128)S(1)} dynamic-slice(f32[500]{0:T(512)} %param.15, s32[]{:T(128)S(6)} %select_n.40), dynamic_slice_sizes={4} | dynamic-slice | bytes 36 | tf_op jit(solution)/shard_map/dynamic_slice | solution.py:387
  21.9 0.8 %broadcast_xor_fusion.4.mine_ref = s32[256,25]{1,0:T(8,128)} fusion(s32[256,25]{1,0:T(8,128)S(1)} %bitcast.54, s32[256]{0:T(256)S(1)} %xor.183), kind=kLoop, calls=%fused_computation.16 | loop fusion | flops 6400 | bytes 52224 | tf_op jit(solution)/shard_map/xor | solution.py:375
  22.7 0.8 %convert_reduce_fusion = s32[4,125]{1,0:T(4,128)} fusion(s32[4,125]{1,0:T(4,128)S(1)} %eq.26, s32[4,125]{0,1:T(8,128)S(1)} %copy.50, pred[125,125]{1,0:T(8,128)(4,1)S(1)} %iota_compare_fusion), kind=kLoop, calls=%fused_computation.14 | loop fusion | flops 249500 | bytes 21625 | tf_op jit(solution)/shard_map/reduce_sum | solution.py:366
  23.5 0.7 broadcast_subtract_fusion.1
  24.7 0.9 %copy-done = s32[256,25]{1,0:T(8,128)S(1)} copy-done((s32[256,25]{1,0:T(8,128)S(1)}, s32[256,25]{1,0:T(8,128)}, u32[]{:S(2)}) %copy-start) | copy-done | bytes 25624
  26.2 3.3 %tables.1 = (s32[9,256,128]{2,1,0:T(8,128)}, f32[25,256,128]{2,1,0:T(8,128)S(1)}, f32[8,128]{1,0:T(8,128)S(1)}) custom-call(s32[4,8]{1,0:T(4,128)S(1)} %convert_reduce_fusion.1.counts_ref, s32[256,25]{1,0:T(8,128)S(1)} %copy-done, s32[512,25]{1,0:T(8,128)S(1)} %bitcast_xor_fusion.all_ref, s32[1,128]{1,0:T(1,128)S(1)} %copy-done.3, s32[1,25]{1,0:T(1,128)S(1)} %copy-done.1, ...), custom_call_target="tpu_custom_call" | custom-call | tf_op jit(solution)/shard_map/tables/pallas_call | solution.py:227
  30.1 0.7 %xor.197 = s32[160,1]{0,1:T(1,128)S(1)} reshape(s32[4,40]{1,0:T(4,128)} %broadcast_xor_fusion.8) | data formatting | bytes 1280 | tf_op jit(solution)/shard_map/xor | solution.py:390
  30.9 0.8 %sub.60 = f32[160,1]{0,1:T(1,128)S(1)} reshape(f32[4,40]{1,0:T(4,128)} %broadcast_subtract_fusion.1) | data formatting | bytes 1280 | tf_op jit(solution)/shard_map/sub | solution.py:388
  32.3 0.7 %constant_dynamic-slice_fusion.rank_ref = s32[1,125]{1,0:T(1,128)S(1)} fusion(s32[4,125]{1,0:T(4,128)} %convert_reduce_fusion, s32[]{:T(128)S(6)} %select_n.41), kind=kLoop, calls=%fused_computation.32 | loop fusion | bytes 1004 | tf_op jit(solution)/shard_map/jit(dynamic_index_in_dim)/dynamic_slice | solution.py:369
  33.0 1.4 %subtract_bitcast_fusion.row_ref = f32[1,125]{1,0:T(1,128)S(1)} fusion(f32[500]{0:T(512)} %param.15, s32[]{:T(128)S(6)} %select_n.42, f32[]{:T(128)} %bitcast.60), kind=kLoop, calls=%fused_computation.31 | loop fusion | flops 125 | bytes 1008 | tf_op jit(solution)/shard_map/reshape | solution.py:386
  34.4 0.8 %broadcast_xor_fusion.5 = s32[128,40]{1,0:T(8,128)S(1)} fusion(s32[40]{0:T(128)} %occ_ref.1, s32[128]{0:T(128)} %get-tuple-element.70), kind=kLoop, calls=%fused_computation.21 | loop fusion | flops 5120 | bytes 21152 | tf_op jit(solution)/shard_map/xor | solution.py:383
  35.3 0.8 %select_add_fusion = s32[4,125]{1,0:T(4,128)S(1)} fusion(s32[4,125]{1,0:T(4,128)} %convert_reduce_fusion, s32[4]{0:T(128)S(1)} %iota_multiply_fusion), kind=kLoop, calls=%fused_computation.25 | loop fusion | flops 2000 | bytes 4016 | tf_op jit(solution)/shard_map/add | solution.py:381
  36.2 1.3 %broadcast_xor_fusion.7 = s32[500]{0:T(512)S(1)} fusion(s32[500]{0:T(512)} %param.13, s32[]{:T(128)} %bitcast.56), kind=kLoop, calls=%fused_computation.26 | loop fusion | flops 500 | bytes 4004 | tf_op jit(solution)/shard_map/xor | solution.py:382
  37.5 11.2 %fold_weights.1 = (bf16[40,128,160]{2,1,0:T(8,128)(2,1)}, bf16[40,128,160]{2,1,0:T(8,128)(2,1)}) custom-call(s32[1,500]{1,0:T(1,128)S(1)} %add.65.place_ref, s32[1,500]{1,0:T(1,128)S(1)} %bitcast.48, s32[1,5120]{1,0:T(1,128)S(1)} %xor.203.have_ref, f32[5000,500]{1,0:T(8,128)} %bitcast.49), custom_call_target="tpu_custom_call" | custom-call | tf_op jit(solution)/shard_map/fold_weights/pallas_call | solution.py:170
  48.7 0.7 %fusion.12 = s32[125]{0:T(128)S(1)} fusion(s32[4,125]{1,0:T(4,128)} %convert_reduce_fusion, s32[]{:T(128)S(6)} %select_n.41), kind=kLoop, calls=%fused_computation.38 | loop fusion | bytes 1004 | tf_op jit(solution)/shard_map/jit(dynamic_index_in_dim)/squeeze | solution.py:369
  49.4 7.1 %contract.1 = f32[4,40,160]{2,1,0:T(8,128)S(1)} custom-call(f32[64,4,640]{2,1,0:T(4,128)} %all-to-all-done.2.far_x_ref, s32[9,256,128]{2,1,0:T(8,128)} %get-tuple-element.44.far_slot_ref, f32[25,256,128]{2,1,0:T(8,128)S(1)} %get-tuple-element.45.valid_ref, s32[1,128]{1,0:T(1,128)S(1)} %pad_bitcast_fusion.rank_ref, ...), custom_call_target="tpu_custom_call" | custom-call | tf_op jit(solution)/shard_map/contract/pallas_call | solution.py:316
  56.6 1.6 %collective-permute-start = (f32[2,40,160]{2,1,0:T(8,128)S(1)}, f32[2,40,160]{2,1,0:T(8,128)S(1)}, u32[]{:S(2)}, u32[]{:S(2)}) collective-permute-start(f32[2,40,160]{2,1,0:T(8,128)S(1)} %slice.40), channel_id=1, source_target_pairs={{0,64},{64,0},{128,192},{192,128},{1,65},{65,1},{129,193},{193,129... | collective-permute-start | bytes 153608 | tf_op jit(solution)/shard_map/ppermute | solution.py:397
  58.2 3.0 %collective-permute-done = f32[2,40,160]{2,1,0:T(8,128)S(1)} collective-permute-done((f32[2,40,160]{2,1,0:T(8,128)S(1)}, f32[2,40,160]{2,1,0:T(8,128)S(1)}, u32[]{:S(2)}, u32[]{:S(2)}) %collective-permute-start) | collective-permute-done | bytes 51232 | tf_op jit(solution)/shard_map/ppermute | solution.py:397
  61.2 2.8 %collective-permute-start.1 = (f32[40,160]{1,0:T(8,128)S(1)}, f32[40,160]{1,0:T(8,128)S(1)}, u32[]{:S(2)}, u32[]{:S(2)}) collective-permute-start(f32[40,160]{1,0:T(8,128)S(1)} %get-tuple-element.66), channel_id=1, source_target_pairs={{0,192},{64,128},{128,64},{192,0},{1,193},{65,129},{129,65},{193,1... | collective-permute-start | bytes 76808 | tf_op jit(solution)/shard_map/ppermute | solution.py:399
  64.3 2.2 %collective-permute-done.1.b_ref = f32[40,160]{1,0:T(8,128)S(1)} collective-permute-done((f32[40,160]{1,0:T(8,128)S(1)}, f32[40,160]{1,0:T(8,128)S(1)}, u32[]{:S(2)}, u32[]{:S(2)}) %collective-permute-start.1) | collective-permute-done | bytes 25632 | tf_op jit(solution)/shard_map/ppermute | solution.py:399
  66.5 1.2 %finish.1 = f32[160,125]{1,0:T(8,128)} custom-call(f32[40,160]{1,0:T(8,128)S(1)} %get-tuple-element.67.a_ref, f32[40,160]{1,0:T(8,128)S(1)} %collective-permute-done.1.b_ref, s32[1,125]{1,0:T(1,128)S(1)} %constant_dynamic-slice_fusion.rank_ref, s32[1,125]{1,0:T(1,128)S(1)} %get-tuple-element.49.need_ref, s32[160,1]{1,0:T(8,128)S(1)} %copy.51.have_ref, ...), custom_call_target="tpu_custom_call" | custom-call | tf_op jit(solution)/shard_map/finish/pallas_call | solution.py:348
  (47 shorter events, 3.5 us)
Async XLA Ops:
  0.0 24.7 %copy-start.1 = (s32[1,25]{1,0:T(1,128)S(1)}, s32[1,25]{1,0:T(1,128)}, u32[]{:S(2)}) copy-start(s32[1,25]{1,0:T(1,128)} %constant.64.from_ref) | copy-start | bytes 304
  0.0 24.7 %copy-start.2 = (s32[1,25]{1,0:T(1,128)S(1)}, s32[1,25]{1,0:T(1,128)}, u32[]{:S(2)}) copy-start(s32[1,25]{1,0:T(1,128)} %constant.65.to_ref) | copy-start | bytes 304
  0.0 19.5 %copy-start.5 = (s32[40]{0:T(128)S(1)}, s32[40]{0:T(128)}, u32[]{:S(2)}) copy-start(s32[40]{0:T(128)} %occ_ref.1) | copy-start | bytes 484
  0.0 19.4 %copy-start.7 = (s32[500]{0:T(512)S(1)}, s32[500]{0:T(512)}, u32[]{:S(2)}) copy-start(s32[500]{0:T(512)} %param.13) | copy-start | bytes 6004
  0.0 23.4 %copy-start.9 = (f32[40]{0:T(128)S(1)}, f32[40]{0:T(128)}, u32[]{:S(2)}) copy-start(f32[40]{0:T(128)} %param.14) | copy-start | bytes 484
  7.2 42.2 %all-to-all-start.2 = ((f32[64,4,640]{2,1,0:T(4,128)}), f32[64,4,640]{2,1,0:T(4,128)}, u32[]{:S(2)}, u32[]{:S(2)}) async-start(f32[64,4,640]{2,1,0:T(4,128)} %pack_amplitudes.1), calls=%async_computation.2 | async-start | bytes 1310720 | tf_op jit(solution)/shard_map/all_to_all | solution.py:361
  24.7 0.9 %copy-start = (s32[256,25]{1,0:T(8,128)S(1)}, s32[256,25]{1,0:T(8,128)}, u32[]{:S(2)}) copy-start(s32[256,25]{1,0:T(8,128)} %broadcast_xor_fusion.4.mine_ref) | copy-start | bytes 76804
  25.6 0.6 copy-start.3
  49.4 18.3 %copy-start.6 = (s32[40]{0:T(128)S(1)}, s32[40]{0:T(128)}, u32[]{:S(2)}) copy-start(s32[40]{0:T(128)} %occ_ref.1) | copy-start | bytes 484
  49.4 18.3 %copy-start.8 = (s32[500]{0:T(512)S(1)}, s32[500]{0:T(512)}, u32[]{:S(2)}) copy-start(s32[500]{0:T(512)} %param.13) | copy-start | bytes 6004
  49.4 18.3 %copy-start.10 = (f32[40]{0:T(128)S(1)}, f32[40]{0:T(128)}, u32[]{:S(2)}) copy-start(f32[40]{0:T(128)} %param.14) | copy-start | bytes 484
  49.4 18.3 %copy-start.11 = (f32[500]{0:T(512)S(1)}, f32[500]{0:T(512)}, u32[]{:S(2)}) copy-start(f32[500]{0:T(512)} %param.15) | copy-start | bytes 6004
  56.6 4.6 %collective-permute-start = (f32[2,40,160]{2,1,0:T(8,128)S(1)}, f32[2,40,160]{2,1,0:T(8,128)S(1)}, u32[]{:S(2)}, u32[]{:S(2)}) collective-permute-start(f32[2,40,160]{2,1,0:T(8,128)S(1)} %slice.40), channel_id=1, source_target_pairs={{0,64},{64,0},{128,192},{192,128},{1,65},{65,1},{129,193},{193,129... | collective-permute-start | bytes 153608 | tf_op jit(solution)/shard_map/ppermute | solution.py:397
  61.2 5.3 %collective-permute-start.1 = (f32[40,160]{1,0:T(8,128)S(1)}, f32[40,160]{1,0:T(8,128)S(1)}, u32[]{:S(2)}, u32[]{:S(2)}) collective-permute-start(f32[40,160]{1,0:T(8,128)S(1)} %get-tuple-element.66), channel_id=1, source_target_pairs={{0,192},{64,128},{128,64},{192,0},{1,193},{65,129},{129,65},{193,1... | collective-permute-start | bytes 76808 | tf_op jit(solution)/shard_map/ppermute | solution.py:399

commit v6 on v5

--- a/solution.py
+++ b/solution.py
@@ -45,6 +45,34 @@
 
 def in_hbm(x):
     return pltpu.with_memory_space_constraint(x, pltpu.HBM)
+
+
+def share_of(ref, share):
+    first = share * CL
+    over = first - (V - CP)
+    if over <= 0:
+        return ref[:, first : first + CP]
+    return pltpu.roll(ref[:, V - CP : V], CP - over, 1)
+
+
+def own_share(ref, g):
+    row = share_of(ref, 0)
+    for share in range(1, G):
+        row = jnp.where(g == share, share_of(ref, share), row)
+    return row
+
+
+def labels_of(row):
+    return jnp.where(iota((1, CP), 1) < CL, row, NONE)
+
+
+def same_before(row):
+    wide = jnp.broadcast_to(row, (CP, CP))
+    return ((wide == jnp.transpose(wide)) & (iota((CP, CP), 0) < iota((CP, CP), 1))).astype(F32)
+
+
+def one_hot(x):
+    return x.astype(F32).astype(BF16)
 
 
 def iota(shape, dim):
@@ -130,29 +158,31 @@
 CS = 16
 
 
-def fold_kernel(place_ref, need_ref, have_ref, w_ref, high_ref, low_ref, pick_ref, turn_ref, rest_ref, first_ref, second_ref):
+def fold_kernel(
+    occ_ref, vir_ref, have_ref, w_ref, high_ref, low_ref, lay_ref, pick_ref, turn_ref, rest_ref, first_ref, second_ref
+):
     step = pl.program_id(0)
 
     @pl.when(step == 0)
     def _():
-        for first in range(0, V, CP):
-            lanes = slice(first, min(first + CP, V))
-            place = jnp.transpose(jnp.broadcast_to(place_ref[:, lanes], (CP, min(CP, V - first))))
-            for at in range(0, NF, CP):
-                wide = min(CP, NF - at)
-                hit = iota((min(CP, V - first), wide), 1) + at == place[:, 0:wide]
-                pick_ref[lanes, at : at + wide] = hit.astype(F32).astype(BF16)
-
+        for share in range(G):
+            before = jnp.transpose(same_before(labels_of(share_of(vir_ref, share))))
+            rank = jnp.sum(before, axis=1, keepdims=True).astype(I32)
+            hit = (iota((CP, NF), 1) == rank + share * FOLD) & (rank < FOLD)
+            lay_ref[share * CL : share * CL + CP, :] = hit.astype(F32)
+        pick_ref[...] = lay_ref[...].astype(BF16)
+
+    need = jnp.bitwise_xor(vir_ref[...], occ_ref[0])
     for part in range(CS * O // CP):
         rows = slice(part * CP, (part + 1) * CP)
         have = jnp.transpose(jnp.broadcast_to(have_ref[:, rows], (CP, CP)))
         for first in range(0, V, CP):
             lanes = slice(first, min(first + CP, V))
-            kept = jnp.where(need_ref[:, lanes] == have[:, : min(CP, V - first)], w_ref[rows, lanes], 0.0)
+            kept = jnp.where(need[:, lanes] == have[:, : min(CP, V - first)], w_ref[rows, lanes], 0.0)
             high, low = halves(kept)
             first_ref[rows, lanes] = high
             second_ref[rows, lanes] = low
-    folded = dot(first_ref[...], pick_ref[...]) + dot(second_ref[...], pick_ref[...])
+    folded = dot(first_ref[...], pick_ref[0:V]) + dot(second_ref[...], pick_ref[0:V])
     turn_ref[...] = folded[:, 0:CP]
     rest_ref[:, 0 : NF - CP] = folded[:, CP:NF]
     for k in range(O):
@@ -163,7 +193,7 @@
         low_ref[k] = low
 
 
-def fold(place, need, have, turned_weight):
+def fold(occ_irrep, vir_row, have, turned_weight):
     rows = CS * O
     out = pltpu.HBM((O, CP, NF), BF16)
     spec = pl.BlockSpec((O, CS, NF), lambda s: (0, s, 0))
@@ -173,57 +203,104 @@
         grid=(CP // CS,),
         out_shape=(out, out),
         in_specs=[
-            pl.BlockSpec((1, V), lambda s: (0, 0)),
+            pl.BlockSpec(memory_space=pltpu.SMEM),
             pl.BlockSpec((1, V), lambda s: (0, 0)),
             pl.BlockSpec((1, rows), lambda s: (0, s)),
             pl.BlockSpec((rows, V), lambda s: (s, 0)),
         ],
         out_specs=(spec, spec),
-        scratch_shapes=[pltpu.VMEM((V, NF), BF16), pltpu.VMEM((rows, CP), F32), pltpu.VMEM((rows, CP), F32)]
+        scratch_shapes=[pltpu.VMEM((G * CP, NF), F32), pltpu.VMEM((G * CP, NF), BF16), pltpu.VMEM((rows, CP), F32), pltpu.VMEM((rows, CP), F32)]
         + [pltpu.VMEM((rows, V), BF16)] * 2,
         compiler_params=pltpu.CompilerParams(vmem_limit_bytes=8 << 20),
-    )(place, need, have, turned_weight)
-
-
-def amounts(kinds, counts_ref, g):
+    )(occ_irrep, vir_row, have, turned_weight)
+
+
+def amounts(kinds, counts):
     found = jnp.zeros(kinds.shape, I32)
     for label in range(8):
-        found = jnp.where(kinds == label, counts_ref[g, label], found)
-    return found.astype(F32).astype(BF16)
-
-
-def table_kernel(counts_ref, mine_ref, all_ref, c_ref, from_ref, to_ref, slot_ref, valid_ref, fits_ref):
+        found = jnp.where(kinds == label, counts[label], found)
+    return one_hot(found)
+
+
+def table_kernel(
+    occ_ref, vir_ref, occ_energy_ref, vir_energy_ref, vir_row_ref, energy_row_ref, from_ref, to_ref,
+    slot_ref, valid_ref, fits_ref, rank_ref, pick_ref, keep_ref, divisor_ref,
+):
     g = lax.axis_index("grp")
-    mine = mine_ref[...]
-    held = amounts(mine, counts_ref, g)
+    m = lax.axis_index("blk")
+    own = labels_of(own_share(vir_row_ref, g))
+    rank = jnp.sum(same_before(own), axis=0, keepdims=True).astype(I32)
+    rank_ref[...] = rank
+    pick_ref[...] = (iota((FOLD, CP), 0) == rank).astype(F32)
+
+    counts = []
+    for share in range(G):
+        row = labels_of(share_of(vir_row_ref, share))
+        counts.append([jnp.sum((row == label).astype(F32), axis=1, keepdims=True).astype(I32) for label in range(8)])
+    held = counts[0]
+    for share in range(1, G):
+        held = [jnp.where(g == share, new, old) for new, old in zip(counts[share], held)]
+
+    number = iota((M, T), 0) * T + iota((M, T), 1)
+    k, j = number // O, number % O
+    kind_k, kind_j = jnp.zeros((M, T), I32), jnp.zeros((M, T), I32)
+    for o in range(O):
+        kind_k = jnp.where(k == o, occ_ref[o], kind_k)
+        kind_j = jnp.where(j == o, occ_ref[o], kind_j)
+    kinds = one_hot(jnp.bitwise_xor(kind_k, kind_j))
+    rows = iota((M * BL, 1), 0)
+    label = jnp.zeros((M * BL, 1), I32)
+    for b in range(BL):
+        label = jnp.where(rows % BL == b, vir_ref[m * BL + b], label)
+    mine = dot(one_hot(iota((M * BL, M), 0) // BL == iota((M * BL, M), 1)), kinds).astype(I32)
+    mine = jnp.bitwise_xor(mine, label)
+    every = dot(one_hot(iota((M * 8, M), 0) // 8 == iota((M * 8, M), 1)), kinds).astype(I32)
+    every = jnp.bitwise_xor(every, iota((M * 8, 1), 0) % 8)
+
+    amount_of = amounts(mine, held)
     pair = iota((T, CP), 0)
     at = iota((T, CP), 1) // FOLD
-    rank = iota((M * BL, CP), 1) % FOLD
+    place = iota((M * BL, CP), 1) % FOLD
     real = iota((M * BL, CP), 1) < GT * FOLD
     for group in range(NG):
-        start = dot(held, (pair < GT * group + at).astype(F32).astype(BF16)).astype(I32)
-        amount = dot(held, (pair == GT * group + at).astype(F32).astype(BF16)).astype(I32)
-        slot_ref[group] = jnp.where(real & (rank < amount), start + rank, -1)
-    label = mine.astype(F32).astype(BF16)
+        start = dot(amount_of, one_hot(pair < GT * group + at)).astype(I32)
+        amount = dot(amount_of, one_hot(pair == GT * group + at)).astype(I32)
+        slot_ref[group] = jnp.where(real & (place < amount), start + place, -1)
+    mine = one_hot(mine)
     for t in range(T):
-        wide = dot(label, (pair == t).astype(F32).astype(BF16)).astype(I32)
-        valid_ref[t] = (wide == c_ref[...]).astype(F32)
+        valid_ref[t] = (dot(mine, one_hot(pair == t)).astype(I32) == own).astype(F32)
+
+    most = counts[0][0]
+    for share in range(G):
+        for count in counts[share]:
+            most = jnp.maximum(most, count)
     good = jnp.ones((8 * M, T), F32)
-    earlier = (iota((T, T), 0) < iota((T, T), 1)).astype(F32).astype(BF16)
-    most = counts_ref[0, 0]
-    for other in range(G):
-        for label in range(8):
-            most = jnp.maximum(most, counts_ref[other, label])
-    for other in range(G):
-        start = dot(amounts(all_ref[...], counts_ref, other), earlier).astype(I32)
+    earlier = one_hot(iota((T, T), 0) < iota((T, T), 1))
+    for share in range(G):
+        start = dot(amounts(every, counts[share]), earlier).astype(I32)
         good = jnp.where((start >= from_ref[...]) & (start + most <= to_ref[...]), good, 0.0)
-    fits = jnp.min(good, axis=(0, 1), keepdims=True)
-    fits = jnp.where(most <= FOLD, fits, 0.0)
+    fits = jnp.where(most <= FOLD, jnp.min(good, axis=(0, 1), keepdims=True), 0.0)
     fits_ref[...] = jnp.broadcast_to(fits, (8, CP))
 
-
-def tables(counts, mine, every, own_c, low, high):
+    row = iota((J4, CP), 0)
+    occ_label, occ_energy = jnp.zeros((J4, CP), I32), jnp.zeros((J4, CP), F32)
+    for o in range(O):
+        occ_label = jnp.where(row % O == o, occ_ref[o], occ_label)
+        occ_energy = jnp.where(row % O == o, occ_energy_ref[o], occ_energy)
+    vir_label, vir_energy = jnp.zeros((J4, CP), I32), jnp.zeros((J4, CP), F32)
+    for b in range(BL):
+        vir_label = jnp.where(row // O == b, vir_ref[m * BL + b], vir_label)
+        vir_energy = jnp.where(row // O == b, vir_energy_ref[m * BL + b], vir_energy)
+    need = jnp.bitwise_xor(own, occ_ref[0])
+    keep_ref[...] = (need == jnp.bitwise_xor(occ_label, vir_label)).astype(F32)
+    row_energy = occ_energy_ref[0] - own_share(energy_row_ref, g)
+    divisor_ref[...] = row_energy + (occ_energy - vir_energy)
+
+
+def tables(occ_irrep, vir_irrep, occ_energy, vir_energy):
+    smem = pl.BlockSpec(memory_space=pltpu.SMEM)
     vmem = pl.BlockSpec(memory_space=pltpu.VMEM)
+    low, high = (jnp.array(x, I32).reshape(1, T) for x in (SLOT_FROM, SLOT_TO))
     return pl.pallas_call(
         table_kernel,
         name="tables",
@@ -231,10 +308,14 @@
             pltpu.HBM((NG, M * BL, CP), I32),
             jax.ShapeDtypeStruct((T, M * BL, CP), F32),
             jax.ShapeDtypeStruct((8, CP), F32),
+            jax.ShapeDtypeStruct((1, CP), I32),
+            jax.ShapeDtypeStruct((FOLD, CP), F32),
+            jax.ShapeDtypeStruct((J4, CP), F32),
+            jax.ShapeDtypeStruct((J4, CP), F32),
         ),
-        in_specs=[pl.BlockSpec(memory_space=pltpu.SMEM)] + [vmem] * 5,
+        in_specs=[smem] * 4 + [vmem] * 4,
         compiler_params=pltpu.CompilerParams(vmem_limit_bytes=8 << 20),
-    )(counts, mine, every, own_c, low, high)
+    )(occ_irrep, vir_irrep, occ_energy, vir_energy, vir_irrep.reshape(1, V), vir_energy.reshape(1, V), low, high)
 
 
 def contract_kernel(
@@ -332,73 +413,44 @@
     )(in_hbm(received), in_hbm(slots), valid, rank, in_hbm(high), in_hbm(low))
 
 
-def finish_kernel(a_ref, b_ref, rank_ref, need_ref, have_ref, row_ref, column_ref, out_ref):
+def finish_kernel(a_ref, b_ref, pick_ref, keep_ref, divisor_ref, out_ref):
     folded = a_ref[...] + b_ref[...]
     source = iota((J4, J4), 0)
     target = iota((J4, J4), 1)
     move = (source % BL) * O + source // BL == target
     folded = jnp.dot(folded, move.astype(F32), precision=HIGHEST, preferred_element_type=F32)
-    pick = (iota((FOLD, CL), 0) == rank_ref[...]).astype(F32)
-    wide = jnp.dot(jnp.transpose(folded), pick, precision=HIGHEST, preferred_element_type=F32)
-    wide = jnp.where(need_ref[...] == have_ref[...], wide, 0.0)
-    out_ref[...] = wide / (row_ref[...] + column_ref[...])
-
-
-def finish(a, b, rank, need, have, row, column):
+    wide = jnp.dot(jnp.transpose(folded), pick_ref[...], precision=HIGHEST, preferred_element_type=F32)
+    wide = jnp.where(keep_ref[...] > 0, wide, 0.0) / divisor_ref[...]
+    out_ref[...] = wide[:, 0:CL]
+
+
+def finish(a, b, pick, keep, divisor):
     return pl.pallas_call(
         finish_kernel,
         name="finish",
         out_shape=pltpu.HBM((J4, CL), F32),
         compiler_params=pltpu.CompilerParams(vmem_limit_bytes=4 << 20),
-    )(a, b, rank, need, have, row, column)
+    )(a, b, pick, keep, divisor)
 
 
 def packed_form(amplitudes, cycle_weight, occ_irrep, vir_irrep, occ_energy, vir_energy):
     g = lax.axis_index("grp")
-    m = lax.axis_index("blk")
-    labels = jnp.arange(8, dtype=I32)
-    sent = pack(occ_irrep, vir_irrep.reshape(1, V), amplitudes)
+    vir_row = vir_irrep.reshape(1, V)
+    sent = pack(occ_irrep, vir_row, amplitudes)
     received = lax.all_to_all(sent, "blk", 0, 0, tiled=True)
 
-    shares = vir_irrep.reshape(G, CL)
-    orbital = jnp.arange(CL)
-    earlier = orbital[:, None] < orbital[None, :]
-    ranks = jnp.sum((shares[:, :, None] == shares[:, None, :]) & earlier[None], axis=1).astype(I32)
-    counts = jnp.sum(shares[:, :, None] == labels, axis=1).astype(I32)
-    own = lax.dynamic_index_in_dim(shares, g, 0, keepdims=False)
-    own_rank = lax.dynamic_index_in_dim(ranks, g, 0, keepdims=False)
-    own_c = jnp.concatenate([own, jnp.full((CP - CL,), NONE, I32)])
-    rank_c = jnp.concatenate([own_rank, jnp.zeros((CP - CL,), I32)])
-
-    pairs = jnp.bitwise_xor(occ_irrep[:, None], occ_irrep[None, :]).reshape(M, 1, T)
-    own_b = lax.dynamic_slice_in_dim(vir_irrep, m * BL, BL)
-    mine = jnp.bitwise_xor(pairs, own_b[:, None]).reshape(M * BL, T)
-    every = jnp.bitwise_xor(pairs, labels[:, None]).reshape(M * 8, T)
-    low, high = (jnp.array(x, I32).reshape(1, T) for x in (SLOT_FROM, SLOT_TO))
-    slots, valid, fits = tables(counts, mine, every, own_c.reshape(1, CP), low, high)
-    fits = fits[0, 0] > 0.5
-
-    place = (jnp.minimum(ranks, FOLD) + jnp.where(ranks < FOLD, jnp.arange(G, dtype=I32)[:, None] * FOLD, V)).reshape(1, V)
-    need = jnp.bitwise_xor(vir_irrep, occ_irrep[0]).reshape(1, V)
-    have = jnp.bitwise_xor(own_c[:, None], occ_irrep[None, :]).reshape(1, CP * O)
-    high, low = fold(place, need, have, cycle_weight.T)
-
-    row_energy = (occ_energy[0] - lax.dynamic_slice_in_dim(vir_energy, g * CL, CL)).reshape(1, CL)
-    slab_energy = lax.dynamic_slice_in_dim(vir_energy, m * BL, BL)
-    col_energy = (occ_energy[None, :] - slab_energy[:, None]).reshape(J4, 1)
-    row_need = jnp.bitwise_xor(own, occ_irrep[0]).reshape(1, CL)
-    col_have = jnp.bitwise_xor(occ_irrep[None, :], own_b[:, None]).reshape(J4, 1)
-    row_rank = own_rank.reshape(1, CL)
-    slots, valid, fits, row_rank, row_need, col_have, row_energy, col_energy = lax.optimization_barrier(
-        (slots, valid, fits, row_rank, row_need, col_have, row_energy, col_energy)
-    )
-
-    partial = contract(received, slots, valid, rank_c.reshape(1, CP), high, low)
+    slots, valid, fits, rank, pick, keep, divisor = tables(occ_irrep, vir_irrep, occ_energy, vir_energy)
+    own = lax.dynamic_slice_in_dim(jnp.pad(vir_irrep, (0, CP - CL)), g * CL, CP)
+    own = jnp.where(jnp.arange(CP) < CL, own, NONE)
+    have = jnp.bitwise_xor(own[:, None], occ_irrep[None, :]).reshape(1, CP * O)
+    high, low = fold(occ_irrep, vir_row, have, cycle_weight.T)
+    fits, slots = lax.optimization_barrier((fits[0, 0] > 0.5, slots))
+
+    partial = contract(received, slots, valid, rank, high, low)
     near = lax.ppermute(partial[1:3], "grp", [(d, d ^ 1) for d in range(G)])
     mine = partial[0] + near[0]
     last = lax.ppermute(partial[3] + near[1], "grp", [(d, d ^ 3) for d in range(G)])
-    out = finish(mine, last, row_rank, row_need, col_have, row_energy, col_energy)
-    return out.T, fits
+    return finish(mine, last, pick, keep, divisor).T, fits
 
 
 def plain_form(amplitudes, cycle_weight, occ_irrep, vir_irrep, occ_energy, vir_energy):

time: 68.9 us -> 59 us (0.86)
  other arithmetic: 7.55 us -> 0.17 us
  local copies, waits for them, and re-layouts: 7.41 us -> 0.67 us
  waiting for transfers between devices: 5.22 us -> 8.08 us
  Pallas kernels: 29.9 us -> 31.6 us
    xor x7 -> x1, other arithmetic: 3.77 us -> 0.08 us  [packed_form(): have = jnp.bitwise_xor(own[:, None], occ_irrep[None, :]).reshape(1, CP * O)]
    all_to_all x1, waiting for transfers between devices: 0.01 us -> 2.68 us  [packed_form(): received = lax.all_to_all(sent, 'blk', 0, 0, tiled=True)]
    unnamed x22 -> x18, local copies, waits for them, and re-layouts: 1.57 us -> 0.04 us
    dynamic_slice x3 -> x0, local copies, waits for them, and re-layouts: 1.53 us -> none  [the longest x1 0.76 us: packed_form(): slab_energy = lax.dynamic_slice_in_dim(vir_energy, m * BL, BL)]
    reshape x1 -> x0, other arithmetic: 1.4 us -> none  [packed_form(): (occ_energy[0] - lax.dynamic_slice_in_dim(vir_energy, g * CL, CL)).reshap...]
    xor x8 -> x1, local copies, waits for them, and re-layouts: 1.16 us -> 0.11 us  [packed_form(): have = jnp.bitwise_xor(own[:, None], occ_irrep[None, :]).reshape(1, CP * O)]
    pallas_call x1, Pallas kernels: 3.3 us -> 4.32 us  [tables(): pl.pallas_call(table_kernel, name='tables', out_shape=(pltpu.HBM((NG, M *...]
    reduce_sum x2 -> x0, other arithmetic: 0.93 us -> none  [the longest x1 0.79 us: packed_form(): jnp.sum((shares[:, :, None] == shares[:, None, :]) & earlier[None], axis=1)]
  transfers between devices with their start and end apart: 3 -> 3, of which waited for: 2 -> 3; matrix products, arithmetic and copies ran while one was open for 20% -> 1% of each run, Pallas kernels for 21% -> 28%
where the time goes in v6:
time: 59 us; the launch traced here: 58.4 us
  Pallas kernels  31.6 us (54%)
  starting transfers between devices  16.9 us (29%)
  waiting for transfers between devices  8.08 us (14%)
  between operations  0.95 us (2%)
  local copies, waits for them, and re-layouts  0.67 us (1%)
    all_to_all x1, starting transfers between devices, packed_form(): received = lax.all_to_all(sent, 'blk', 0, 0, tiled=True)  12.3 us
    pallas_call x1, Pallas kernels, fold(): pl.pallas_call(fold_kernel, name='fold_weights', grid=(CP // CS,), out_sh...  11.8 us
    pallas_call x1, Pallas kernels, contract(): pl.pallas_call(contract_kernel, name='contract', out_shape=jax.ShapeDtype...  7.16 us
    pallas_call x1, Pallas kernels, pack(): pl.pallas_call(pack_kernel, name='pack_amplitudes', grid=(T // TS,), out_...  7.13 us
    pallas_call x1, Pallas kernels, tables(): pl.pallas_call(table_kernel, name='tables', out_shape=(pltpu.HBM((NG, M *...  4.32 us
    ppermute x1, starting transfers between devices, packed_form(): lax.ppermute(partial[3] + near[1], 'grp', [(d, d ^ 3) for d in range(G)])  3.03 us
    ppermute x1, waiting for transfers between devices, packed_form(): near = lax.ppermute(partial[1:3], 'grp', [(d, d ^ 1) for d in range(G)])  2.95 us
    all_to_all x1, waiting for transfers between devices, packed_form(): received = lax.all_to_all(sent, 'blk', 0, 0, tiled=True)  2.68 us
  transfers between devices with their start and end apart: 3, of which 3 were waited for; matrix products, arithmetic and copies ran while one was open for 1% of the time, Pallas kernels for 28%

profile of v6, /device:TPU:8, one launch (start us, length us, event | category | flops | bytes accessed | tf_op | source)
XLA Modules:
  0.0 58.4 jit_solution(4821715572814535290)
XLA Ops:
  0.0 0.0 copy-start.4
  0.0 0.0 copy-start.6
  0.0 0.0 copy-start.8
  0.0 7.1 %pack_amplitudes.1 = f32[64,4,640]{2,1,0:T(4,128)} custom-call(s32[40]{0:T(128)} %occ_ref.5, s32[1,500]{1,0:T(1,128)} %bitcast.37, f32[25,125,256]{2,1,0:T(8,128)} %amp_ref.1), custom_call_target="tpu_custom_call" | custom-call | tf_op jit(solution)/shard_map/pack_amplitudes/pallas_call | solution.py:133
  7.2 12.3 %all-to-all-start.2 = ((f32[64,4,640]{2,1,0:T(4,128)}), f32[64,4,640]{2,1,0:T(4,128)}, u32[]{:S(2)}, u32[]{:S(2)}) async-start(f32[64,4,640]{2,1,0:T(4,128)} %pack_amplitudes.1), calls=%async_computation.2 | async-start | bytes 1310720 | tf_op jit(solution)/shard_map/all_to_all | solution.py:440
  19.5 0.0 copy-done
  19.5 0.0 copy-done.1
  19.5 0.0 copy-done.3
  19.5 0.0 copy-done.4
  19.5 0.0 copy-done.6
  19.5 4.3 %tables.1 = (s32[9,256,128]{2,1,0:T(8,128)}, f32[25,256,128]{2,1,0:T(8,128)S(1)}, f32[8,128]{1,0:T(8,128)S(1)}, s32[1,128]{1,0:T(1,128)S(1)}, f32[40,128]{1,0:T(...) custom-call(s32[40]{0:T(128)S(1)} %copy-done.4, s32[500]{0:T(512)S(1)} %copy-done.3, f32[40]{0:T(128)S(1)} %copy-done.8, ...), custom_call_target="tpu_custom_call" | custom-call | tf_op jit(solution)/shard_map/tables/pallas_call | solution.py:304
  23.8 0.5 slice.24
  25.0 0.1 compare_select_fusion.2
  25.1 0.1 broadcast_xor_fusion.4
  25.2 0.1 xor.83.have_ref
  25.3 11.8 %fold_weights.1 = (bf16[40,128,160]{2,1,0:T(8,128)(2,1)}, bf16[40,128,160]{2,1,0:T(8,128)(2,1)}) custom-call(s32[40]{0:T(128)} %occ_ref.5, s32[1,500]{1,0:T(1,128)S(1)} %bitcast.39, s32[1,5120]{1,0:T(1,128)S(1)} %xor.83.have_ref, f32[5000,500]{1,0:T(8,128)} %bitcast.31), custom_call_target="tpu_custom_call" | custom-call | tf_op jit(solution)/shard_map/fold_weights/pallas_call | solution.py:200
  37.1 2.7 %all-to-all-done.2.far_x_ref = f32[64,4,640]{2,1,0:T(4,128)} async-done(((f32[64,4,640]{2,1,0:T(4,128)}), f32[64,4,640]{2,1,0:T(4,128)}, u32[]{:S(2)}, u32[]{:S(2)}) %all-to-all-start.2) | async-done | bytes 655392 | tf_op jit(solution)/shard_map/all_to_all | solution.py:440
  39.8 7.2 %contract.1 = f32[4,40,160]{2,1,0:T(8,128)S(1)} custom-call(f32[64,4,640]{2,1,0:T(4,128)} %all-to-all-done.2.far_x_ref, s32[9,256,128]{2,1,0:T(8,128)} %get-tuple-element.41.far_slot_ref, f32[25,256,128]{2,1,0:T(8,128)S(1)} %get-tuple-element.42.valid_ref, s32[1,128]{1,0:T(1,128)S(1)} %get-tuple-element.43.rank_ref, ...), custom_call_target="tpu_custom_call" | custom-call | tf_op jit(solution)/shard_map/contract/pallas_call | solution.py:397
  47.0 1.6 %collective-permute-start = (f32[2,40,160]{2,1,0:T(8,128)S(1)}, f32[2,40,160]{2,1,0:T(8,128)S(1)}, u32[]{:S(2)}, u32[]{:S(2)}) collective-permute-start(f32[2,40,160]{2,1,0:T(8,128)S(1)} %slice.31), channel_id=1, source_target_pairs={{0,64},{64,0},{128,192},{192,128},{1,65},{65,1},{129,193},{193,129... | collective-permute-start | bytes 153608 | tf_op jit(solution)/shard_map/ppermute | solution.py:450
  48.5 2.9 %collective-permute-done = f32[2,40,160]{2,1,0:T(8,128)S(1)} collective-permute-done((f32[2,40,160]{2,1,0:T(8,128)S(1)}, f32[2,40,160]{2,1,0:T(8,128)S(1)}, u32[]{:S(2)}, u32[]{:S(2)}) %collective-permute-start) | collective-permute-done | bytes 51232 | tf_op jit(solution)/shard_map/ppermute | solution.py:450
  51.5 3.0 %collective-permute-start.1 = (f32[40,160]{1,0:T(8,128)S(1)}, f32[40,160]{1,0:T(8,128)S(1)}, u32[]{:S(2)}, u32[]{:S(2)}) collective-permute-start(f32[40,160]{1,0:T(8,128)S(1)} %get-tuple-element.62), channel_id=1, source_target_pairs={{0,192},{64,128},{128,64},{192,0},{1,193},{65,129},{129,65},{193,1... | collective-permute-start | bytes 76808 | tf_op jit(solution)/shard_map/ppermute | solution.py:452
  54.5 2.5 %collective-permute-done.1.b_ref = f32[40,160]{1,0:T(8,128)S(1)} collective-permute-done((f32[40,160]{1,0:T(8,128)S(1)}, f32[40,160]{1,0:T(8,128)S(1)}, u32[]{:S(2)}, u32[]{:S(2)}) %collective-permute-start.1) | collective-permute-done | bytes 25632 | tf_op jit(solution)/shard_map/ppermute | solution.py:452
  57.0 1.2 %finish.1 = f32[160,125]{1,0:T(8,128)} custom-call(f32[40,160]{1,0:T(8,128)S(1)} %get-tuple-element.63.a_ref, f32[40,160]{1,0:T(8,128)S(1)} %collective-permute-done.1.b_ref, f32[40,128]{1,0:T(8,128)S(1)} %get-tuple-element.46.pick_ref, f32[160,128]{1,0:T(8,128)S(1)} %get-tuple-element.47.keep_ref, f32[160,128]{1,0:T(8,128)S(1)} %get-tuple-element.48.divisor_ref), custom_call_target="tpu_custom_call" | custom-call | tf_op jit(solution)/shard_map/finish/pallas_call | solution.py:428
  58.2 0.0 copy-done.9
  (12 shorter events, 0.0 us)
Async XLA Ops:
  0.0 19.5 %copy-start = (s32[1,25]{1,0:T(1,128)S(1)}, s32[1,25]{1,0:T(1,128)}, u32[]{:S(2)}) copy-start(s32[1,25]{1,0:T(1,128)} %constant.48.from_ref) | copy-start | bytes 304
  0.0 19.5 %copy-start.1 = (s32[1,25]{1,0:T(1,128)S(1)}, s32[1,25]{1,0:T(1,128)}, u32[]{:S(2)}) copy-start(s32[1,25]{1,0:T(1,128)} %constant.49.to_ref) | copy-start | bytes 304
  0.0 19.5 %copy-start.3 = (s32[500]{0:T(512)S(1)}, s32[500]{0:T(512)}, u32[]{:S(2)}) copy-start(s32[500]{0:T(512)} %vir_ref.1) | copy-start | bytes 6004
  0.0 19.5 %copy-start.4 = (s32[40]{0:T(128)S(1)}, s32[40]{0:T(128)}, u32[]{:S(2)}) copy-start(s32[40]{0:T(128)} %occ_ref.5) | copy-start | bytes 484
  0.0 19.5 %copy-start.6 = (f32[500]{0:T(512)S(1)}, f32[500]{0:T(512)}, u32[]{:S(2)}) copy-start(f32[500]{0:T(512)} %vir_energy_ref.1) | copy-start | bytes 6004
  0.0 19.5 %copy-start.8 = (f32[40]{0:T(128)S(1)}, f32[40]{0:T(128)}, u32[]{:S(2)}) copy-start(f32[40]{0:T(128)} %occ_energy_ref.1) | copy-start | bytes 484
  7.2 32.6 %all-to-all-start.2 = ((f32[64,4,640]{2,1,0:T(4,128)}), f32[64,4,640]{2,1,0:T(4,128)}, u32[]{:S(2)}, u32[]{:S(2)}) async-start(f32[64,4,640]{2,1,0:T(4,128)} %pack_amplitudes.1), calls=%async_computation.2 | async-start | bytes 1310720 | tf_op jit(solution)/shard_map/all_to_all | solution.py:440
  39.8 18.4 %copy-start.5 = (s32[40]{0:T(128)S(1)}, s32[40]{0:T(128)}, u32[]{:S(2)}) copy-start(s32[40]{0:T(128)} %occ_ref.5) | copy-start | bytes 484
  39.8 18.4 %copy-start.7 = (f32[500]{0:T(512)S(1)}, f32[500]{0:T(512)}, u32[]{:S(2)}) copy-start(f32[500]{0:T(512)} %vir_energy_ref.1) | copy-start | bytes 6004
  39.8 18.4 %copy-start.9 = (f32[40]{0:T(128)S(1)}, f32[40]{0:T(128)}, u32[]{:S(2)}) copy-start(f32[40]{0:T(128)} %occ_energy_ref.1) | copy-start | bytes 484
  47.0 4.5 %collective-permute-start = (f32[2,40,160]{2,1,0:T(8,128)S(1)}, f32[2,40,160]{2,1,0:T(8,128)S(1)}, u32[]{:S(2)}, u32[]{:S(2)}) collective-permute-start(f32[2,40,160]{2,1,0:T(8,128)S(1)} %slice.31), channel_id=1, source_target_pairs={{0,64},{64,0},{128,192},{192,128},{1,65},{65,1},{129,193},{193,129... | collective-permute-start | bytes 153608 | tf_op jit(solution)/shard_map/ppermute | solution.py:450
  51.5 5.5 %collective-permute-start.1 = (f32[40,160]{1,0:T(8,128)S(1)}, f32[40,160]{1,0:T(8,128)S(1)}, u32[]{:S(2)}, u32[]{:S(2)}) collective-permute-start(f32[40,160]{1,0:T(8,128)S(1)} %get-tuple-element.62), channel_id=1, source_target_pairs={{0,192},{64,128},{128,64},{192,0},{1,193},{65,129},{129,65},{193,1... | collective-permute-start | bytes 76808 | tf_op jit(solution)/shard_map/ppermute | solution.py:452

commit v7 on v6

--- a/solution.py
+++ b/solution.py
@@ -79,7 +79,7 @@
     return lax.broadcasted_iota(I32, shape, dim)
 
 
-def pack_kernel(occ_ref, vir_ref, amp_ref, out_ref, rank_ref, column_ref, count_ref, base_ref, total_ref, pick_ref, high_ref, low_ref):
+def pack_kernel(occ_ref, vir_ref, amp_ref, out_ref, rank_ref, column_ref, count_ref, base_ref, total_ref, pick_ref, both_ref):
     step = pl.program_id(0)
     g = lax.axis_index("grp")
     m = lax.axis_index("blk")
@@ -119,10 +119,10 @@
                     lanes = slice(half * CP, (half + 1) * CP)
                     block = jnp.where(need == vir_ref[:, lanes], amp_ref[t, :, lanes], 0.0)
                     high, low = halves(block)
-                    high_ref[columns, lanes] = high
-                    low_ref[columns, lanes] = low
+                    both_ref[columns, lanes] = high
+                    both_ref[TS * CP + t * CP : TS * CP + (t + 1) * CP, lanes] = low
             pick = pick_ref[0 : last - first]
-            total_ref[first:last] += dot(pick, high_ref[...]) + dot(pick, low_ref[...])
+            total_ref[first:last] += dot(jnp.concatenate([pick, pick], axis=1), both_ref[...])
 
     @pl.when(step == pl.num_programs(0) - 1)
     def _():
@@ -148,8 +148,7 @@
             pltpu.VMEM((8, CP), I32),
             pltpu.VMEM((SLOTS, BW), F32),
             pltpu.VMEM((SLOTS, TS * CP), BF16),
-            pltpu.VMEM((TS * CP, BW), BF16),
-            pltpu.VMEM((TS * CP, BW), BF16),
+            pltpu.VMEM((2 * TS * CP, BW), BF16),
         ],
         compiler_params=pltpu.CompilerParams(vmem_limit_bytes=8 << 20),
     )(occ_irrep, vir_row, amplitudes)
@@ -318,40 +317,64 @@
     )(occ_irrep, vir_irrep, occ_energy, vir_energy, vir_irrep.reshape(1, V), vir_energy.reshape(1, V), low, high)
 
 
+REST = J4 - CP
+DENSE = FOLD + 16
+
+
+def to_lanes(x):
+    rest = [x[at : at + 8, CP:J4] for at in range(0, FOLD, 8)]
+    tail = jnp.concatenate(rest[4:] + [jnp.zeros((8, CP - REST), F32)], axis=1)
+    return jnp.concatenate([x[:, 0:CP], jnp.concatenate(rest[:4], axis=1), tail], axis=0)
+
+
+def from_lanes(x):
+    rest = [x[FOLD : FOLD + 8, at * REST : (at + 1) * REST] for at in range(4)] + [x[FOLD + 8 : DENSE, 0:REST]]
+    return jnp.concatenate([x[0:FOLD], jnp.concatenate(rest, axis=0)], axis=1)
+
+
 def contract_kernel(
     far_x_ref, far_slot_ref, valid_ref, rank_ref, far_high_ref, far_low_ref, out_ref,
     x_ref, slot_ref, seen_ref, spread_ref, wide_ref, high_ref, low_ref, sem,
 ):
     g = lax.axis_index("grp")
-    first_copies = [
-        pltpu.make_async_copy(far_x_ref, x_ref, sem.at[2]),
-        pltpu.make_async_copy(far_slot_ref, slot_ref, sem.at[3]),
-    ]
+    quarter = M // 4
+    x_copies, slot_copies = [], []
+    for part in range(4):
+        x_rows = pl.ds(part * quarter, quarter)
+        slot_rows = pl.ds(part * quarter * BL, quarter * BL)
+        x_copies.append(pltpu.make_async_copy(far_x_ref.at[x_rows], x_ref.at[x_rows], sem.at[2 + part]))
+        slot_copies.append(
+            pltpu.make_async_copy(far_slot_ref.at[:, slot_rows], slot_ref.at[:, slot_rows], sem.at[6 + part])
+        )
+        x_copies[part].start()
+        slot_copies[part].start()
     copies = [
         pltpu.make_async_copy(far_high_ref, high_ref, sem.at[0]),
         pltpu.make_async_copy(far_low_ref, low_ref, sem.at[1]),
     ]
-    for copy in first_copies + copies:
+    for copy in copies:
         copy.start()
-    for copy in first_copies:
-        copy.wait()
-
-    @pl.loop(0, M // 8)
-    def _(i):
-        for near in range(4):
-            packed = x_ref[pl.ds(8 * i + 2 * near, 2)].reshape(2 * BL, SLOTS)
-            rows = pl.ds(pl.multiple_of(32 * i, 8) + 8 * near, 8)
-            for group, (first, last) in enumerate(GROUP_BLOCKS):
-                slot = slot_ref[group, rows, :]
-                lane = jnp.bitwise_and(slot, CP - 1)
-                where = jnp.right_shift(slot, 7)
-                found = jnp.zeros((8, CP), F32)
-                for part in range(first, last):
-                    taken = jnp.take_along_axis(
-                        packed[:, part * CP : (part + 1) * CP], lane, axis=1, mode="promise_in_bounds"
-                    )
-                    found = jnp.where(where == part, taken, found)
-                seen_ref[group, rows, :] = found
+
+    for quarter_at in range(4):
+        x_copies[quarter_at].wait()
+        slot_copies[quarter_at].wait()
+
+        @pl.loop(quarter_at * 2, quarter_at * 2 + 2)
+        def _(i):
+            for near in range(4):
+                packed = x_ref[pl.ds(8 * i + 2 * near, 2)].reshape(2 * BL, SLOTS)
+                rows = pl.ds(pl.multiple_of(32 * i, 8) + 8 * near, 8)
+                for group, (first, last) in enumerate(GROUP_BLOCKS):
+                    slot = slot_ref[group, rows, :]
+                    lane = jnp.bitwise_and(slot, CP - 1)
+                    where = jnp.right_shift(slot, 7)
+                    found = jnp.zeros((8, CP), F32)
+                    for part in range(first, last):
+                        taken = jnp.take_along_axis(
+                            packed[:, part * CP : (part + 1) * CP], lane, axis=1, mode="promise_in_bounds"
+                        )
+                        found = jnp.where(where == part, taken, found)
+                    seen_ref[group, rows, :] = found
 
     place = [(iota((CP, CP), 0) - at * FOLD == rank_ref[...]).astype(F32).astype(BF16) for at in range(GT)]
     place = jnp.concatenate(place, axis=1)
@@ -388,7 +411,8 @@
 
     turned = jnp.transpose(total)
     for block in range(G):
-        out_ref[jnp.bitwise_xor(g, block)] = turned[block * FOLD : (block + 1) * FOLD]
+        part = turned[block * FOLD : (block + 1) * FOLD]
+        out_ref[jnp.bitwise_xor(g, block)] = to_lanes(part)
 
 
 def contract(received, slots, valid, rank, high, low):
@@ -397,7 +421,7 @@
     return pl.pallas_call(
         contract_kernel,
         name="contract",
-        out_shape=jax.ShapeDtypeStruct((G, FOLD, J4), F32),
+        out_shape=jax.ShapeDtypeStruct((G, DENSE, CP), F32),
         in_specs=[hbm, hbm, vmem, vmem, hbm, hbm],
         scratch_shapes=[
             pltpu.VMEM((M, BL, SLOTS), F32),
@@ -407,19 +431,22 @@
             pltpu.VMEM((O * O * BL, CP), F32),
             pltpu.VMEM((O, CP, NF), BF16),
             pltpu.VMEM((O, CP, NF), BF16),
-            pltpu.SemaphoreType.DMA((4,)),
+            pltpu.SemaphoreType.DMA((10,)),
         ],
         compiler_params=pltpu.CompilerParams(vmem_limit_bytes=20 << 20),
     )(in_hbm(received), in_hbm(slots), valid, rank, in_hbm(high), in_hbm(low))
 
 
 def finish_kernel(a_ref, b_ref, pick_ref, keep_ref, divisor_ref, out_ref):
-    folded = a_ref[...] + b_ref[...]
+    folded = from_lanes(a_ref[...] + b_ref[...])
     source = iota((J4, J4), 0)
     target = iota((J4, J4), 1)
     move = (source % BL) * O + source // BL == target
-    folded = jnp.dot(folded, move.astype(F32), precision=HIGHEST, preferred_element_type=F32)
-    wide = jnp.dot(jnp.transpose(folded), pick_ref[...], precision=HIGHEST, preferred_element_type=F32)
+    high, low = halves(folded)
+    folded = dot(high, one_hot(move)) + dot(low, one_hot(move))
+    high, low = halves(jnp.transpose(folded))
+    pick = pick_ref[...].astype(BF16)
+    wide = dot(high, pick) + dot(low, pick)
     wide = jnp.where(keep_ref[...] > 0, wide, 0.0) / divisor_ref[...]
     out_ref[...] = wide[:, 0:CL]
 

time: 59 us -> 58.2 us (0.986)
  Pallas kernels: 31.6 us -> 31 us
where the time goes in v7:
time: 58.2 us; the launch traced here: 57.7 us
  Pallas kernels  31 us (53%)
  starting transfers between devices  16.9 us (29%)
  waiting for transfers between devices  7.69 us (13%)
  between operations  0.99 us (2%)
  local copies, waits for them, and re-layouts  0.67 us (1%)
    all_to_all x1, starting transfers between devices, packed_form(): received = lax.all_to_all(sent, 'blk', 0, 0, tiled=True)  12.3 us
    pallas_call x1, Pallas kernels, fold(): pl.pallas_call(fold_kernel, name='fold_weights', grid=(CP // CS,), out_sh...  11.8 us
    pallas_call x1, Pallas kernels, pack(): pl.pallas_call(pack_kernel, name='pack_amplitudes', grid=(T // TS,), out_...  6.97 us
    pallas_call x1, Pallas kernels, contract(): pl.pallas_call(contract_kernel, name='contract', out_shape=jax.ShapeDtype...  6.87 us
    pallas_call x1, Pallas kernels, tables(): pl.pallas_call(table_kernel, name='tables', out_shape=(pltpu.HBM((NG, M *...  4.32 us
    ppermute x1, starting transfers between devices, packed_form(): lax.ppermute(partial[3] + near[1], 'grp', [(d, d ^ 3) for d in range(G)])  3.03 us
    ppermute x1, waiting for transfers between devices, packed_form(): near = lax.ppermute(partial[1:3], 'grp', [(d, d ^ 1) for d in range(G)])  2.69 us
    all_to_all x1, waiting for transfers between devices, packed_form(): received = lax.all_to_all(sent, 'blk', 0, 0, tiled=True)  2.68 us
  transfers between devices with their start and end apart: 3, of which 3 were waited for; matrix products, arithmetic and copies ran while one was open for 1% of the time, Pallas kernels for 28%

profile of v7, /device:TPU:8, one launch (start us, length us, event | category | flops | bytes accessed | tf_op | source)
XLA Modules:
  0.0 57.7 jit_solution(10413018326028295359)
XLA Ops:
  0.0 0.0 copy-start.4
  0.0 0.0 copy-start.6
  0.0 0.0 copy-start.8
  0.0 7.0 %pack_amplitudes.1 = f32[64,4,640]{2,1,0:T(4,128)} custom-call(s32[40]{0:T(128)} %occ_ref.5, s32[1,500]{1,0:T(1,128)} %bitcast.37, f32[25,125,256]{2,1,0:T(8,128)} %amp_ref.1), custom_call_target="tpu_custom_call" | custom-call | tf_op jit(solution)/shard_map/pack_amplitudes/pallas_call | solution.py:133
  7.0 12.3 %all-to-all-start.2 = ((f32[64,4,640]{2,1,0:T(4,128)}), f32[64,4,640]{2,1,0:T(4,128)}, u32[]{:S(2)}, u32[]{:S(2)}) async-start(f32[64,4,640]{2,1,0:T(4,128)} %pack_amplitudes.1), calls=%async_computation.2 | async-start | bytes 1310720 | tf_op jit(solution)/shard_map/all_to_all | solution.py:467
  19.3 0.0 copy-done
  19.3 0.0 copy-done.1
  19.3 0.0 copy-done.3
  19.3 0.0 copy-done.4
  19.3 4.3 %tables.1 = (s32[9,256,128]{2,1,0:T(8,128)}, f32[25,256,128]{2,1,0:T(8,128)S(1)}, f32[8,128]{1,0:T(8,128)S(1)}, s32[1,128]{1,0:T(1,128)S(1)}, f32[40,128]{1,0:T(...) custom-call(s32[40]{0:T(128)S(1)} %copy-done.4, s32[500]{0:T(512)S(1)} %copy-done.3, f32[40]{0:T(128)S(1)} %copy-done.8, ...), custom_call_target="tpu_custom_call" | custom-call | tf_op jit(solution)/shard_map/tables/pallas_call | solution.py:303
  23.7 0.5 slice.24
  24.8 0.1 compare_select_fusion.2
  24.9 0.1 broadcast_xor_fusion.4
  25.0 0.1 xor.83.have_ref
  25.1 11.8 %fold_weights.1 = (bf16[40,128,160]{2,1,0:T(8,128)(2,1)}, bf16[40,128,160]{2,1,0:T(8,128)(2,1)}) custom-call(s32[40]{0:T(128)} %occ_ref.5, s32[1,500]{1,0:T(1,128)S(1)} %bitcast.39, s32[1,5120]{1,0:T(1,128)S(1)} %xor.83.have_ref, f32[5000,500]{1,0:T(8,128)} %bitcast.31), custom_call_target="tpu_custom_call" | custom-call | tf_op jit(solution)/shard_map/fold_weights/pallas_call | solution.py:199
  36.9 2.7 %all-to-all-done.2.far_x_ref = f32[64,4,640]{2,1,0:T(4,128)} async-done(((f32[64,4,640]{2,1,0:T(4,128)}), f32[64,4,640]{2,1,0:T(4,128)}, u32[]{:S(2)}, u32[]{:S(2)}) %all-to-all-start.2) | async-done | bytes 655392 | tf_op jit(solution)/shard_map/all_to_all | solution.py:467
  39.6 6.9 %contract.1 = f32[4,56,128]{2,1,0:T(8,128)S(1)} custom-call(f32[64,4,640]{2,1,0:T(4,128)} %all-to-all-done.2.far_x_ref, s32[9,256,128]{2,1,0:T(8,128)} %get-tuple-element.41.far_slot_ref, f32[25,256,128]{2,1,0:T(8,128)S(1)} %get-tuple-element.42.valid_ref, s32[1,128]{1,0:T(1,128)S(1)} %get-tuple-element.43.rank_ref, ...), custom_call_target="tpu_custom_call" | custom-call | tf_op jit(solution)/shard_map/contract/pallas_call | solution.py:421
  46.5 1.6 %collective-permute-start = (f32[2,56,128]{2,1,0:T(8,128)S(1)}, f32[2,56,128]{2,1,0:T(8,128)S(1)}, u32[]{:S(2)}, u32[]{:S(2)}) collective-permute-start(f32[2,56,128]{2,1,0:T(8,128)S(1)} %slice.31), channel_id=1, source_target_pairs={{0,64},{64,0},{128,192},{192,128},{1,65},{65,1},{129,193},{193,129... | collective-permute-start | bytes 172040 | tf_op jit(solution)/shard_map/ppermute | solution.py:477
  48.1 2.7 %collective-permute-done = f32[2,56,128]{2,1,0:T(8,128)S(1)} collective-permute-done((f32[2,56,128]{2,1,0:T(8,128)S(1)}, f32[2,56,128]{2,1,0:T(8,128)S(1)}, u32[]{:S(2)}, u32[]{:S(2)}) %collective-permute-start) | collective-permute-done | bytes 57376 | tf_op jit(solution)/shard_map/ppermute | solution.py:477
  50.8 3.0 %collective-permute-start.1 = (f32[56,128]{1,0:T(8,128)S(1)}, f32[56,128]{1,0:T(8,128)S(1)}, u32[]{:S(2)}, u32[]{:S(2)}) collective-permute-start(f32[56,128]{1,0:T(8,128)S(1)} %get-tuple-element.62), channel_id=1, source_target_pairs={{0,192},{64,128},{128,64},{192,0},{1,193},{65,129},{129,65},{193,1... | collective-permute-start | bytes 86024 | tf_op jit(solution)/shard_map/ppermute | solution.py:479
  53.8 2.3 %collective-permute-done.1.b_ref = f32[56,128]{1,0:T(8,128)S(1)} collective-permute-done((f32[56,128]{1,0:T(8,128)S(1)}, f32[56,128]{1,0:T(8,128)S(1)}, u32[]{:S(2)}, u32[]{:S(2)}) %collective-permute-start.1) | collective-permute-done | bytes 28704 | tf_op jit(solution)/shard_map/ppermute | solution.py:479
  56.1 1.1 %finish.1 = f32[160,125]{1,0:T(8,128)} custom-call(f32[56,128]{1,0:T(8,128)S(1)} %get-tuple-element.63.a_ref, f32[56,128]{1,0:T(8,128)S(1)} %collective-permute-done.1.b_ref, f32[40,128]{1,0:T(8,128)S(1)} %get-tuple-element.46.pick_ref, f32[160,128]{1,0:T(8,128)S(1)} %get-tuple-element.47.keep_ref, f32[160,128]{1,0:T(8,128)S(1)} %get-tuple-element.48.divisor_ref), custom_call_target="tpu_custom_call" | custom-call | tf_op jit(solution)/shard_map/finish/pallas_call | solution.py:455
  57.2 0.0 copy-done.7
  57.2 0.3 conditional.1
  (12 shorter events, 0.0 us)
Async XLA Ops:
  0.0 19.3 %copy-start = (s32[1,25]{1,0:T(1,128)S(1)}, s32[1,25]{1,0:T(1,128)}, u32[]{:S(2)}) copy-start(s32[1,25]{1,0:T(1,128)} %constant.48.from_ref) | copy-start | bytes 304
  0.0 19.3 %copy-start.1 = (s32[1,25]{1,0:T(1,128)S(1)}, s32[1,25]{1,0:T(1,128)}, u32[]{:S(2)}) copy-start(s32[1,25]{1,0:T(1,128)} %constant.49.to_ref) | copy-start | bytes 304
  0.0 19.3 %copy-start.3 = (s32[500]{0:T(512)S(1)}, s32[500]{0:T(512)}, u32[]{:S(2)}) copy-start(s32[500]{0:T(512)} %vir_ref.1) | copy-start | bytes 6004
  0.0 19.3 %copy-start.4 = (s32[40]{0:T(128)S(1)}, s32[40]{0:T(128)}, u32[]{:S(2)}) copy-start(s32[40]{0:T(128)} %occ_ref.5) | copy-start | bytes 484
  0.0 19.3 %copy-start.6 = (f32[500]{0:T(512)S(1)}, f32[500]{0:T(512)}, u32[]{:S(2)}) copy-start(f32[500]{0:T(512)} %vir_energy_ref.1) | copy-start | bytes 6004
  0.0 19.3 %copy-start.8 = (f32[40]{0:T(128)S(1)}, f32[40]{0:T(128)}, u32[]{:S(2)}) copy-start(f32[40]{0:T(128)} %occ_energy_ref.1) | copy-start | bytes 484
  7.0 32.6 %all-to-all-start.2 = ((f32[64,4,640]{2,1,0:T(4,128)}), f32[64,4,640]{2,1,0:T(4,128)}, u32[]{:S(2)}, u32[]{:S(2)}) async-start(f32[64,4,640]{2,1,0:T(4,128)} %pack_amplitudes.1), calls=%async_computation.2 | async-start | bytes 1310720 | tf_op jit(solution)/shard_map/all_to_all | solution.py:467
  39.6 17.6 %copy-start.5 = (s32[40]{0:T(128)S(1)}, s32[40]{0:T(128)}, u32[]{:S(2)}) copy-start(s32[40]{0:T(128)} %occ_ref.5) | copy-start | bytes 484
  39.6 17.6 %copy-start.7 = (f32[500]{0:T(512)S(1)}, f32[500]{0:T(512)}, u32[]{:S(2)}) copy-start(f32[500]{0:T(512)} %vir_energy_ref.1) | copy-start | bytes 6004
  39.6 17.6 %copy-start.9 = (f32[40]{0:T(128)S(1)}, f32[40]{0:T(128)}, u32[]{:S(2)}) copy-start(f32[40]{0:T(128)} %occ_energy_ref.1) | copy-start | bytes 484
  46.5 4.3 %collective-permute-start = (f32[2,56,128]{2,1,0:T(8,128)S(1)}, f32[2,56,128]{2,1,0:T(8,128)S(1)}, u32[]{:S(2)}, u32[]{:S(2)}) collective-permute-start(f32[2,56,128]{2,1,0:T(8,128)S(1)} %slice.31), channel_id=1, source_target_pairs={{0,64},{64,0},{128,192},{192,128},{1,65},{65,1},{129,193},{193,129... | collective-permute-start | bytes 172040 | tf_op jit(solution)/shard_map/ppermute | solution.py:477
  50.8 5.3 %collective-permute-start.1 = (f32[56,128]{1,0:T(8,128)S(1)}, f32[56,128]{1,0:T(8,128)S(1)}, u32[]{:S(2)}, u32[]{:S(2)}) collective-permute-start(f32[56,128]{1,0:T(8,128)S(1)} %get-tuple-element.62), channel_id=1, source_target_pairs={{0,192},{64,128},{128,64},{192,0},{1,193},{65,129},{129,65},{193,1... | collective-permute-start | bytes 86024 | tf_op jit(solution)/shard_map/ppermute | solution.py:479

commit v8 on v7

--- a/solution.py
+++ b/solution.py
@@ -22,7 +22,7 @@
 NF = G * FOLD
 GT = 3
 NG = -(-T // GT)
-STEP_SLOTS = ((0, 176), (16, 304), (48, 416), (112, 528), (160, SLOTS))
+STEP_SLOTS = ((0, 192), (16, 320), (48, 432), (96, 544), (144, SLOTS))
 GROUP_BLOCKS = ((0, 1), (0, 2), (0, 3), (0, 3), (0, 4), (0, 4), (1, 5), (1, 5), (1, 5))
 SLOT_FROM = tuple(max(CP * GROUP_BLOCKS[t // GT][0], STEP_SLOTS[t // TS][0]) for t in range(T))
 SLOT_TO = tuple(min(CP * GROUP_BLOCKS[t // GT][1], STEP_SLOTS[t // TS][1]) for t in range(T))

time: 58.2 us -> 58.3 us (level)
  no operation moved by 1% of the time
where the time goes in v8:
time: 58.3 us; the launch traced here: 57.7 us
  Pallas kernels  31.1 us (53%)
  starting transfers between devices  16.9 us (29%)
  waiting for transfers between devices  7.69 us (13%)
  between operations  0.99 us (2%)
  local copies, waits for them, and re-layouts  0.67 us (1%)
    all_to_all x1, starting transfers between devices, packed_form(): received = lax.all_to_all(sent, 'blk', 0, 0, tiled=True)  12.3 us
    pallas_call x1, Pallas kernels, fold(): pl.pallas_call(fold_kernel, name='fold_weights', grid=(CP // CS,), out_sh...  11.8 us
    pallas_call x1, Pallas kernels, pack(): pl.pallas_call(pack_kernel, name='pack_amplitudes', grid=(T // TS,), out_...  7 us
    pallas_call x1, Pallas kernels, contract(): pl.pallas_call(contract_kernel, name='contract', out_shape=jax.ShapeDtype...  6.86 us
    pallas_call x1, Pallas kernels, tables(): pl.pallas_call(table_kernel, name='tables', out_shape=(pltpu.HBM((NG, M *...  4.32 us
    ppermute x1, starting transfers between devices, packed_form(): lax.ppermute(partial[3] + near[1], 'grp', [(d, d ^ 3) for d in range(G)])  3.03 us
    ppermute x1, waiting for transfers between devices, packed_form(): near = lax.ppermute(partial[1:3], 'grp', [(d, d ^ 1) for d in range(G)])  2.69 us
    all_to_all x1, waiting for transfers between devices, packed_form(): received = lax.all_to_all(sent, 'blk', 0, 0, tiled=True)  2.68 us
  transfers between devices with their start and end apart: 3, of which 3 were waited for; matrix products, arithmetic and copies ran while one was open for 1% of the time, Pallas kernels for 28%

profile of v8, /device:TPU:8, one launch (start us, length us, event | category | flops | bytes accessed | tf_op | source)
XLA Modules:
  0.0 57.7 jit_solution(10964600566171047722)
XLA Ops:
  0.0 0.0 copy-start.4
  0.0 0.0 copy-start.6
  0.0 0.0 copy-start.8
  0.0 7.0 %pack_amplitudes.1 = f32[64,4,640]{2,1,0:T(4,128)} custom-call(s32[40]{0:T(128)} %occ_ref.5, s32[1,500]{1,0:T(1,128)} %bitcast.37, f32[25,125,256]{2,1,0:T(8,128)} %amp_ref.1), custom_call_target="tpu_custom_call" | custom-call | tf_op jit(solution)/shard_map/pack_amplitudes/pallas_call | solution.py:133
  7.0 12.3 %all-to-all-start.2 = ((f32[64,4,640]{2,1,0:T(4,128)}), f32[64,4,640]{2,1,0:T(4,128)}, u32[]{:S(2)}, u32[]{:S(2)}) async-start(f32[64,4,640]{2,1,0:T(4,128)} %pack_amplitudes.1), calls=%async_computation.2 | async-start | bytes 1310720 | tf_op jit(solution)/shard_map/all_to_all | solution.py:467
  19.3 0.0 copy-done
  19.3 0.0 copy-done.1
  19.3 0.0 copy-done.3
  19.4 0.0 copy-done.4
  19.4 0.0 copy-done.6
  19.4 4.3 %tables.1 = (s32[9,256,128]{2,1,0:T(8,128)}, f32[25,256,128]{2,1,0:T(8,128)S(1)}, f32[8,128]{1,0:T(8,128)S(1)}, s32[1,128]{1,0:T(1,128)S(1)}, f32[40,128]{1,0:T(...) custom-call(s32[40]{0:T(128)S(1)} %copy-done.4, s32[500]{0:T(512)S(1)} %copy-done.3, f32[40]{0:T(128)S(1)} %copy-done.8, ...), custom_call_target="tpu_custom_call" | custom-call | tf_op jit(solution)/shard_map/tables/pallas_call | solution.py:303
  23.7 0.5 slice.24
  24.9 0.1 compare_select_fusion.2
  25.0 0.1 broadcast_xor_fusion.4
  25.0 0.1 xor.83.have_ref
  25.2 11.8 %fold_weights.1 = (bf16[40,128,160]{2,1,0:T(8,128)(2,1)}, bf16[40,128,160]{2,1,0:T(8,128)(2,1)}) custom-call(s32[40]{0:T(128)} %occ_ref.5, s32[1,500]{1,0:T(1,128)S(1)} %bitcast.39, s32[1,5120]{1,0:T(1,128)S(1)} %xor.83.have_ref, f32[5000,500]{1,0:T(8,128)} %bitcast.31), custom_call_target="tpu_custom_call" | custom-call | tf_op jit(solution)/shard_map/fold_weights/pallas_call | solution.py:199
  36.9 2.7 %all-to-all-done.2.far_x_ref = f32[64,4,640]{2,1,0:T(4,128)} async-done(((f32[64,4,640]{2,1,0:T(4,128)}), f32[64,4,640]{2,1,0:T(4,128)}, u32[]{:S(2)}, u32[]{:S(2)}) %all-to-all-start.2) | async-done | bytes 655392 | tf_op jit(solution)/shard_map/all_to_all | solution.py:467
  39.6 6.9 %contract.1 = f32[4,56,128]{2,1,0:T(8,128)S(1)} custom-call(f32[64,4,640]{2,1,0:T(4,128)} %all-to-all-done.2.far_x_ref, s32[9,256,128]{2,1,0:T(8,128)} %get-tuple-element.41.far_slot_ref, f32[25,256,128]{2,1,0:T(8,128)S(1)} %get-tuple-element.42.valid_ref, s32[1,128]{1,0:T(1,128)S(1)} %get-tuple-element.43.rank_ref, ...), custom_call_target="tpu_custom_call" | custom-call | tf_op jit(solution)/shard_map/contract/pallas_call | solution.py:421
  46.5 1.6 %collective-permute-start = (f32[2,56,128]{2,1,0:T(8,128)S(1)}, f32[2,56,128]{2,1,0:T(8,128)S(1)}, u32[]{:S(2)}, u32[]{:S(2)}) collective-permute-start(f32[2,56,128]{2,1,0:T(8,128)S(1)} %slice.31), channel_id=1, source_target_pairs={{0,64},{64,0},{128,192},{192,128},{1,65},{65,1},{129,193},{193,129... | collective-permute-start | bytes 172040 | tf_op jit(solution)/shard_map/ppermute | solution.py:477
  48.1 2.7 %collective-permute-done = f32[2,56,128]{2,1,0:T(8,128)S(1)} collective-permute-done((f32[2,56,128]{2,1,0:T(8,128)S(1)}, f32[2,56,128]{2,1,0:T(8,128)S(1)}, u32[]{:S(2)}, u32[]{:S(2)}) %collective-permute-start) | collective-permute-done | bytes 57376 | tf_op jit(solution)/shard_map/ppermute | solution.py:477
  50.8 3.0 %collective-permute-start.1 = (f32[56,128]{1,0:T(8,128)S(1)}, f32[56,128]{1,0:T(8,128)S(1)}, u32[]{:S(2)}, u32[]{:S(2)}) collective-permute-start(f32[56,128]{1,0:T(8,128)S(1)} %get-tuple-element.62), channel_id=1, source_target_pairs={{0,192},{64,128},{128,64},{192,0},{1,193},{65,129},{129,65},{193,1... | collective-permute-start | bytes 86024 | tf_op jit(solution)/shard_map/ppermute | solution.py:479
  53.8 2.3 %collective-permute-done.1.b_ref = f32[56,128]{1,0:T(8,128)S(1)} collective-permute-done((f32[56,128]{1,0:T(8,128)S(1)}, f32[56,128]{1,0:T(8,128)S(1)}, u32[]{:S(2)}, u32[]{:S(2)}) %collective-permute-start.1) | collective-permute-done | bytes 28704 | tf_op jit(solution)/shard_map/ppermute | solution.py:479
  56.1 1.1 %finish.1 = f32[160,125]{1,0:T(8,128)} custom-call(f32[56,128]{1,0:T(8,128)S(1)} %get-tuple-element.63.a_ref, f32[56,128]{1,0:T(8,128)S(1)} %collective-permute-done.1.b_ref, f32[40,128]{1,0:T(8,128)S(1)} %get-tuple-element.46.pick_ref, f32[160,128]{1,0:T(8,128)S(1)} %get-tuple-element.47.keep_ref, f32[160,128]{1,0:T(8,128)S(1)} %get-tuple-element.48.divisor_ref), custom_call_target="tpu_custom_call" | custom-call | tf_op jit(solution)/shard_map/finish/pallas_call | solution.py:455
  57.2 0.3 conditional.1
  (12 shorter events, 0.0 us)
Async XLA Ops:
  0.0 19.3 %copy-start = (s32[1,25]{1,0:T(1,128)S(1)}, s32[1,25]{1,0:T(1,128)}, u32[]{:S(2)}) copy-start(s32[1,25]{1,0:T(1,128)} %constant.48.from_ref) | copy-start | bytes 304
  0.0 19.3 %copy-start.1 = (s32[1,25]{1,0:T(1,128)S(1)}, s32[1,25]{1,0:T(1,128)}, u32[]{:S(2)}) copy-start(s32[1,25]{1,0:T(1,128)} %constant.49.to_ref) | copy-start | bytes 304
  0.0 19.3 %copy-start.3 = (s32[500]{0:T(512)S(1)}, s32[500]{0:T(512)}, u32[]{:S(2)}) copy-start(s32[500]{0:T(512)} %vir_ref.1) | copy-start | bytes 6004
  0.0 19.3 %copy-start.4 = (s32[40]{0:T(128)S(1)}, s32[40]{0:T(128)}, u32[]{:S(2)}) copy-start(s32[40]{0:T(128)} %occ_ref.5) | copy-start | bytes 484
  0.0 19.3 %copy-start.6 = (f32[500]{0:T(512)S(1)}, f32[500]{0:T(512)}, u32[]{:S(2)}) copy-start(f32[500]{0:T(512)} %vir_energy_ref.1) | copy-start | bytes 6004
  0.0 19.3 %copy-start.8 = (f32[40]{0:T(128)S(1)}, f32[40]{0:T(128)}, u32[]{:S(2)}) copy-start(f32[40]{0:T(128)} %occ_energy_ref.1) | copy-start | bytes 484
  7.0 32.6 %all-to-all-start.2 = ((f32[64,4,640]{2,1,0:T(4,128)}), f32[64,4,640]{2,1,0:T(4,128)}, u32[]{:S(2)}, u32[]{:S(2)}) async-start(f32[64,4,640]{2,1,0:T(4,128)} %pack_amplitudes.1), calls=%async_computation.2 | async-start | bytes 1310720 | tf_op jit(solution)/shard_map/all_to_all | solution.py:467
  39.6 17.6 %copy-start.5 = (s32[40]{0:T(128)S(1)}, s32[40]{0:T(128)}, u32[]{:S(2)}) copy-start(s32[40]{0:T(128)} %occ_ref.5) | copy-start | bytes 484
  39.6 17.6 %copy-start.7 = (f32[500]{0:T(512)S(1)}, f32[500]{0:T(512)}, u32[]{:S(2)}) copy-start(f32[500]{0:T(512)} %vir_energy_ref.1) | copy-start | bytes 6004
  39.6 17.6 %copy-start.9 = (f32[40]{0:T(128)S(1)}, f32[40]{0:T(128)}, u32[]{:S(2)}) copy-start(f32[40]{0:T(128)} %occ_energy_ref.1) | copy-start | bytes 484
  46.5 4.3 %collective-permute-start = (f32[2,56,128]{2,1,0:T(8,128)S(1)}, f32[2,56,128]{2,1,0:T(8,128)S(1)}, u32[]{:S(2)}, u32[]{:S(2)}) collective-permute-start(f32[2,56,128]{2,1,0:T(8,128)S(1)} %slice.31), channel_id=1, source_target_pairs={{0,64},{64,0},{128,192},{192,128},{1,65},{65,1},{129,193},{193,129... | collective-permute-start | bytes 172040 | tf_op jit(solution)/shard_map/ppermute | solution.py:477
  50.8 5.3 %collective-permute-start.1 = (f32[56,128]{1,0:T(8,128)S(1)}, f32[56,128]{1,0:T(8,128)S(1)}, u32[]{:S(2)}, u32[]{:S(2)}) collective-permute-start(f32[56,128]{1,0:T(8,128)S(1)} %get-tuple-element.62), channel_id=1, source_target_pairs={{0,192},{64,128},{128,64},{192,0},{1,193},{65,129},{129,65},{193,1... | collective-permute-start | bytes 86024 | tf_op jit(solution)/shard_map/ppermute | solution.py:479
